TPU v7x, 32 devices: a whole 2x2x4 slice. The times are simulated.
32 devices in a mesh: batch: 8 (over z, y), seq: 4 (over x, core).
Axes of the slice: x: 2, y: 2, z: 4, core: 2. Of those that a mesh axis runs over, the one named last changes fastest.
Arguments:
- tokens: bfloat16 [8, 3072, 512], P('batch', 'seq'), may hold values from -6 to 6
- source: bfloat16 [8, 1536, 512], P('batch', 'seq'), may hold values from -6 to 6
- out_grad: bfloat16 [8, 3072, 512], P('batch', 'seq'), may hold values from -6 to 6
- target_ids: int32 [8, 3072], P('batch', 'seq'), may hold values from 0 to 3, as said below
- source_ids: int32 [8, 1536], P('batch', 'seq'), may hold values from 0 to 3, as said below
- source_len: int32 [8], P('batch'), may hold values from 1488 to 1535
- self_qkv: bfloat16 [512, 1536], replicated, may hold values from -0.25 to 0.25
- self_out: bfloat16 [512, 512], replicated, may hold values from -1 to 1
- cross_q: bfloat16 [512, 512], replicated, may hold values from -0.25 to 0.25
- cross_kv: bfloat16 [512, 1024], replicated, may hold values from -0.25 to 0.25
- cross_out: bfloat16 [512, 512], replicated, may hold values from -1 to 1
- ffn_in: bfloat16 [512, 2048], replicated, may hold values from -0.25 to 0.25
- ffn_out: bfloat16 [2048, 512], replicated, may hold values from -0.125 to 0.125
- norm_gain: float32 [3, 512], replicated, may hold values from 0.25 to 1.75
- norm_bias: float32 [3, 512], replicated, may hold values from -3 to 3
- proj_bias: float32 [4, 512], replicated, may hold values from -3 to 3
- out_bias: float32 [3, 512], replicated, may hold values from -3 to 3
- ffn_bias: float32 [2048], replicated, may hold values from -3 to 3
Outputs:
- output: bfloat16 [8, 3072, 512], P('batch', 'seq')
- tokens_grad: bfloat16 [8, 3072, 512], P('batch', 'seq')
- source_grad: bfloat16 [8, 1536, 512], P('batch', 'seq')
- self_qkv_grad: float32 [512, 1536], replicated
- self_out_grad: float32 [512, 512], replicated
- cross_q_grad: float32 [512, 512], replicated
- cross_kv_grad: float32 [512, 1024], replicated
- cross_out_grad: float32 [512, 512], replicated
- ffn_in_grad: float32 [512, 2048], replicated
- ffn_out_grad: float32 [2048, 512], replicated
- norm_gain_grad: float32 [3, 512], replicated
- norm_bias_grad: float32 [3, 512], replicated
- proj_bias_grad: float32 [4, 512], replicated
- out_bias_grad: float32 [3, 512], replicated
- ffn_bias_grad: float32 [2048], replicated
Inputs may be any that keep to these rules, and one draw needn't show every extreme that they name: `target_ids`: along a row the numbers never fall, and each of 0 to 3 occurs. `source_ids`: along a row the numbers never fall, and each of 0 to 3 occurs below the row's source_len.
All inputs are finite; a program needn't handle non-finite values.
Results may differ from a plain program's by a relative error of at most 0.02.
Values may be sent and summed in bfloat16 or wider, within the bound.
No kernel may reach another device: no remote copies, remote signals or barrier semaphores. Data moves between devices by JAX's collectives and lax.ppermute only.
A program may use at most 192 MiB of HBM per device.

v0:
```python
import math

import jax
import jax.numpy as jnp
from jax import lax
from jax.sharding import PartitionSpec as P

HEADS = 8


NEG = -1e30
EPS = 1e-05


def product(left, right):
    return jnp.dot(left, right, preferred_element_type=jnp.float32)


def left_product(left, right):
    return lax.dot_general(
        left, right, (((0,), (0,)), ((), ())), preferred_element_type=jnp.float32
    )


def right_product(left, right):
    return lax.dot_general(
        left, right, (((1,), (1,)), ((), ())), preferred_element_type=jnp.float32
    )


def normalize(value, gain, shift):
    centred = value - jnp.mean(value, axis=-1, keepdims=True)
    inverse = lax.rsqrt(jnp.mean(centred * centred, axis=-1, keepdims=True) + EPS)
    unit = centred * inverse
    return (unit * gain + shift, unit, inverse)


def normalize_back(grad_output, unit, inverse, gain):
    scaled = grad_output * gain
    inner = (
        scaled
        - jnp.mean(scaled, axis=-1, keepdims=True)
        - unit * jnp.mean(scaled * unit, axis=-1, keepdims=True)
    )
    return (inner * inverse, jnp.sum(grad_output * unit, axis=0), jnp.sum(grad_output, axis=0))


def split_heads(value, heads):
    return value.reshape(value.shape[0], heads, value.shape[1] // heads)


def key_blocks(array):
    size = math.gcd(array.shape[0], 512)
    return array.reshape((array.shape[0] // size, size) + array.shape[1:])


def masked_scores(query_heads, block_keys, query_ids, block_ids, scale):
    scores = (
        jnp.einsum("qhe,khe->hqk", query_heads, block_keys, preferred_element_type=jnp.float32)
        * scale
    )
    allowed = query_ids[:, None] == block_ids[None, :]
    return jnp.where(allowed[None], scores, NEG)


def attend_forward(query_heads, key_heads, value_heads, query_ids, key_ids, scale):
    count, heads = (query_heads.shape[0], query_heads.shape[1])
    blocks = (key_blocks(key_heads), key_blocks(value_heads), key_blocks(key_ids))

    def peak_step(carry, block):
        largest, total = carry
        scores = masked_scores(query_heads, block[0], query_ids, block[2], scale)
        raised = jnp.maximum(largest, jnp.max(scores, axis=-1))
        total = total * jnp.exp(largest - raised) + jnp.sum(
            jnp.exp(scores - raised[..., None]), axis=-1
        )
        return ((raised, total), None)

    start = (jnp.full((heads, count), NEG, jnp.float32), jnp.zeros((heads, count), jnp.float32))
    (largest, total), unused = lax.scan(peak_step, start, blocks)

    def value_step(carry, block):
        scores = masked_scores(query_heads, block[0], query_ids, block[2], scale)
        probs = (jnp.exp(scores - largest[..., None]) / total[..., None]).astype(jnp.bfloat16)
        return (
            carry + jnp.einsum("hqk,khe->qhe", probs, block[1], preferred_element_type=jnp.float32),
            None,
        )

    mixed, unused = lax.scan(value_step, jnp.zeros(query_heads.shape, jnp.float32), blocks)
    return (mixed, largest, total)


def attend_back(
    query_heads,
    key_heads,
    value_heads,
    query_ids,
    key_ids,
    scale,
    largest,
    total,
    mixed,
    grad_mixed,
):
    blocks = (key_blocks(key_heads), key_blocks(value_heads), key_blocks(key_ids))
    spread = jnp.sum(grad_mixed.astype(jnp.float32) * mixed, axis=-1).T

    def grad_step(carry, block):
        scores = masked_scores(query_heads, block[0], query_ids, block[2], scale)
        probs = jnp.exp(scores - largest[..., None]) / total[..., None]
        rounded = probs.astype(jnp.bfloat16)
        grad_probs = jnp.einsum(
            "qhe,khe->hqk", grad_mixed, block[1], preferred_element_type=jnp.float32
        )
        grad_scores = (probs * (grad_probs - spread[..., None])).astype(jnp.bfloat16)
        carry = carry + jnp.einsum(
            "hqk,khe->qhe", grad_scores, block[0], preferred_element_type=jnp.float32
        )
        grad_keys = (
            jnp.einsum("hqk,qhe->khe", grad_scores, query_heads, preferred_element_type=jnp.float32)
            * scale
        )
        grad_values = jnp.einsum(
            "hqk,qhe->khe", rounded, grad_mixed, preferred_element_type=jnp.float32
        )
        return (carry, (grad_keys, grad_values))

    grad_queries, (grad_keys, grad_values) = lax.scan(
        grad_step, jnp.zeros(query_heads.shape, jnp.float32), blocks
    )
    count = key_heads.shape[0]
    return (grad_queries * scale, grad_keys.reshape(count, -1), grad_values.reshape(count, -1))


def body(
    tokens,
    source,
    out_grad,
    target_ids,
    source_ids,
    source_len,
    self_qkv,
    self_out,
    cross_q,
    cross_kv,
    cross_out,
    ffn_in,
    ffn_out,
    norm_gain,
    norm_bias,
    proj_bias,
    out_bias,
    ffn_bias,
):
    width = tokens.shape[2]
    heads = HEADS
    scale = 1.0 / math.sqrt(width // heads)
    all_target, all_source = (
        lax.all_gather(target_ids, "seq", axis=1, tiled=True),
        lax.all_gather(source_ids, "seq", axis=1, tiled=True),
    )
    own_ids = target_ids[0]
    places = jnp.arange(all_source.shape[1], dtype=jnp.int32)
    source_key_ids = jnp.where(places < source_len[0], all_source[0], -1)
    tokens_full = tokens[0].astype(jnp.float32)
    normed_one, unit_one, inverse_one = normalize(tokens_full, norm_gain[0], norm_bias[0])
    normed_one = normed_one.astype(jnp.bfloat16)
    joined = product(normed_one, self_qkv)
    queries = (joined[:, :width] + proj_bias[0]).astype(jnp.bfloat16)
    keys = joined[:, width : 2 * width].astype(jnp.bfloat16)
    values = (joined[:, 2 * width :] + proj_bias[1]).astype(jnp.bfloat16)
    all_keys, all_values = (
        lax.all_gather(keys, "seq", axis=0, tiled=True),
        lax.all_gather(values, "seq", axis=0, tiled=True),
    )
    query_heads = split_heads(queries, heads)
    key_heads = split_heads(all_keys, heads)
    value_heads = split_heads(all_values, heads)
    mixed, largest, total = attend_forward(
        query_heads, key_heads, value_heads, own_ids, all_target[0], scale
    )
    mixed_low = mixed.reshape(-1, width).astype(jnp.bfloat16)
    first = tokens_full + product(mixed_low, self_out) + out_bias[0]
    normed_two, unit_two, inverse_two = normalize(first, norm_gain[1], norm_bias[1])
    normed_two = normed_two.astype(jnp.bfloat16)
    cross_queries = (product(normed_two, cross_q) + proj_bias[2]).astype(jnp.bfloat16)
    source_joined = product(lax.all_gather(source[0], "seq", axis=0, tiled=True), cross_kv)
    cross_keys = source_joined[:, :width].astype(jnp.bfloat16)
    cross_values = (source_joined[:, width:] + proj_bias[3]).astype(jnp.bfloat16)
    cross_query_heads = split_heads(cross_queries, heads)
    cross_key_heads = split_heads(cross_keys, heads)
    cross_value_heads = split_heads(cross_values, heads)
    cross_mixed, cross_largest, cross_total = attend_forward(
        cross_query_heads, cross_key_heads, cross_value_heads, own_ids, source_key_ids, scale
    )
    cross_low = cross_mixed.reshape(-1, width).astype(jnp.bfloat16)
    second = first + product(cross_low, cross_out) + out_bias[1]
    normed_three, unit_three, inverse_three = normalize(second, norm_gain[2], norm_bias[2])
    normed_three = normed_three.astype(jnp.bfloat16)
    hidden = product(normed_three, ffn_in) + ffn_bias
    active, gelu_back = jax.vjp(jax.nn.gelu, hidden)
    active_low = active.astype(jnp.bfloat16)
    output = second + product(active_low, ffn_out) + out_bias[2]
    grad_low = out_grad[0]
    grad_full = grad_low.astype(jnp.float32)
    ffn_out_grad = left_product(active_low, grad_low)
    out_bias_two = jnp.sum(grad_full, axis=0)
    grad_hidden = gelu_back(right_product(grad_low, ffn_out))[0].astype(jnp.bfloat16)
    ffn_in_grad = left_product(normed_three, grad_hidden)
    ffn_bias_grad = jnp.sum(grad_hidden.astype(jnp.float32), axis=0)
    grad_normed, gain_three, shift_three = normalize_back(
        right_product(grad_hidden, ffn_in), unit_three, inverse_three, norm_gain[2]
    )
    grad_second = grad_full + grad_normed
    second_low = grad_second.astype(jnp.bfloat16)
    cross_out_grad = left_product(cross_low, second_low)
    out_bias_one = jnp.sum(second_low.astype(jnp.float32), axis=0)
    grad_cross_mixed = right_product(second_low, cross_out).astype(jnp.bfloat16)
    grad_cross_queries, grad_cross_keys, grad_cross_values = attend_back(
        cross_query_heads,
        cross_key_heads,
        cross_value_heads,
        own_ids,
        source_key_ids,
        scale,
        cross_largest,
        cross_total,
        cross_mixed,
        split_heads(grad_cross_mixed, heads),
    )
    cross_queries_low = grad_cross_queries.reshape(-1, width).astype(jnp.bfloat16)
    cross_q_grad = left_product(normed_two, cross_queries_low)
    bias_two = jnp.sum(cross_queries_low.astype(jnp.float32), axis=0)
    own_key_grads, own_value_grads = (
        lax.psum_scatter(
            grad_cross_keys.astype(jnp.bfloat16), "seq", scatter_dimension=0, tiled=True
        ).astype(jnp.float32),
        lax.psum_scatter(
            grad_cross_values.astype(jnp.bfloat16), "seq", scatter_dimension=0, tiled=True
        ).astype(jnp.float32),
    )
    source_pair_low = jnp.concatenate([own_key_grads, own_value_grads], axis=1).astype(jnp.bfloat16)
    cross_kv_grad = left_product(source[0], source_pair_low)
    bias_three = jnp.sum(source_pair_low[:, width:].astype(jnp.float32), axis=0)
    source_grad = right_product(source_pair_low, cross_kv).astype(jnp.bfloat16)
    grad_normed, gain_two, shift_two = normalize_back(
        right_product(cross_queries_low, cross_q), unit_two, inverse_two, norm_gain[1]
    )
    grad_first = grad_second + grad_normed
    first_low = grad_first.astype(jnp.bfloat16)
    self_out_grad = left_product(mixed_low, first_low)
    out_bias_zero = jnp.sum(first_low.astype(jnp.float32), axis=0)
    grad_mixed = right_product(first_low, self_out).astype(jnp.bfloat16)
    grad_queries, grad_keys, grad_values = attend_back(
        query_heads,
        key_heads,
        value_heads,
        own_ids,
        all_target[0],
        scale,
        largest,
        total,
        mixed,
        split_heads(grad_mixed, heads),
    )
    own_keys_grad, own_values_grad = (
        lax.psum_scatter(
            grad_keys.astype(jnp.bfloat16), "seq", scatter_dimension=0, tiled=True
        ).astype(jnp.float32),
        lax.psum_scatter(
            grad_values.astype(jnp.bfloat16), "seq", scatter_dimension=0, tiled=True
        ).astype(jnp.float32),
    )
    self_pair_low = jnp.concatenate(
        [grad_queries.reshape(-1, width), own_keys_grad, own_values_grad], axis=1
    ).astype(jnp.bfloat16)
    self_qkv_grad = left_product(normed_one, self_pair_low)
    bias_zero = jnp.sum(self_pair_low[:, :width].astype(jnp.float32), axis=0)
    bias_one = jnp.sum(self_pair_low[:, 2 * width :].astype(jnp.float32), axis=0)
    grad_normed, gain_one, shift_one = normalize_back(
        right_product(self_pair_low, self_qkv), unit_one, inverse_one, norm_gain[0]
    )
    tokens_grad = (grad_first + grad_normed).astype(jnp.bfloat16)
    (
        ffn_in_grad,
        ffn_out_grad,
        ffn_bias_grad,
        gain_three,
        shift_three,
        out_bias_two,
        cross_q_grad,
        cross_kv_grad,
        cross_out_grad,
        gain_two,
        shift_two,
        out_bias_one,
        bias_two,
        bias_three,
        self_qkv_grad,
        self_out_grad,
        gain_one,
        shift_one,
        out_bias_zero,
        bias_zero,
        bias_one,
    ) = lax.psum(
        (
            ffn_in_grad,
            ffn_out_grad,
            ffn_bias_grad,
            gain_three,
            shift_three,
            out_bias_two,
            cross_q_grad,
            cross_kv_grad,
            cross_out_grad,
            gain_two,
            shift_two,
            out_bias_one,
            bias_two,
            bias_three,
            self_qkv_grad,
            self_out_grad,
            gain_one,
            shift_one,
            out_bias_zero,
            bias_zero,
            bias_one,
        ),
        ("batch", "seq"),
    )
    norm_gain_grad = jnp.stack([gain_one, gain_two, gain_three])
    norm_bias_grad = jnp.stack([shift_one, shift_two, shift_three])
    proj_bias_grad = jnp.stack([bias_zero, bias_one, bias_two, bias_three])
    out_bias_grad = jnp.stack([out_bias_zero, out_bias_one, out_bias_two])
    return (
        output.astype(jnp.bfloat16)[None],
        tokens_grad[None],
        source_grad[None],
        self_qkv_grad,
        self_out_grad,
        cross_q_grad,
        cross_kv_grad,
        cross_out_grad,
        ffn_in_grad,
        ffn_out_grad,
        norm_gain_grad,
        norm_bias_grad,
        proj_bias_grad,
        out_bias_grad,
        ffn_bias_grad,
    )


def solution(mesh):
    return jax.shard_map(
        body,
        mesh=mesh,
        in_specs=(
            P("batch", "seq", None),
            P("batch", "seq", None),
            P("batch", "seq", None),
            P("batch", "seq"),
            P("batch", "seq"),
            P("batch"),
            P(),
            P(),
            P(),
            P(),
            P(),
            P(),
            P(),
            P(),
            P(),
            P(),
            P(),
            P(),
        ),
        out_specs=(
            P("batch", "seq", None),
            P("batch", "seq", None),
            P("batch", "seq", None),
            P(),
            P(),
            P(),
            P(),
            P(),
            P(),
            P(),
            P(),
            P(),
            P(),
            P(),
            P(),
        ),
        check_vma=False,
    )
```

profile of v0, /device:TPU:0, one launch (start us, length us, event | category | flops | bytes accessed | tf_op | source)
XLA Modules:
  0.0 861.5 jit_solution(11288429075755598473)
XLA Ops:
  21.0 6.2 all_gather.19
  27.8 5.4 all_gather.16
  43.6 5.3 reshape.333
  53.7 5.1 reshape.332
  63.5 8.9 %reshape.331 = bf16[6,512,8,64]{3,2,1,0:T(8,128)(2,1)} reshape(bf16[3072,512]{1,0:T(8,128)(2,1)} %all-gather.7.cloned.1.call-done) | data formatting | bytes 6291456 | tf_op jit(solution)/shard_map/reshape;reshape | solution.py:54
  72.4 7.8 copy.117
  80.2 36.9 %while.78 = (s32[]{:T(128)}, f32[8,768]{1,0:T(8,128)S(1)}, f32[8,768]{1,0:T(8,128)S(1)}, s32[1,768]{1,0:T(1,128)S(1)}, s32[6,512]{1,0:T(8,128)S(1)}, /*index=5*/...) while((s32[]{:T(128)}, f32[8,768]{1,0:T(8,128)S(1)}, ...), condition=%wide.region_5.6_spmd.clone, body=%wide.region_2.5_spmd.clone.sunk | while | flops 425097216 | bytes 27991164 | solution.py:80
  117.2 8.9 %reshape.330 = bf16[6,512,8,64]{3,2,1,0:T(8,128)(2,1)} reshape(bf16[3072,512]{1,0:T(8,128)(2,1)} %all-gather.5.cloned.1.call-done) | data formatting | bytes 6291456 | tf_op jit(solution)/shard_map/reshape;reshape | solution.py:54
  126.1 7.6 copy.116
  133.7 46.9 %while.79 = (s32[]{:T(128)}, f32[768,8,64]{0,2,1:T(8,128)}, bf16[6,512,8,64]{1,3,2,0:T(8,128)(2,1)}, s32[1,768]{1,0:T(1,128)S(1)}, s32[6,512]{1,0:T(8,128)S(1)},...) while((s32[]{:T(128)}, f32[768,8,64]{0,2,1:T(8,128)}, ...), condition=%wide.region_7.8_spmd.clone, body=%wide.region_6.7_spmd.clone.sunk | while | flops 822214656 | bytes 5833350 | solution.py:90
  134.4 7.0 bitcast_add_fusion.8
  141.7 7.5 bitcast_add_fusion.8
  149.5 7.5 bitcast_add_fusion.8
  157.4 7.5 bitcast_add_fusion.8
  165.2 7.5 bitcast_add_fusion.8
  173.0 7.5 bitcast_add_fusion.8
  185.6 18.4 %while.80 = (s32[]{:T(128)}, f32[8,768]{1,0:T(8,128)S(1)}, f32[8,768]{1,0:T(8,128)S(1)}, s32[1,768]{1,0:T(1,128)S(1)}, s32[3,512]{1,0:T(4,128)S(1)}, /*index=5*/...) while((s32[]{:T(128)}, f32[8,768]{1,0:T(8,128)S(1)}, ...), condition=%wide.region_13.14_spmd.clone, body=%wide.region_10.13_spmd.clone.sunk | while | flops 425097216 | bytes 27991164 | solution.py:80
  204.1 25.9 %while.81 = (s32[]{:T(128)}, f32[768,8,64]{0,2,1:T(8,128)}, bf16[3,512,8,64]{1,3,2,0:T(8,128)(2,1)}, s32[1,768]{1,0:T(1,128)S(1)}, s32[3,512]{1,0:T(4,128)S(1)},...) while((s32[]{:T(128)}, f32[768,8,64]{0,2,1:T(8,128)}, ...), condition=%wide.region_15.16_spmd.clone, body=%wide.region_14.15_spmd.clone.sunk | while | flops 822214656 | bytes 5833350 | solution.py:90
  205.4 7.1 bitcast_add_fusion.9
  213.6 7.7 bitcast_add_fusion.9
  222.3 7.7 bitcast_add_fusion.9
  236.2 6.3 convert_reduce_fusion
  255.1 54.3 %while.82 = (s32[]{:T(128)}, f32[768,8,64]{0,2,1:T(8,128)}, bf16[3,512,8,64]{1,3,2,0:T(8,128)(2,1)}, bf16[3,512,8,64]{1,3,2,0:T(8,128)(2,1)}, bf16[3,512,8,64]{1...) while((s32[]{:T(128)}, f32[768,8,64]{0,2,1:T(8,128)}, ...), condition=%wide.region_22.23_spmd.clone, body=%wide.region_21.22_spmd.clone.sunk | while | flops 2039873536 | bytes 83189008 | solution.py:129
  314.3 5.6 reshape.328
  328.5 5.0 copy.165
  333.4 5.4 reshape.326
  347.5 110.3 %while.83 = (s32[]{:T(128)}, f32[768,8,64]{0,2,1:T(8,128)}, bf16[6,512,8,64]{1,3,2,0:T(8,128)(2,1)}, bf16[6,512,8,64]{1,3,2,0:T(8,128)(2,1)}, bf16[6,512,8,64]{1...) while((s32[]{:T(128)}, f32[768,8,64]{0,2,1:T(8,128)}, ...), condition=%wide.region_27.28_spmd.clone, body=%wide.region_26.27_spmd.clone.sunk | while | flops 2039873536 | bytes 70606032 | solution.py:129
  496.5 8.7 %reduce-scatter.11.cloned.1.call-done = bf16[768,512]{0,1:T(8,128)(2,1)} async-done(((bf16[3072,512]{0,1:T(8,128)(2,1)}), bf16[768,512]{0,1:T(8,128)(2,1)}) %reduce-scatter.11.cloned.1.call-update) | async-done | bytes 786448 | tf_op jit(solution)/shard_map/reduce_scatter | solution.py:271
  505.2 40.6 %reduce-scatter.9.cloned.1.call-done = bf16[768,512]{0,1:T(8,128)(2,1)} async-done(((bf16[3072,512]{0,1:T(8,128)(2,1)}), bf16[768,512]{0,1:T(8,128)(2,1)}) %reduce-scatter.9.cloned.1.call-update) | async-done | bytes 786448 | tf_op jit(solution)/shard_map/reduce_scatter | solution.py:268
  551.3 7.1 fusion.128
  578.9 42.0 %all-reduce = (f32[1,512]{1,0:T(1,128)S(1)}, f32[1,512]{1,0:T(1,128)S(1)}, f32[1,512]{1,0:T(1,128)S(1)}, f32[1,512]{1,0:T(1,128)S(1)}, f32[1,512]{1,0:T(1,128)S(...) all-reduce(f32[1,512]{1,0:T(1,128)S(1)} %bitcast.442, ...), channel_id=1, replica_groups=mesh['batch'=8,'seq'=4] {'batch','seq'}, use_global_device_ids=true, to_apply=%region_46.47 | all-reduce | flops 8704 | bytes 69632 | tf_op jit(solution)/shard_map/psum | solution.py:307
  623.3 215.4 %all-reduce.4.cloned.1.call-done = (f32[512,1536]{1,0:T(8,128)}, f32[512,512]{1,0:T(8,128)}, f32[512,512]{1,0:T(8,128)}, f32[512,1024]{0,1:T(8,128)}, f32[512,51...) async-done(((f32[512,1536]{1,0:T(8,128)}, f32[512,512]{1,0:T(8,128)}, f32[512,512]{1,0:T(8,128)}, f32[512,1024]{0,1:T(8,128)}, f32[512,512]{1,0:T(8,128)}, ...) | async-done | bytes 16777232 | tf_op jit(solution)/shard_map/psum | solution.py:307
  (545 shorter events, 385.0 us)
Async XLA Ops:
  7.2 229.0 %copy-start = (bf16[2048,512]{1,0:T(8,128)(2,1)S(1)}, bf16[2048,512]{1,0:T(8,128)(2,1)}, u32[]{:S(2)}) copy-start(bf16[2048,512]{1,0:T(8,128)(2,1)} %param.42) | copy-start | bytes 6291460
  7.2 29.8 %all-gather.9.cloned.1.call-start = ((), (), s32[]{:S(2)}) async-start(), calls=%async_computation.8 | async-start | bytes 1966080 | tf_op jit(solution)/shard_map/all_gather | solution.py:188
  7.9 55.5 %all-gather.7.cloned.1.call-start = ((), (), s32[]{:S(2)}) async-start(), calls=%async_computation.5 | async-start | bytes 3932160 | tf_op jit(solution)/shard_map/all_gather | solution.py:174
  15.9 101.3 %all-gather.5.cloned.1.call-start = ((), (), s32[]{:S(2)}) async-start(), calls=%async_computation.4 | async-start | bytes 3932160 | tf_op jit(solution)/shard_map/all_gather | solution.py:175
  16.5 4.4 copy-start.102
  16.5 10.7 %copy-start.92 = (f32[3,512]{1,0:T(4,128)S(1)}, f32[3,512]{1,0:T(4,128)}, u32[]{:S(2)}) copy-start(f32[3,512]{1,0:T(4,128)} %param.46) | copy-start | bytes 18436
  16.5 11.3 %copy-start.35 = (s32[1,768]{1,0:T(1,128)S(1)}, s32[1,768]{1,0:T(1,128)}, u32[]{:S(2)}) copy-start(s32[1,768]{1,0:T(1,128)} %param.33) | copy-start | bytes 9220
  16.5 17.9 %copy-start.46 = (bf16[1,768,512]{2,1,0:T(8,128)(2,1)S(1)}, bf16[1,768,512]{2,1,0:T(8,128)(2,1)}, u32[]{:S(2)}) copy-start(bf16[1,768,512]{2,1,0:T(8,128)(2,1)} %param.32) | copy-start | bytes 2359300
  20.2 469.9 %reduce-scatter.15.cloned.1.call-start = ((), (), s32[]{:S(2)}) async-start(), calls=%async_computation.10 | async-start | bytes 1966080
  230.0 6.2 copy-start.3
  232.9 19.3 %copy-start.64 = (f32[768]{0:T(1024)}, f32[768]{0:T(1024)S(1)}, u32[]{:S(2)}) copy-start(f32[768]{0:T(1024)S(1)} %broadcast_multiply_fusion.6) | copy-start | bytes 9220
  233.2 19.1 %copy-start.71 = (f32[768]{0:T(1024)}, f32[768]{0:T(1024)S(1)}, u32[]{:S(2)}) copy-start(f32[768]{0:T(1024)S(1)} %add_rsqrt_fusion) | copy-start | bytes 9220
  236.2 6.3 copy-start.109
  246.0 6.3 copy-start.32
  283.9 4.1 copy-start.4
  302.1 4.1 copy-start.4
  319.9 171.4 %reduce-scatter.13.cloned.1.call-start = ((), (), s32[]{:S(2)}) async-start(), calls=%async_computation.9 | async-start | bytes 1966080
  333.4 5.5 copy-start.62
  333.4 5.5 copy-start.69
  333.4 5.5 copy-start.78
  346.8 158.4 %reduce-scatter.11.cloned.1.call-start = ((), (), s32[]{:S(2)}) async-start(), calls=%async_computation.7 | async-start | bytes 3932160 | tf_op jit(solution)/shard_map/reduce_scatter | solution.py:271
  465.1 80.7 %reduce-scatter.9.cloned.1.call-start = ((), (), s32[]{:S(2)}) async-start(), calls=%async_computation.6 | async-start | bytes 3932160 | tf_op jit(solution)/shard_map/reduce_scatter | solution.py:268
  472.8 365.9 %all-reduce.4.cloned.1.call-start = ((), (), s32[]{:S(2)}) async-start(), calls=%async_computation.11 | async-start | bytes 33554432 | tf_op jit(solution)/shard_map/psum | solution.py:307
  479.4 5.9 slice-start
  493.2 52.6 %copy-start.20 = (bf16[1,768,512]{1,2,0:T(8,128)(2,1)S(1)}, bf16[1,768,512]{1,2,0:T(8,128)(2,1)}, u32[]{:S(2)}) copy-start(bf16[1,768,512]{1,2,0:T(8,128)(2,1)} %copy-done.18) | copy-start | bytes 2359300
  493.2 52.6 %copy-start.60 = (f32[768]{0:T(1024)S(1)}, f32[768]{0:T(1024)}, u32[]{:S(2)}) copy-start(f32[768]{0:T(1024)} %copy-done.59) | copy-start | bytes 9220
  493.2 52.6 %copy-start.67 = (f32[768]{0:T(1024)S(1)}, f32[768]{0:T(1024)}, u32[]{:S(2)}) copy-start(f32[768]{0:T(1024)} %copy-done.66) | copy-start | bytes 9220
  493.2 52.6 %copy-start.74 = (f32[1,512]{1,0:T(1,128)S(1)}, f32[1,512]{1,0:T(1,128)}, u32[]{:S(2)}) copy-start(f32[1,512]{1,0:T(1,128)} %copy-done.73) | copy-start | bytes 6148
  493.2 52.6 %copy-start.95 = (f32[1,512]{1,0:T(1,128)S(1)}, f32[1,512]{1,0:T(1,128)}, u32[]{:S(2)}) copy-start(f32[1,512]{1,0:T(1,128)} %copy-done.94) | copy-start | bytes 6148
  561.0 4.4 copy-start.106
  841.5 4.9 copy-start.44
  841.5 5.9 copy-start.43
  (101 other events, 240.2 us)
Sparse Core Ops, SparseCore 0:
  9.6 22.3 all-gather.8
  34.1 28.5 all-gather.6
  64.9 28.5 all-gather.4
  320.0 29.7 reduce-scatter.14
  352.3 28.1 reduce-scatter.12
  465.3 39.8 reduce-scatter.10
  507.9 37.9 reduce-scatter.8
  553.4 285.1 all-reduce.3
where the time goes:
time: 871 us; the launch traced here: 862 us
  matrix products  306 us (35%)
  waiting for transfers between devices  266 us (31%)
  local copies, waits for them, and re-layouts  149 us (17%)
  other arithmetic  69 us (8%)
  blocking collectives  53.6 us (6%)
  between operations  16.5 us (2%)
    psum x1, waiting for transfers between devices, body(): lax.psum((ffn_in_grad, ffn_out_grad, ffn_bias_grad, gain_three, shift_thr...  215 us
    unnamed x243, local copies, waits for them, and re-layouts  88.9 us
    dot_general x18, matrix products, masked_scores(): jnp.einsum('qhe,khe->hqk', query_heads, block_keys, preferred_element_typ...  71.9 us
    dot_general x9, matrix products, value_step(): jnp.einsum('hqk,khe->qhe', probs, block[1], preferred_element_type=jnp.fl...  67.1 us
    psum x1, blocking collectives, body(): lax.psum((ffn_in_grad, ffn_out_grad, ffn_bias_grad, gain_three, shift_thr...  42 us
    reduce_scatter x1, waiting for transfers between devices, body(): lax.psum_scatter(grad_keys.astype(jnp.bfloat16), 'seq', scatter_dimension...  40.6 us
    dot_general x9, matrix products, grad_step(): jnp.einsum('hqk,khe->qhe', grad_scores, block[0], preferred_element_type=...  35.2 us
    another operation x5, local copies, waits for them, and re-layouts, key_blocks(): return array.reshape((array.shape[0] // size, size) + array.shape[1:])  28.3 us
  transfers between devices with their start and end apart: 8, of which 3 were waited for; matrix products, arithmetic and copies ran while one was open for 34% of the time, Pallas kernels for 0%

commit v1 on v0

v1 whole, which is shorter than its diff:
```python
import functools
import math

import jax
import jax.numpy as jnp
from jax import lax
from jax.experimental import pallas as pl
from jax.experimental.pallas import tpu as pltpu
from jax.sharding import PartitionSpec as P

HEADS = 8
EPS = 1e-05
F32 = jnp.float32
BF = jnp.bfloat16
LN2 = math.log(2.0)
LOG2E = 1.0 / LN2
VMEM = 60 * 1024 * 1024


def nn(left, right):
    return lax.dot_general(left, right, (((1,), (0,)), ((), ())), preferred_element_type=F32)


def nt(left, right):
    return lax.dot_general(left, right, (((1,), (1,)), ((), ())), preferred_element_type=F32)


def tn(left, right):
    return lax.dot_general(left, right, (((0,), (0,)), ((), ())), preferred_element_type=F32)


def key_marks(ids):
    lane = lax.broadcasted_iota(jnp.int32, (1, 128), 1)
    ids = ids[:, None]
    hit = ((lane < 4) & (lane == ids)) | ((lane == 4) & (ids < 0)) | ((lane >= 5) & (lane <= 9))
    return hit.astype(BF)


def query_marks(ids):
    lane = lax.broadcasted_iota(jnp.int32, (1, 128), 1)
    shut = ((lane < 4) & (lane != ids[:, None])) | (lane == 4)
    return jnp.where(shut, -1e30, 0.0).astype(BF)


def forward_kernel(q_ref, aux_ref, k_ref, v_ref, e_ref, o_ref, aux_out_ref, *, block):
    count = k_ref.shape[0]
    lane = lax.broadcasted_iota(jnp.int32, (1, 128), 1)
    low = lane < 64
    zero = jnp.zeros((), BF)
    one = jnp.ones((), BF)
    q = q_ref[...]
    aux = aux_ref[...]
    done = []
    for head in range(2):
        mine = low if head == 0 else ~low
        query = jnp.concatenate([jnp.where(mine, q, zero), aux], axis=1)
        peak = total = None
        for start in range(0, count, block):
            rows = pl.ds(start, block)
            scores = nt(query, jnp.concatenate([k_ref[rows, :], e_ref[rows, :]], axis=1))
            value = jnp.where(mine, v_ref[rows, :], one)
            largest = jnp.max(scores, axis=1, keepdims=True)
            if peak is None:
                peak = largest
                total = nn(jnp.exp2(scores - peak).astype(BF), value)
            else:
                raised = jnp.maximum(peak, largest)
                total = total * jnp.exp2(peak - raised) + nn(
                    jnp.exp2(scores - raised).astype(BF), value
                )
                peak = raised
        done.append((total, peak))
    top = jnp.where(low, done[0][0], done[1][0])
    below = jnp.where(low, pltpu.roll(done[0][0], 64, 1), pltpu.roll(done[1][0], 64, 1))
    o_ref[...] = (top / below).astype(BF)
    for head in range(2):
        total, peak = done[head]
        weight = total[:, 64:65] if head == 0 else total[:, 0:1]
        minus = -(peak + jnp.log2(weight))
        first = minus.astype(BF)
        rest = minus - first.astype(F32)
        second = rest.astype(BF)
        third = (rest - second.astype(F32)).astype(BF)
        aux_out_ref[head] = jnp.where(
            lane == 5, first, jnp.where(lane == 6, second, jnp.where(lane == 7, third, aux))
        )


def attend(queries, aux, keys, values, marks):
    rows, count = queries.shape[0], keys.shape[0]
    width = queries.shape[1]
    block = 1024 if count % 1024 == 0 else math.gcd(count, 512)
    return pl.pallas_call(
        functools.partial(forward_kernel, block=block),
        grid=(width // 128,),
        in_specs=[
            pl.BlockSpec((rows, 128), lambda i: (0, i)),
            pl.BlockSpec((rows, 128), lambda i: (0, 0)),
            pl.BlockSpec((count, 128), lambda i: (0, i)),
            pl.BlockSpec((count, 128), lambda i: (0, i)),
            pl.BlockSpec((count, 128), lambda i: (0, 0)),
        ],
        out_specs=[
            pl.BlockSpec((rows, 128), lambda i: (0, i)),
            pl.BlockSpec((2, rows, 128), lambda i: (i, 0, 0)),
        ],
        out_shape=[
            jax.ShapeDtypeStruct((rows, width), BF),
            jax.ShapeDtypeStruct((width // 64, rows, 128), BF),
        ],
        compiler_params=pltpu.CompilerParams(vmem_limit_bytes=VMEM),
        name="attend",
    )(queries, aux, keys, values, marks)


def backward_kernel(
    q_ref, do_ref, mix_ref, aux_ref, k_ref, v_ref, e_ref, dq_ref, dk_ref, dv_ref, dq_sum, *, block
):
    count = k_ref.shape[0]
    lane = lax.broadcasted_iota(jnp.int32, (1, 128), 1)
    low = lane < 64
    zero = jnp.zeros((), BF)
    q = q_ref[...]
    do = do_ref[...]
    product = do.astype(F32) * mix_ref[...].astype(F32)
    score_side, probs_side, query_side, grad_side = [], [], [], []
    for head in range(2):
        mine = low if head == 0 else ~low
        q_head = jnp.where(mine, q, zero)
        do_head = jnp.where(mine, do, zero)
        minus = -jnp.sum(jnp.where(mine, product, 0.0), axis=1, keepdims=True)
        first = minus.astype(BF)
        second = (minus - first.astype(F32)).astype(BF)
        extra = jnp.where(lane == 8, first, jnp.where(lane == 9, second, zero))
        score_side.append(jnp.concatenate([q_head, aux_ref[head]], axis=1))
        probs_side.append(jnp.concatenate([do_head, extra], axis=1))
        query_side.append(q_head)
        grad_side.append(do_head)
    for start in range(0, count, block):
        rows = pl.ds(start, block)
        k = k_ref[rows, :]
        e = e_ref[rows, :]
        key = jnp.concatenate([k, e], axis=1)
        value = jnp.concatenate([v_ref[rows, :], e], axis=1)
        dk = dv = None
        for head in range(2):
            mine = low if head == 0 else ~low
            probs = jnp.exp2(nt(key, score_side[head]))
            ds = (probs * nt(value, probs_side[head])).astype(BF)
            dv_head = nn(probs.astype(BF), grad_side[head])
            dk_head = nn(ds, query_side[head])
            dv = dv_head if head == 0 else dv + dv_head
            dk = dk_head if head == 0 else dk + dk_head
            part = tn(jnp.where(mine, k, zero), ds)
            if start == 0 and head == 0:
                dq_sum[...] = part
            else:
                dq_sum[...] += part
        dk_ref[rows, :] = (dk * LN2).astype(BF)
        dv_ref[rows, :] = dv.astype(BF)
    dq_ref[...] = (dq_sum[...].T * 0.125).astype(BF)


def attend_back(queries, grad_mixed, mixed, aux, keys, values, marks):
    rows, count = queries.shape[0], keys.shape[0]
    width = queries.shape[1]
    by_query = pl.BlockSpec((rows, 128), lambda i: (0, i))
    by_key = pl.BlockSpec((count, 128), lambda i: (0, i))
    return pl.pallas_call(
        functools.partial(backward_kernel, block=math.gcd(count, 512)),
        grid=(width // 128,),
        in_specs=[
            by_query,
            by_query,
            by_query,
            pl.BlockSpec((2, rows, 128), lambda i: (i, 0, 0)),
            by_key,
            by_key,
            pl.BlockSpec((count, 128), lambda i: (0, 0)),
        ],
        out_specs=[by_query, by_key, by_key],
        out_shape=[
            jax.ShapeDtypeStruct((rows, width), BF),
            jax.ShapeDtypeStruct((count, width), BF),
            jax.ShapeDtypeStruct((count, width), BF),
        ],
        scratch_shapes=[pltpu.VMEM((128, rows), F32)],
        compiler_params=pltpu.CompilerParams(vmem_limit_bytes=VMEM),
        name="attend_back",
    )(queries, grad_mixed, mixed, aux, keys, values, marks)


def normalize(value, gain, shift):
    centred = value - jnp.mean(value, axis=-1, keepdims=True)
    inverse = lax.rsqrt(jnp.mean(centred * centred, axis=-1, keepdims=True) + EPS)
    unit = centred * inverse
    return (unit * gain + shift, unit, inverse)


def normalize_back(grad_output, unit, inverse, gain):
    scaled = grad_output * gain
    inner = (
        scaled
        - jnp.mean(scaled, axis=-1, keepdims=True)
        - unit * jnp.mean(scaled * unit, axis=-1, keepdims=True)
    )
    return inner * inverse


def swap(value, axis, size, step):
    return lax.ppermute(value, axis, [(i, i ^ step) for i in range(size)])


def gather_row(own, size):
    blocks = [own]
    step = size // 2
    pieces = {0: own}
    while step:
        for place in sorted(pieces):
            pieces[place ^ step] = swap(pieces[place], "seq", size, step)
        step //= 2
    return [pieces[place] for place in range(size)]


def scatter_row(parts, size):
    step = 1
    held = dict(enumerate(parts))
    while step < size:
        kept = {}
        for place in held:
            if not place & step:
                kept[place] = held[place] + swap(held[place | step], "seq", size, step).astype(F32)
        step *= 2
        if step < size:
            held = {
                place: (kept[place].astype(BF) if place & step else kept[place]) for place in kept
            }
        else:
            held = kept
    return held[0]


def sum_all(value, seq, batch):
    steps = [("seq", seq, 1 << k) for k in range(seq.bit_length() - 1)]
    steps += [("batch", batch, 1 << k) for k in range(batch.bit_length() - 1)]
    taken = []
    for axis, size, step in steps:
        rows = value.shape[0]
        if rows % 32:
            value = (value.astype(F32) + swap(value, axis, size, step).astype(F32)).astype(BF)
            continue
        bit = (lax.axis_index(axis) // step) % 2
        half = rows // 2
        kept = lax.dynamic_slice_in_dim(value, bit * half, half, 0)
        sent = lax.dynamic_slice_in_dim(value, (1 - bit) * half, half, 0)
        value = (kept.astype(F32) + swap(sent, axis, size, step).astype(F32)).astype(BF)
        taken.append((axis, size, step, bit))
    for axis, size, step, bit in reversed(taken):
        other = swap(value, axis, size, step)
        first = jnp.where(bit == 0, value, other)
        second = jnp.where(bit == 0, other, value)
        value = jnp.concatenate([first, second], axis=0)
    return value


def body(
    seq,
    batch,
    tokens,
    source,
    out_grad,
    target_ids,
    source_ids,
    source_len,
    self_qkv,
    self_out,
    cross_q,
    cross_kv,
    cross_out,
    ffn_in,
    ffn_out,
    norm_gain,
    norm_bias,
    proj_bias,
    out_bias,
    ffn_bias,
):
    width = tokens.shape[2]
    count = tokens.shape[1]
    scale = LOG2E / math.sqrt(width // HEADS)
    own_ids = target_ids[0]
    places = lax.axis_index("seq") * source.shape[1] + jnp.arange(source.shape[1], dtype=jnp.int32)
    own_source_ids = jnp.where(places < source_len[0], source_ids[0], -1)
    ids = gather_row(jnp.concatenate([own_ids, own_source_ids]), seq)
    token_blocks = gather_row(tokens[0], seq)
    source_blocks = gather_row(source[0], seq)
    marks = key_marks(jnp.concatenate([part[:count] for part in ids]))
    source_marks = key_marks(jnp.concatenate([part[count:] for part in ids]))
    aux = query_marks(own_ids)

    all_tokens = jnp.concatenate(token_blocks, axis=0).astype(F32)
    all_normed, all_unit, all_inverse = normalize(all_tokens, norm_gain[0], norm_bias[0])
    all_normed = all_normed.astype(BF)
    tokens_full = tokens[0].astype(F32)
    own_normed = normalize(tokens_full, norm_gain[0], norm_bias[0])[0].astype(BF)
    queries = ((nn(own_normed, self_qkv[:, :width]) + proj_bias[0]) * scale).astype(BF)
    keys = nn(all_normed, self_qkv[:, width : 2 * width]).astype(BF)
    values = (nn(all_normed, self_qkv[:, 2 * width :]) + proj_bias[1]).astype(BF)
    mixed, self_aux = attend(queries, aux, keys, values, marks)
    first = tokens_full + nn(mixed, self_out) + out_bias[0]
    normed_two, unit_two, inverse_two = normalize(first, norm_gain[1], norm_bias[1])
    normed_two = normed_two.astype(BF)
    cross_queries = ((nn(normed_two, cross_q) + proj_bias[2]) * scale).astype(BF)
    all_source = jnp.concatenate(source_blocks, axis=0)
    cross_keys = nn(all_source, cross_kv[:, :width]).astype(BF)
    cross_values = (nn(all_source, cross_kv[:, width:]) + proj_bias[3]).astype(BF)
    cross_mixed, cross_aux = attend(cross_queries, aux, cross_keys, cross_values, source_marks)
    second = first + nn(cross_mixed, cross_out) + out_bias[1]
    normed_three, unit_three, inverse_three = normalize(second, norm_gain[2], norm_bias[2])
    normed_three = normed_three.astype(BF)
    hidden = nn(normed_three, ffn_in) + ffn_bias
    active, gelu_back = jax.vjp(jax.nn.gelu, hidden)
    active = active.astype(BF)
    output = (second + nn(active, ffn_out) + out_bias[2]).astype(BF)

    grad_low = out_grad[0]
    grad_full = grad_low.astype(F32)
    ffn_out_grad = tn(active, grad_low)
    grad_hidden = gelu_back(nt(grad_low, ffn_out))[0].astype(BF)
    ffn_in_grad = tn(normed_three, grad_hidden)
    ffn_bias_grad = jnp.sum(grad_hidden.astype(F32), axis=0)
    ffn_sum = lax.psum(jnp.concatenate([ffn_in_grad.reshape(-1, width), ffn_out_grad]).astype(BF), ("batch", "seq"))
    grad_three = nt(grad_hidden, ffn_in)
    vectors = {}
    vectors["gain2"] = jnp.sum(grad_three * unit_three, axis=0)
    vectors["shift2"] = jnp.sum(grad_three, axis=0)
    vectors["out2"] = jnp.sum(grad_full, axis=0)
    for k in range(4):
        vectors["ffn%d" % k] = ffn_bias_grad.reshape(4, width)[k]
    grad_second = grad_full + normalize_back(grad_three, unit_three, inverse_three, norm_gain[2])
    second_low = grad_second.astype(BF)
    cross_out_grad = tn(cross_mixed, second_low)
    vectors["out1"] = jnp.sum(second_low.astype(F32), axis=0)
    grad_cross_mixed = nt(second_low, cross_out).astype(BF)
    grad_cross_queries, grad_cross_keys, grad_cross_values = attend_back(
        cross_queries, grad_cross_mixed, cross_mixed, cross_aux, cross_keys, cross_values, source_marks
    )
    cross_q_grad = tn(normed_two, grad_cross_queries)
    vectors["proj2"] = jnp.sum(grad_cross_queries.astype(F32), axis=0)
    vectors["proj3"] = jnp.sum(grad_cross_values.astype(F32), axis=0)
    cross_k_grad = tn(all_source, grad_cross_keys)
    cross_v_grad = tn(all_source, grad_cross_values)
    source_part = (
        nt(grad_cross_keys, cross_kv[:, :width]) + nt(grad_cross_values, cross_kv[:, width:])
    ).astype(BF)
    source_grad = scatter_row(jnp.split(source_part, seq), seq).astype(BF)
    grad_two = nt(grad_cross_queries, cross_q)
    vectors["gain1"] = jnp.sum(grad_two * unit_two, axis=0)
    vectors["shift1"] = jnp.sum(grad_two, axis=0)
    grad_first = grad_second + normalize_back(grad_two, unit_two, inverse_two, norm_gain[1])
    first_low = grad_first.astype(BF)
    self_out_grad = tn(mixed, first_low)
    vectors["out0"] = jnp.sum(first_low.astype(F32), axis=0)
    grad_mixed = nt(first_low, self_out).astype(BF)

    def pack(arrays, names):
        small = jnp.stack([vectors[name] for name in names])
        small = jnp.pad(small, ((0, 128 - len(names)), (0, 0))).T
        return jnp.concatenate([item.astype(BF) for item in arrays] + [small.astype(BF)], axis=1)

    early = ["gain2", "shift2", "out2", "ffn0", "ffn1", "ffn2", "ffn3", "out1", "proj2", "proj3", "gain1", "shift1", "out0"]
    middle = sum_all(pack([cross_out_grad, cross_q_grad, cross_k_grad, cross_v_grad, self_out_grad], early), seq, batch)

    grad_queries, grad_keys, grad_values = attend_back(
        queries, grad_mixed, mixed, self_aux, keys, values, marks
    )
    vectors["proj0"] = jnp.sum(grad_queries.astype(F32), axis=0)
    vectors["proj1"] = jnp.sum(grad_values.astype(F32), axis=0)
    part = nt(grad_keys, self_qkv[:, width : 2 * width]) + nt(grad_values, self_qkv[:, 2 * width :])
    own_part = nt(grad_queries, self_qkv[:, :width])
    blocks = [part[k * count : (k + 1) * count] for k in range(seq)]
    blocks[0] = blocks[0] + own_part
    vectors["gain0"] = sum(
        jnp.sum(blocks[k] * all_unit[k * count : (k + 1) * count], axis=0) for k in range(seq)
    )
    vectors["shift0"] = sum(jnp.sum(blocks[k], axis=0) for k in range(seq))
    grad_one = scatter_row([blocks[k].astype(BF) for k in range(seq)], seq)
    query_grad = tn(own_normed, grad_queries)
    key_grad = tn(all_normed, grad_keys)
    value_grad = tn(all_normed, grad_values)
    late = ["proj0", "proj1", "gain0", "shift0"]
    last = sum_all(pack([query_grad, key_grad, value_grad], late), seq, batch)
    own_unit, own_inverse = all_unit[:count], all_inverse[:count]
    tokens_grad = (
        grad_first + normalize_back(grad_one.astype(F32), own_unit, own_inverse, norm_gain[0])
    ).astype(BF)

    middle = middle.astype(F32)
    last = last.astype(F32)
    ffn_sum = ffn_sum.astype(F32)
    sums = dict(zip(early, middle[:, 5 * width :].T))
    sums.update(zip(late, last[:, 3 * width :].T))
    hidden_rows = ffn_in.shape[0] * ffn_in.shape[1] // width
    return (
        output[None],
        tokens_grad[None],
        source_grad[None],
        last[:, : 3 * width],
        middle[:, 4 * width : 5 * width],
        middle[:, width : 2 * width],
        middle[:, 2 * width : 4 * width],
        middle[:, :width],
        ffn_sum[:hidden_rows].reshape(ffn_in.shape),
        ffn_sum[hidden_rows:],
        jnp.stack([sums["gain0"], sums["gain1"], sums["gain2"]]),
        jnp.stack([sums["shift0"], sums["shift1"], sums["shift2"]]),
        jnp.stack([sums["proj0"], sums["proj1"], sums["proj2"], sums["proj3"]]),
        jnp.stack([sums["out0"], sums["out1"], sums["out2"]]),
        jnp.concatenate([sums["ffn%d" % k] for k in range(4)]),
    )


def solution(mesh):
    row = P("batch", "seq", None)
    flat = P("batch", "seq")
    return jax.shard_map(
        functools.partial(body, mesh.shape["seq"], mesh.shape["batch"]),
        mesh=mesh,
        in_specs=(row, row, row, flat, flat, P("batch")) + (P(),) * 12,
        out_specs=(row, row, row) + (P(),) * 12,
        check_vma=False,
    )
```

time: 871 us -> 521 us (0.60)
  matrix products: 306 us -> 83.5 us
  Pallas kernels: 0 us -> 123 us
  waiting for transfers between devices: 266 us -> 145 us
  local copies, waits for them, and re-layouts: 149 us -> 56 us
  blocking collectives: 53.6 us -> 0 us
  starting transfers between devices: 0.54 us -> 27.2 us
    dot_general x84 -> x30, matrix products: 306 us -> 83.5 us  [the longest x10 29.1 us: nt(): lax.dot_general(left, right, (((1,), (1,)), ((), ())), preferred_element_...]
    psum x1, waiting for transfers between devices: 215 us -> 0.01 us  [body(): lax.psum(jnp.concatenate([ffn_in_grad.reshape(-1, width), ffn_out_grad])....]
    ppermute x0 -> x35, waiting for transfers between devices: none -> 145 us  [swap(): return lax.ppermute(value, axis, [(i, i ^ step) for i in range(size)])]
    pallas_call x0 -> x4, Pallas kernels: none -> 123 us  [the longest x2 81.3 us: attend_back(): pl.pallas_call(functools.partial(backward_kernel, block=math.gcd(count, 5...]
    unnamed x243 -> x132, local copies, waits for them, and re-layouts: 88.9 us -> 17 us
    reduce_scatter x2 -> x0, waiting for transfers between devices: 49.4 us -> none  [the longest x1 40.6 us: body(): lax.psum_scatter(grad_keys.astype(jnp.bfloat16), 'seq', scatter_dimension...]
    psum x1 -> x0, blocking collectives: 42 us -> none  [body(): lax.psum((ffn_in_grad, ffn_out_grad, ffn_bias_grad, gain_three, shift_thr...]
    ppermute x0 -> x35, starting transfers between devices: none -> 27.1 us  [swap(): return lax.ppermute(value, axis, [(i, i ^ step) for i in range(size)])]
  transfers between devices with their start and end apart: 8 -> 36, of which waited for: 3 -> 18; matrix products, arithmetic and copies ran while one was open for 34% -> 15% of each run, Pallas kernels for 0% -> 0%
where the time goes in v1:
time: 521 us; the launch traced here: 517 us
  waiting for transfers between devices  145 us (28%)
  Pallas kernels  123 us (24%)
  matrix products  83.5 us (16%)
  other arithmetic  66.2 us (13%)
  local copies, waits for them, and re-layouts  56 us (11%)
  starting transfers between devices  27.2 us (5%)
  between operations  16.4 us (3%)
    ppermute x35, waiting for transfers between devices, swap(): return lax.ppermute(value, axis, [(i, i ^ step) for i in range(size)])  145 us
    pallas_call x2, Pallas kernels, attend_back(): pl.pallas_call(functools.partial(backward_kernel, block=math.gcd(count, 5...  81.3 us
    pallas_call x2, Pallas kernels, attend(): pl.pallas_call(functools.partial(forward_kernel, block=block), grid=(widt...  41.8 us
    dot_general x10, matrix products, nt(): lax.dot_general(left, right, (((1,), (1,)), ((), ())), preferred_element_...  29.1 us
    dot_general x10, matrix products, nn(): lax.dot_general(left, right, (((1,), (0,)), ((), ())), preferred_element_...  28.4 us
    ppermute x35, starting transfers between devices, swap(): return lax.ppermute(value, axis, [(i, i ^ step) for i in range(size)])  27.1 us
    dot_general x10, matrix products, tn(): lax.dot_general(left, right, (((0,), (0,)), ((), ())), preferred_element_...  26 us
    unnamed x132, local copies, waits for them, and re-layouts  17 us
  transfers between devices with their start and end apart: 36, of which 18 were waited for; matrix products, arithmetic and copies ran while one was open for 15% of the time, Pallas kernels for 0%

profile of v1, /device:TPU:0, one launch (start us, length us, event | category | flops | bytes accessed | tf_op | source)
XLA Modules:
  0.0 517.0 jit_solution(3468648348625306814)
XLA Ops:
  24.7 3.5 fusion.25.e_ref
  28.4 12.8 %collective-permute-done.1 = bf16[768,512]{0,1:T(8,128)(2,1)} collective-permute-done((bf16[768,512]{0,1:T(8,128)(2,1)S(1)}, bf16[768,512]{0,1:T(8,128)(2,1)}, u32[]{:S(2)}, u32[]{:S(2)}) %collective-permute-start.1) | collective-permute-done | bytes 786464 | tf_op jit(solution)/shard_map/ppermute | solution.py:211
  43.0 3.6 convolution_convert_fusion.1.k_ref
  54.4 5.0 fusion
  59.4 3.5 convolution_convert_fusion.k_ref
  62.9 3.5 add_convert_fusion.v_ref
  66.4 26.1 %attend.2 = (bf16[768,512]{1,0:T(8,128)(2,1)}, bf16[8,768,128]{2,1,0:T(8,128)(2,1)}) custom-call(bf16[768,512]{1,0:T(8,128)(2,1)} %multiply_convert_fusion.2.q_ref, bf16[768,128]{1,0:T(8,128)(2,1)} %select_convert_fusion.aux_ref, bf16[3072,512]{1,0:T(8,128)(2,1)} %convolution_convert_fusion.k_ref, bf16[3072,512]{1,0:T(8,128)(2,1)} %add_convert_fusion.v_ref, ...), custom_call_target="tpu_custom_call" | custom-call | tf_op jit(solution)/shard_map/attend/pallas_call | solution.py:93
  97.2 15.7 %attend.3 = (bf16[768,512]{1,0:T(8,128)(2,1)}, bf16[8,768,128]{2,1,0:T(8,128)(2,1)}) custom-call(bf16[768,512]{1,0:T(8,128)(2,1)} %multiply_convert_fusion.1.q_ref, bf16[768,128]{1,0:T(8,128)(2,1)} %select_convert_fusion.aux_ref, bf16[1536,512]{1,0:T(8,128)(2,1)} %convolution_convert_fusion.1.k_ref, bf16[1536,512]{1,0:T(8,128)(2,1)} %fusion.10.v_ref, ...), custom_call_target="tpu_custom_call" | custom-call | tf_op jit(solution)/shard_map/attend/pallas_call | solution.py:93
  117.6 4.2 convolution_convert_fusion.2
  121.8 5.6 %fusion.82 = (bf16[2048]{0:T(1024)(128)(2,1)S(1)}, bf16[768,2048]{1,0:T(8,128)(2,1)S(1)}) fusion(f32[768,2048]{1,0:T(8,128)S(1)} %fusion.69, f32[2048]{0:T(1024)S(1)} %copy-done.58, bf16[2048,512]{1,0:T(8,128)(2,1)S(1)} %copy-done, bf16[1,768,512]{2,1,0:T(8,128)(2,1)S(1)} %copy-done.28), kind=kOutput, calls=%fused_computation.243 | convolution fusion | flops 1645213696 | bytes 12333056 | tf_op jit(solution)/shard_map/dot_general | solution.py:25
  144.2 28.2 %attend_back.2 = (bf16[768,512]{1,0:T(8,128)(2,1)}, bf16[1536,512]{1,0:T(8,128)(2,1)}, bf16[1536,512]{1,0:T(8,128)(2,1)}) custom-call(bf16[768,512]{1,0:T(8,128)(2,1)} %multiply_convert_fusion.1.q_ref, bf16[768,512]{1,0:T(8,128)(2,1)} %convolution_convert_fusion.5.do_ref, bf16[768,512]{1,0:T(8,128)(2,1)} %get-tuple-element.26.mix_ref, ...), custom_call_target="tpu_custom_call" | custom-call | tf_op jit(solution)/shard_map/attend_back/pallas_call | solution.py:169
  188.9 53.2 %attend_back.3 = (bf16[768,512]{1,0:T(8,128)(2,1)}, bf16[3072,512]{1,0:T(8,128)(2,1)}, bf16[3072,512]{1,0:T(8,128)(2,1)}) custom-call(bf16[768,512]{1,0:T(8,128)(2,1)} %multiply_convert_fusion.2.q_ref, bf16[768,512]{1,0:T(8,128)(2,1)} %convolution_convert_fusion.4.do_ref, bf16[768,512]{1,0:T(8,128)(2,1)} %get-tuple-element.25.mix_ref, ...), custom_call_target="tpu_custom_call" | custom-call | tf_op jit(solution)/shard_map/attend_back/pallas_call | solution.py:169
  242.1 4.8 convolution_convert_fusion.9
  247.0 5.6 %fusion.46 = f32[3072,512]{0,1:T(8,128)} fusion(bf16[3072,512]{1,0:T(8,128)(2,1)S(1)} %copy-done.24, bf16[512,1536]{1,0:T(8,128)(2,1)} %param.24), kind=kOutput, calls=%fused_computation.136 | convolution fusion | flops 1610612736 | bytes 9961472 | tf_op jit(solution)/shard_map/dot_general | solution.py:25
  252.6 4.0 fusion.26
  256.7 4.5 reshape.281
  291.7 3.6 slice_add_fusion
  313.8 21.5 %collective-permute-done.11 = bf16[768,512]{0,1:T(8,128)(2,1)S(1)} collective-permute-done((bf16[768,512]{0,1:T(8,128)(2,1)S(1)}, bf16[768,512]{0,1:T(8,128)(2,1)S(1)}, u32[]{:S(2)}, u32[]{:S(2)}) %collective-permute-start.11) | collective-permute-done | bytes 786464 | tf_op jit(solution)/shard_map/ppermute | solution.py:211
  335.3 5.2 %fusion.21 = (f32[512]{0:T(512)S(1)}, f32[512]{0:T(512)S(1)}, f32[512]{0:T(512)S(1)}, f32[512]{0:T(512)S(1)}, f32[512]{0:T(512)S(1)}, /*index=5*/f32[512]{0:T(51...) fusion(f32[3072,512]{0,1:T(8,128)} %get-tuple-element.171, ...), kind=kLoop, calls=%fused_computation.48 | loop fusion | flops 8645120 | bytes 15753216 | tf_op jit(solution)/shard_map/reduce_sum | solution.py:384
  342.4 8.7 %collective-permute-done.26 = bf16[128,2688]{1,0:T(8,128)(2,1)S(1)} collective-permute-done((bf16[128,2688]{1,0:T(8,128)(2,1)S(1)}, bf16[128,2688]{1,0:T(8,128)(2,1)S(1)}, u32[]{:S(2)}, u32[]{:S(2)}) %collective-permute-start.26) | collective-permute-done | bytes 688160 | tf_op jit(solution)/shard_map/ppermute | solution.py:211
  355.0 5.8 %collective-permute-done.27 = bf16[64,2688]{1,0:T(8,128)(2,1)S(1)} collective-permute-done((bf16[64,2688]{1,0:T(8,128)(2,1)}, bf16[64,2688]{1,0:T(8,128)(2,1)S(1)}, u32[]{:S(2)}, u32[]{:S(2)}) %collective-permute-start.27) | collective-permute-done | bytes 344096 | tf_op jit(solution)/shard_map/ppermute | solution.py:211
  362.6 3.8 collective-permute-done.28
  382.0 5.2 collective-permute-done.17
  389.7 12.9 %collective-permute-done.18 = bf16[32,1664]{0,1:T(8,128)(2,1)S(1)} collective-permute-done((bf16[32,1664]{0,1:T(8,128)(2,1)S(1)}, bf16[32,1664]{0,1:T(8,128)(2,1)S(1)}, u32[]{:S(2)}, u32[]{:S(2)}) %collective-permute-start.18) | collective-permute-done | bytes 106528 | tf_op jit(solution)/shard_map/ppermute | solution.py:211
  404.6 25.4 %collective-permute-done.19 = bf16[16,1664]{0,1:T(8,128)(2,1)S(1)} collective-permute-done((bf16[16,1664]{0,1:T(8,128)(2,1)S(1)}, bf16[16,1664]{0,1:T(8,128)(2,1)S(1)}, u32[]{:S(2)}, u32[]{:S(2)}) %collective-permute-start.19) | collective-permute-done | bytes 53280 | tf_op jit(solution)/shard_map/ppermute | solution.py:211
  431.4 17.7 %collective-permute-done.20 = bf16[16,1664]{0,1:T(8,128)(2,1)S(1)} collective-permute-done((bf16[16,1664]{0,1:T(8,128)(2,1)S(1)}, bf16[16,1664]{0,1:T(8,128)(2,1)S(1)}, u32[]{:S(2)}, u32[]{:S(2)}) %collective-permute-start.20) | collective-permute-done | bytes 53280 | tf_op jit(solution)/shard_map/ppermute | solution.py:211
  450.0 6.3 %collective-permute-done.21 = bf16[32,1664]{1,0:T(8,128)(2,1)S(1)} collective-permute-done((bf16[32,1664]{1,0:T(8,128)(2,1)S(1)}, bf16[32,1664]{1,0:T(8,128)(2,1)S(1)}, u32[]{:S(2)}, u32[]{:S(2)}) %collective-permute-start.21) | collective-permute-done | bytes 106528 | tf_op jit(solution)/shard_map/ppermute | solution.py:211
  458.5 3.8 collective-permute-done.22
  462.7 6.7 %collective-permute-done.33 = bf16[128,2688]{1,0:T(8,128)(2,1)S(1)} collective-permute-done((bf16[128,2688]{1,0:T(8,128)(2,1)S(1)}, bf16[128,2688]{1,0:T(8,128)(2,1)S(1)}, u32[]{:S(2)}, u32[]{:S(2)}) %collective-permute-start.33) | collective-permute-done | bytes 688160 | tf_op jit(solution)/shard_map/ppermute | solution.py:211
  469.7 4.3 collective-permute-done.23
  476.0 6.7 %fusion.71 = (f32[2048,512]{1,0:T(8,128)}, f32[2048,512]{1,0:T(8,128)}) fusion(bf16[4096,512]{1,0:T(8,128)(2,1)} %all-reduce.4.cloned.1.call-done), kind=kLoop, calls=%fused_computation.232 | loop fusion | bytes 16777216 | tf_op jit(solution)/shard_map/slice | solution.py:414
  482.7 5.6 %reshape.282 = f32[512,2048]{1,0:T(8,128)} reshape(f32[2048,512]{1,0:T(8,128)} %get-tuple-element.170) | data formatting | bytes 8388608 | tf_op jit(solution)/shard_map/reshape | solution.py:413
  (367 shorter events, 173.6 us)
Async XLA Ops:
  7.2 468.8 %all-reduce.4.cloned.1.call-start = ((), (), s32[]{:S(2)}) async-start(), calls=%async_computation | async-start | bytes 8388608 | tf_op jit(solution)/shard_map/psum | solution.py:332
  9.5 10.8 %collective-permute-start.4 = (s32[1152]{0:T(1024)S(1)}, s32[1152]{0:T(1024)S(1)}, u32[]{:S(2)}, u32[]{:S(2)}) collective-permute-start(s32[1152]{0:T(1024)S(1)} %pad_add_fusion.1), channel_id=1, source_target_pairs={{0,2},{1,3},{2,0},{3,1},{4,6},{5,7},{6,4},{7,5},{8,10},{9,11},{10,... | collective-permute-start | bytes 13832 | tf_op jit(solution)/shard_map/ppermute | solution.py:211
  12.5 11.7 %collective-permute-start.3 = (s32[1152]{0:T(1024)S(1)}, s32[1152]{0:T(1024)S(1)}, u32[]{:S(2)}, u32[]{:S(2)}) collective-permute-start(s32[1152]{0:T(1024)S(1)} %pad_add_fusion.1), channel_id=1, source_target_pairs={{0,1},{1,0},{2,3},{3,2},{4,5},{5,4},{6,7},{7,6},{8,9},{9,8},{10,11... | collective-permute-start | bytes 13832 | tf_op jit(solution)/shard_map/ppermute | solution.py:211
  12.5 15.7 %collective-permute-start.7 = (bf16[384,512]{1,0:T(8,128)(2,1)}, bf16[384,512]{1,0:T(8,128)(2,1)}, u32[]{:S(2)}, u32[]{:S(2)}) collective-permute-start(bf16[384,512]{1,0:T(8,128)(2,1)} %bitcast.115), channel_id=1, source_target_pairs={{0,2},{1,3},{2,0},{3,1},{4,6},{5,7},{6,4},{7,5},{8,10},{9,11},{10,... | collective-permute-start | bytes 1179656 | tf_op jit(solution)/shard_map/ppermute | solution.py:211
  12.7 30.3 %collective-permute-start.6 = (bf16[384,512]{1,0:T(8,128)(2,1)}, bf16[384,512]{1,0:T(8,128)(2,1)}, u32[]{:S(2)}, u32[]{:S(2)}) collective-permute-start(bf16[384,512]{1,0:T(8,128)(2,1)} %bitcast.116), channel_id=1, source_target_pairs={{0,1},{1,0},{2,3},{3,2},{4,5},{5,4},{6,7},{7,6},{8,9},{9,8},{10,11... | collective-permute-start | bytes 1179656 | tf_op jit(solution)/shard_map/ppermute | solution.py:211
  14.4 26.8 %collective-permute-start.1 = (bf16[768,512]{0,1:T(8,128)(2,1)S(1)}, bf16[768,512]{0,1:T(8,128)(2,1)}, u32[]{:S(2)}, u32[]{:S(2)}) collective-permute-start(bf16[768,512]{0,1:T(8,128)(2,1)S(1)} %bitcast.83), channel_id=1, source_target_pairs={{0,2},{1,3},{2,0},{3,1},{4,6},{5,7},{6,4},{7,5},{8,10},{9,11},{10,... | collective-permute-start | bytes 2359304 | tf_op jit(solution)/shard_map/ppermute | solution.py:211
  24.2 25.7 %collective-permute-start = (bf16[768,512]{0,1:T(8,128)(2,1)S(1)}, bf16[768,512]{0,1:T(8,128)(2,1)S(1)}, u32[]{:S(2)}, u32[]{:S(2)}) collective-permute-start(bf16[768,512]{0,1:T(8,128)(2,1)S(1)} %bitcast.84), channel_id=1, source_target_pairs={{0,1},{1,0},{2,3},{3,2},{4,5},{5,4},{6,7},{7,6},{8,9},{9,8},{10,11... | collective-permute-start | bytes 2359304 | tf_op jit(solution)/shard_map/ppermute | solution.py:211
  28.2 14.7 %collective-permute-start.8 = (bf16[384,512]{1,0:T(8,128)(2,1)}, bf16[384,512]{1,0:T(8,128)(2,1)S(1)}, u32[]{:S(2)}, u32[]{:S(2)}) collective-permute-start(bf16[384,512]{1,0:T(8,128)(2,1)} %collective-permute-done.7), channel_id=1, source_target_pairs={{0,1},{1,0},{2,3},{3,2},{4,5},{5,4},{6,7},{7,6},{8,9},{9,8},{10,11... | collective-permute-start | bytes 1179656 | tf_op jit(solution)/shard_map/ppermute | solution.py:211
  41.2 8.6 %collective-permute-start.2 = (bf16[768,512]{0,1:T(8,128)(2,1)}, bf16[768,512]{0,1:T(8,128)(2,1)S(1)}, u32[]{:S(2)}, u32[]{:S(2)}) collective-permute-start(bf16[768,512]{0,1:T(8,128)(2,1)} %collective-permute-done.1), channel_id=1, source_target_pairs={{0,1},{1,0},{2,3},{3,2},{4,5},{5,4},{6,7},{7,6},{8,9},{9,8},{10,11... | collective-permute-start | bytes 2359304 | tf_op jit(solution)/shard_map/ppermute | solution.py:211
  277.9 33.4 %collective-permute-start.25 = (bf16[256,2688]{1,0:T(8,128)(2,1)}, bf16[256,2688]{1,0:T(8,128)(2,1)}, u32[]{:S(2)}, u32[]{:S(2)}) collective-permute-start(bf16[256,2688]{1,0:T(8,128)(2,1)} %constant_dynamic-slice_fusion.4), channel_id=1, source_target_pairs={{0,1},{1,0},{2,3},{3,2},{4,5},{5,4},{6,7},{7,6},{8,9},{9,8},{10,11... | collective-permute-start | bytes 4128776 | tf_op jit(solution)/shard_map/ppermute | solution.py:211
  280.2 28.0 %collective-permute-start.12 = (bf16[384,512]{1,0:T(8,128)(2,1)}, bf16[384,512]{1,0:T(8,128)(2,1)}, u32[]{:S(2)}, u32[]{:S(2)}) collective-permute-start(bf16[384,512]{1,0:T(8,128)(2,1)} %get-tuple-element.180), channel_id=1, source_target_pairs={{0,1},{1,0},{2,3},{3,2},{4,5},{5,4},{6,7},{7,6},{8,9},{9,8},{10,11... | collective-permute-start | bytes 1179656 | tf_op jit(solution)/shard_map/ppermute | solution.py:211
  280.7 14.7 %collective-permute-start.13 = (bf16[384,512]{1,0:T(8,128)(2,1)S(1)}, bf16[384,512]{1,0:T(8,128)(2,1)}, u32[]{:S(2)}, u32[]{:S(2)}) collective-permute-start(bf16[384,512]{1,0:T(8,128)(2,1)S(1)} %get-tuple-element.181), channel_id=1, source_target_pairs={{0,1},{1,0},{2,3},{3,2},{4,5},{5,4},{6,7},{7,6},{8,9},{9,8},{10,11... | collective-permute-start | bytes 1179656 | tf_op jit(solution)/shard_map/ppermute | solution.py:211
  288.6 15.9 %collective-permute-start.10 = (bf16[768,512]{0,1:T(8,128)(2,1)}, bf16[768,512]{0,1:T(8,128)(2,1)}, u32[]{:S(2)}, u32[]{:S(2)}) collective-permute-start(bf16[768,512]{0,1:T(8,128)(2,1)} %get-tuple-element.168), channel_id=1, source_target_pairs={{0,1},{1,0},{2,3},{3,2},{4,5},{5,4},{6,7},{7,6},{8,9},{9,8},{10,11... | collective-permute-start | bytes 2359304 | tf_op jit(solution)/shard_map/ppermute | solution.py:211
  297.3 11.8 %collective-permute-start.14 = (bf16[384,512]{1,0:T(8,128)(2,1)}, bf16[384,512]{1,0:T(8,128)(2,1)}, u32[]{:S(2)}, u32[]{:S(2)}) collective-permute-start(bf16[384,512]{1,0:T(8,128)(2,1)} %add_convert_fusion.15), channel_id=1, source_target_pairs={{0,2},{1,3},{2,0},{3,1},{4,6},{5,7},{6,4},{7,5},{8,10},{9,11},{10,... | collective-permute-start | bytes 1179656 | tf_op jit(solution)/shard_map/ppermute | solution.py:211
  304.2 9.6 %collective-permute-start.9 = (bf16[768,512]{0,1:T(8,128)(2,1)}, bf16[768,512]{0,1:T(8,128)(2,1)S(1)}, u32[]{:S(2)}, u32[]{:S(2)}) collective-permute-start(bf16[768,512]{0,1:T(8,128)(2,1)} %get-tuple-element.167), channel_id=1, source_target_pairs={{0,1},{1,0},{2,3},{3,2},{4,5},{5,4},{6,7},{7,6},{8,9},{9,8},{10,11... | collective-permute-start | bytes 2359304 | tf_op jit(solution)/shard_map/ppermute | solution.py:211
  306.5 28.9 %collective-permute-start.11 = (bf16[768,512]{0,1:T(8,128)(2,1)S(1)}, bf16[768,512]{0,1:T(8,128)(2,1)S(1)}, u32[]{:S(2)}, u32[]{:S(2)}) collective-permute-start(bf16[768,512]{0,1:T(8,128)(2,1)S(1)} %add_convert_fusion.5), channel_id=1, source_target_pairs={{0,2},{1,3},{2,0},{3,1},{4,6},{5,7},{6,4},{7,5},{8,10},{9,11},{10,... | collective-permute-start | bytes 2359304 | tf_op jit(solution)/shard_map/ppermute | solution.py:211
  313.4 37.7 %collective-permute-start.26 = (bf16[128,2688]{1,0:T(8,128)(2,1)S(1)}, bf16[128,2688]{1,0:T(8,128)(2,1)S(1)}, u32[]{:S(2)}, u32[]{:S(2)}) collective-permute-start(bf16[128,2688]{1,0:T(8,128)(2,1)S(1)} %constant_dynamic-slice_fusion.3), channel_id=1, source_target_pairs={{0,2},{1,3},{2,0},{3,1},{4,6},{5,7},{6,4},{7,5},{8,10},{9,11},{10,... | collective-permute-start | bytes 2064392 | tf_op jit(solution)/shard_map/ppermute | solution.py:211
  352.2 8.6 %collective-permute-start.27 = (bf16[64,2688]{1,0:T(8,128)(2,1)}, bf16[64,2688]{1,0:T(8,128)(2,1)S(1)}, u32[]{:S(2)}, u32[]{:S(2)}) collective-permute-start(bf16[64,2688]{1,0:T(8,128)(2,1)} %constant_dynamic-slice_fusion.2), channel_id=1, source_target_pairs={{0,4},{4,0},{8,12},{12,8},{16,20},{20,16},{24,28},{28,24},{1,5},{5... | collective-permute-start | bytes 1032200 | tf_op jit(solution)/shard_map/ppermute | solution.py:211
  355.0 7.4 %collective-permute-start.15 = (bf16[256,1664]{0,1:T(8,128)(2,1)S(1)}, bf16[256,1664]{0,1:T(8,128)(2,1)S(1)}, u32[]{:S(2)}, u32[]{:S(2)}) collective-permute-start(bf16[256,1664]{0,1:T(8,128)(2,1)S(1)} %constant_dynamic-slice_fusion.9), channel_id=1, source_target_pairs={{0,1},{1,0},{2,3},{3,2},{4,5},{5,4},{6,7},{7,6},{8,9},{9,8},{10,11... | collective-permute-start | bytes 2555912 | tf_op jit(solution)/shard_map/ppermute | solution.py:211
  366.5 9.1 %collective-permute-start.29 = (bf16[16,2688]{1,0:T(8,128)(2,1)S(1)}, bf16[16,2688]{1,0:T(8,128)(2,1)S(1)}, u32[]{:S(2)}, u32[]{:S(2)}) collective-permute-start(bf16[16,2688]{1,0:T(8,128)(2,1)S(1)} %constant_dynamic-slice_fusion), channel_id=1, source_target_pairs={{0,16},{4,20},{8,24},{12,28},{16,0},{20,4},{24,8},{28,12},{1,17},{... | collective-permute-start | bytes 258056 | tf_op jit(solution)/shard_map/ppermute | solution.py:211
  369.9 8.7 %collective-permute-start.16 = (bf16[128,1664]{0,1:T(8,128)(2,1)S(1)}, bf16[128,1664]{0,1:T(8,128)(2,1)S(1)}, u32[]{:S(2)}, u32[]{:S(2)}) collective-permute-start(bf16[128,1664]{0,1:T(8,128)(2,1)S(1)} %constant_dynamic-slice_fusion.8), channel_id=1, source_target_pairs={{0,2},{1,3},{2,0},{3,1},{4,6},{5,7},{6,4},{7,5},{8,10},{9,11},{10,... | collective-permute-start | bytes 1277960 | tf_op jit(solution)/shard_map/ppermute | solution.py:211
  378.9 8.2 %collective-permute-start.17 = (bf16[64,1664]{0,1:T(8,128)(2,1)S(1)}, bf16[64,1664]{0,1:T(8,128)(2,1)S(1)}, u32[]{:S(2)}, u32[]{:S(2)}) collective-permute-start(bf16[64,1664]{0,1:T(8,128)(2,1)S(1)} %constant_dynamic-slice_fusion.7), channel_id=1, source_target_pairs={{0,4},{4,0},{8,12},{12,8},{16,20},{20,16},{24,28},{28,24},{1,5},{5... | collective-permute-start | bytes 638984 | tf_op jit(solution)/shard_map/ppermute | solution.py:211
  387.5 15.1 %collective-permute-start.18 = (bf16[32,1664]{0,1:T(8,128)(2,1)S(1)}, bf16[32,1664]{0,1:T(8,128)(2,1)S(1)}, u32[]{:S(2)}, u32[]{:S(2)}) collective-permute-start(bf16[32,1664]{0,1:T(8,128)(2,1)S(1)} %constant_dynamic-slice_fusion.6), channel_id=1, source_target_pairs={{0,8},{4,12},{8,0},{12,4},{16,24},{20,28},{24,16},{28,20},{1,9},{5... | collective-permute-start | bytes 319496 | tf_op jit(solution)/shard_map/ppermute | solution.py:211
  389.0 15.5 %collective-permute-start.31 = (bf16[32,2688]{1,0:T(8,128)(2,1)S(1)}, bf16[32,2688]{1,0:T(8,128)(2,1)S(1)}, u32[]{:S(2)}, u32[]{:S(2)}) collective-permute-start(bf16[32,2688]{1,0:T(8,128)(2,1)S(1)} %pad_maximum_fusion.10), channel_id=1, source_target_pairs={{0,8},{4,12},{8,0},{12,4},{16,24},{20,28},{24,16},{28,20},{1,9},{5... | collective-permute-start | bytes 516104 | tf_op jit(solution)/shard_map/ppermute | solution.py:211
  403.0 27.0 %collective-permute-start.19 = (bf16[16,1664]{0,1:T(8,128)(2,1)S(1)}, bf16[16,1664]{0,1:T(8,128)(2,1)S(1)}, u32[]{:S(2)}, u32[]{:S(2)}) collective-permute-start(bf16[16,1664]{0,1:T(8,128)(2,1)S(1)} %constant_dynamic-slice_fusion.5), channel_id=1, source_target_pairs={{0,16},{4,20},{8,24},{12,28},{16,0},{20,4},{24,8},{28,12},{1,17},{... | collective-permute-start | bytes 159752 | tf_op jit(solution)/shard_map/ppermute | solution.py:211
  430.2 18.9 %collective-permute-start.20 = (bf16[16,1664]{0,1:T(8,128)(2,1)S(1)}, bf16[16,1664]{0,1:T(8,128)(2,1)S(1)}, u32[]{:S(2)}, u32[]{:S(2)}) collective-permute-start(bf16[16,1664]{0,1:T(8,128)(2,1)S(1)} %add_convert_fusion.10), channel_id=1, source_target_pairs={{0,16},{4,20},{8,24},{12,28},{16,0},{20,4},{24,8},{28,12},{1,17},{... | collective-permute-start | bytes 159752 | tf_op jit(solution)/shard_map/ppermute | solution.py:211
  430.3 19.6 %collective-permute-start.32 = (bf16[64,2688]{1,0:T(8,128)(2,1)S(1)}, bf16[64,2688]{1,0:T(8,128)(2,1)S(1)}, u32[]{:S(2)}, u32[]{:S(2)}) collective-permute-start(bf16[64,2688]{1,0:T(8,128)(2,1)S(1)} %pad_maximum_fusion.8), channel_id=1, source_target_pairs={{0,4},{4,0},{8,12},{12,8},{16,20},{20,16},{24,28},{28,24},{1,5},{5... | collective-permute-start | bytes 1032200 | tf_op jit(solution)/shard_map/ppermute | solution.py:211
  449.5 6.8 %collective-permute-start.21 = (bf16[32,1664]{1,0:T(8,128)(2,1)S(1)}, bf16[32,1664]{1,0:T(8,128)(2,1)S(1)}, u32[]{:S(2)}, u32[]{:S(2)}) collective-permute-start(bf16[32,1664]{1,0:T(8,128)(2,1)S(1)} %pad_maximum_fusion.11), channel_id=1, source_target_pairs={{0,8},{4,12},{8,0},{12,4},{16,24},{20,28},{24,16},{28,20},{1,9},{5... | collective-permute-start | bytes 319496 | tf_op jit(solution)/shard_map/ppermute | solution.py:211
  458.4 11.0 %collective-permute-start.33 = (bf16[128,2688]{1,0:T(8,128)(2,1)S(1)}, bf16[128,2688]{1,0:T(8,128)(2,1)S(1)}, u32[]{:S(2)}, u32[]{:S(2)}) collective-permute-start(bf16[128,2688]{1,0:T(8,128)(2,1)S(1)} %pad_maximum_fusion.6), channel_id=1, source_target_pairs={{0,2},{1,3},{2,0},{3,1},{4,6},{5,7},{6,4},{7,5},{8,10},{9,11},{10,... | collective-permute-start | bytes 2064392 | tf_op jit(solution)/shard_map/ppermute | solution.py:211
  462.4 11.6 %collective-permute-start.23 = (bf16[128,1664]{1,0:T(8,128)(2,1)S(1)}, bf16[128,1664]{1,0:T(8,128)(2,1)S(1)}, u32[]{:S(2)}, u32[]{:S(2)}) collective-permute-start(bf16[128,1664]{1,0:T(8,128)(2,1)S(1)} %pad_maximum_fusion.7), channel_id=1, source_target_pairs={{0,2},{1,3},{2,0},{3,1},{4,6},{5,7},{6,4},{7,5},{8,10},{9,11},{10,... | collective-permute-start | bytes 1277960 | tf_op jit(solution)/shard_map/ppermute | solution.py:211
  474.2 14.1 %collective-permute-start.24 = (bf16[256,1664]{1,0:T(8,128)(2,1)S(1)}, bf16[256,1664]{1,0:T(8,128)(2,1)}, u32[]{:S(2)}, u32[]{:S(2)}) collective-permute-start(bf16[256,1664]{1,0:T(8,128)(2,1)S(1)} %pad_maximum_fusion.5), channel_id=1, source_target_pairs={{0,1},{1,0},{2,3},{3,2},{4,5},{5,4},{6,7},{7,6},{8,9},{9,8},{10,11... | collective-permute-start | bytes 2555912 | tf_op jit(solution)/shard_map/ppermute | solution.py:211
  475.5 17.2 %collective-permute-start.34 = (bf16[256,2688]{1,0:T(8,128)(2,1)}, bf16[256,2688]{1,0:T(8,128)(2,1)}, u32[]{:S(2)}, u32[]{:S(2)}) collective-permute-start(bf16[256,2688]{1,0:T(8,128)(2,1)} %pad_maximum_fusion.4), channel_id=1, source_target_pairs={{0,1},{1,0},{2,3},{3,2},{4,5},{5,4},{6,7},{7,6},{8,9},{9,8},{10,11... | collective-permute-start | bytes 4128776 | tf_op jit(solution)/shard_map/ppermute | solution.py:211
  (69 other events, 751.7 us)
Sparse Core Ops, SparseCore 0:
  304.3 162.2 all-reduce.3

commit v2 on v1

v2 whole, which is shorter than its diff:
```python
import functools
import math

import jax
import jax.numpy as jnp
from jax import lax
from jax.experimental import pallas as pl
from jax.experimental.pallas import tpu as pltpu
from jax.sharding import PartitionSpec as P

HEADS = 8
EPS = 1e-05
F32 = jnp.float32
BF = jnp.bfloat16
LN2 = math.log(2.0)
LOG2E = 1.0 / LN2
VMEM = 60 * 1024 * 1024
SCALE = 1.0 / 8.0
ROOT = math.sqrt(2.0 / math.pi)
CUBE = 0.044715


def nn(left, right):
    return lax.dot_general(left, right, (((1,), (0,)), ((), ())), preferred_element_type=F32)


def nt(left, right):
    return lax.dot_general(left, right, (((1,), (1,)), ((), ())), preferred_element_type=F32)


def tn(left, right):
    return lax.dot_general(left, right, (((0,), (0,)), ((), ())), preferred_element_type=F32)


def shape(rows, columns, kind=BF):
    return jax.ShapeDtypeStruct((rows, columns), kind)


def cost(micros):
    return pl.CostEstimate(flops=int(micros * 3e8), bytes_accessed=0, transcendentals=0)


def run(name, micros, kernel, inputs, outputs, after=(), scalars=(), scratch=()):
    whole = pl.BlockSpec(memory_space=pltpu.VMEM)
    small = pl.BlockSpec(memory_space=pltpu.SMEM)
    away = pl.BlockSpec(memory_space=pl.ANY)

    def wrapped(*refs):
        first = len(scalars) + len(inputs)
        kernel(*refs[:first], *refs[first + len(after) :])

    return pl.pallas_call(
        wrapped,
        in_specs=[small] * len(scalars) + [whole] * len(inputs) + [away] * len(after),
        out_specs=[whole] * len(outputs),
        out_shape=list(outputs),
        scratch_shapes=list(scratch),
        compiler_params=pltpu.CompilerParams(vmem_limit_bytes=VMEM),
        cost_estimate=cost(micros),
        name=name,
    )(*scalars, *inputs, *after)


def key_marks(ids):
    lane = lax.broadcasted_iota(jnp.int32, (128, ids.shape[1]), 0)
    hit = ((lane < 4) & (lane == ids)) | ((lane == 4) & (ids < 0)) | ((lane >= 5) & (lane <= 9))
    return jnp.where(hit, 1.0, 0.0).T.astype(BF)


def query_marks(ids):
    lane = lax.broadcasted_iota(jnp.int32, (128, ids.shape[1]), 0)
    shut = ((lane < 4) & (lane != ids)) | (lane == 4)
    return jnp.where(shut, -1e30, 0.0).T.astype(BF)


def forward_kernel(*refs, blocks, begun, ended):
    q_ref, aux_ref = refs[:2]
    key_refs = refs[2 : 2 + 3 * len(blocks)]
    lane = lax.broadcasted_iota(jnp.int32, (1, 128), 1)
    low = lane < 64
    zero = jnp.zeros((), BF)
    one = jnp.ones((), BF)
    q = q_ref[...]
    aux = aux_ref[...]
    done = []
    for head in range(2):
        mine = low if head == 0 else ~low
        spare = 127 if head == 0 else 63
        query = jnp.concatenate([jnp.where(mine, q, zero), aux], axis=1)
        peak = total = None
        if begun:
            total = refs[2 + 3 * len(blocks)][head]
            peak = jnp.max(jnp.where(lane == spare, total, -jnp.inf), axis=1, keepdims=True)
            total = jnp.where(lane == spare, pltpu.roll(total, 1, 1), total)
        for part, block in enumerate(blocks):
            k_ref, v_ref, e_ref = key_refs[3 * part : 3 * part + 3]
            for start in range(0, k_ref.shape[0], block):
                rows = pl.ds(start, block)
                scores = nt(query, jnp.concatenate([k_ref[rows, :], e_ref[rows, :]], axis=1))
                value = jnp.where(mine, v_ref[rows, :], one)
                largest = jnp.max(scores, axis=1, keepdims=True)
                if peak is None:
                    peak = largest
                    total = nn(jnp.exp2(scores - peak).astype(BF), value)
                else:
                    raised = jnp.maximum(peak, largest)
                    total = total * jnp.exp2(peak - raised) + nn(
                        jnp.exp2(scores - raised).astype(BF), value
                    )
                    peak = raised
        if not ended:
            refs[-1][head] = jnp.where(lane == spare, peak, total)
        done.append((total, peak))
    if not ended:
        return
    o_ref, aux_out_ref = refs[-2:]
    top = jnp.where(low, done[0][0], done[1][0])
    below = jnp.where(low, pltpu.roll(done[0][0], 64, 1), pltpu.roll(done[1][0], 64, 1))
    o_ref[...] = (top / below).astype(BF)
    for head in range(2):
        total, peak = done[head]
        weight = pltpu.roll(total, 64, 1) if head == 0 else total
        minus = -(peak + jnp.log2(jnp.where(low, weight, 1.0)))
        first = minus.astype(BF)
        rest = minus - first.astype(F32)
        second = rest.astype(BF)
        third = (rest - second.astype(F32)).astype(BF)
        aux_out_ref[head] = jnp.where(
            lane == 5, first, jnp.where(lane == 6, second, jnp.where(lane == 7, third, aux))
        )


def largest_block(count, most):
    return max(size for size in range(128, most + 1, 128) if count % size == 0)


def attend(queries, aux, keys, begun=None, ended=True):
    rows, width = queries.shape
    by_head = pl.BlockSpec((2, rows, 128), lambda i: (i, 0, 0))
    specs, flat = [], []
    for k, v, e in keys:
        count = k.shape[0]
        specs += [
            pl.BlockSpec((count, 128), lambda i: (0, i)),
            pl.BlockSpec((count, 128), lambda i: (0, i)),
            pl.BlockSpec((count, 128), lambda i: (0, 0)),
        ]
        flat += [k, v, e]
    if begun is not None:
        specs.append(by_head)
        flat.append(begun)
    blocks = [largest_block(k.shape[0], 1024) for k, v, e in keys]
    totals = jax.ShapeDtypeStruct((width // 64, rows, 128), F32)
    return pl.pallas_call(
        functools.partial(forward_kernel, blocks=blocks, begun=begun is not None, ended=ended),
        grid=(width // 128,),
        in_specs=[
            pl.BlockSpec((rows, 128), lambda i: (0, i)),
            pl.BlockSpec((rows, 128), lambda i: (0, 0)),
        ]
        + specs,
        out_specs=[pl.BlockSpec((rows, 128), lambda i: (0, i)), by_head] if ended else by_head,
        out_shape=[
            jax.ShapeDtypeStruct((rows, width), BF),
            jax.ShapeDtypeStruct((width // 64, rows, 128), BF),
        ]
        if ended
        else totals,
        compiler_params=pltpu.CompilerParams(vmem_limit_bytes=VMEM),
        cost_estimate=cost(26 * sum(k.shape[0] for k, v, e in keys) / 3072),
        name="attend",
    )(queries, aux, *flat)


def backward_kernel(*refs, blocks, fences):
    q_ref, do_ref, mix_ref, aux_ref = refs[:4]
    parts = len(blocks)
    key_refs = refs[4 : 4 + 3 * parts]
    dq_ref, *dkv_refs, dq_sum = refs[4 + 3 * parts + fences :]
    lane = lax.broadcasted_iota(jnp.int32, (1, 128), 1)
    low = lane < 64
    zero = jnp.zeros((), BF)
    q = q_ref[...]
    do = do_ref[...]
    product = do.astype(F32) * mix_ref[...].astype(F32)
    score_side, probs_side, query_side, grad_side = [], [], [], []
    for head in range(2):
        mine = low if head == 0 else ~low
        q_head = jnp.where(mine, q, zero)
        do_head = jnp.where(mine, do, zero)
        minus = -jnp.sum(jnp.where(mine, product, 0.0), axis=1, keepdims=True)
        first = minus.astype(BF)
        second = (minus - first.astype(F32)).astype(BF)
        extra = jnp.where(lane == 8, first, jnp.where(lane == 9, second, zero))
        score_side.append(jnp.concatenate([q_head, aux_ref[head]], axis=1))
        probs_side.append(jnp.concatenate([do_head, extra], axis=1))
        query_side.append(q_head)
        grad_side.append(do_head)
    fresh = True
    for part, block in enumerate(blocks):
        k_ref, v_ref, e_ref = key_refs[3 * part : 3 * part + 3]
        dk_ref, dv_ref = dkv_refs[2 * part : 2 * part + 2]
        for start in range(0, k_ref.shape[0], block):
            rows = pl.ds(start, block)
            k = k_ref[rows, :]
            e = e_ref[rows, :]
            key = jnp.concatenate([k, e], axis=1)
            value = jnp.concatenate([v_ref[rows, :], e], axis=1)
            dk = dv = None
            for head in range(2):
                mine = low if head == 0 else ~low
                probs = jnp.exp2(nt(key, score_side[head]))
                ds = (probs * nt(value, probs_side[head])).astype(BF)
                dv_head = nn(probs.astype(BF), grad_side[head])
                dk_head = nn(ds, query_side[head])
                dv = dv_head if head == 0 else dv + dv_head
                dk = dk_head if head == 0 else dk + dk_head
                piece = tn(jnp.where(mine, k, zero), ds)
                if fresh:
                    dq_sum[...] = piece
                    fresh = False
                else:
                    dq_sum[...] += piece
            dk_ref[rows, :] = (dk * LN2).astype(BF)
            dv_ref[rows, :] = dv.astype(BF)
    dq_ref[...] = (dq_sum[...].T * SCALE).astype(BF)


def attend_back(queries, grad_mixed, mixed, aux, keys, pairs, after=()):
    rows = queries.shape[0]
    base, number = pairs
    by_query = pl.BlockSpec((rows, 128), lambda i: (0, i + base))
    specs, flat, out_specs, out_shapes = [], [], [], []
    for k, v, e in keys:
        count = k.shape[0]
        specs += [
            pl.BlockSpec((count, 128), lambda i: (0, i + base)),
            pl.BlockSpec((count, 128), lambda i: (0, i + base)),
            pl.BlockSpec((count, 128), lambda i: (0, 0)),
        ]
        flat += [k, v, e]
        out_specs += [pl.BlockSpec((count, 128), lambda i: (0, i))] * 2
        out_shapes += [shape(count, 128 * number)] * 2
    return pl.pallas_call(
        functools.partial(
            backward_kernel,
            blocks=[largest_block(k.shape[0], 512) for k, v, e in keys],
            fences=len(after),
        ),
        grid=(number,),
        in_specs=[
            by_query,
            by_query,
            by_query,
            pl.BlockSpec((2, rows, 128), lambda i: (i + base, 0, 0)),
        ]
        + specs
        + [pl.BlockSpec(memory_space=pl.ANY)] * len(after),
        out_specs=[pl.BlockSpec((rows, 128), lambda i: (0, i))] + out_specs,
        out_shape=[shape(rows, 128 * number)] + out_shapes,
        scratch_shapes=[pltpu.VMEM((128, rows), F32)],
        compiler_params=pltpu.CompilerParams(vmem_limit_bytes=VMEM),
        cost_estimate=cost(14 * number * sum(k.shape[0] for k, v, e in keys) / 3072),
        name="attend_back",
    )(queries, grad_mixed, mixed, aux, *flat, *after)


def normalize(value):
    centred = value - jnp.mean(value, axis=-1, keepdims=True)
    inverse = lax.rsqrt(jnp.mean(centred * centred, axis=-1, keepdims=True) + EPS)
    return centred * inverse, inverse


def normalize_back(grad_output, unit, inverse, gain):
    scaled = grad_output * gain
    inner = (
        scaled
        - jnp.mean(scaled, axis=-1, keepdims=True)
        - unit * jnp.mean(scaled * unit, axis=-1, keepdims=True)
    )
    return inner * inverse


def columns_sum(value):
    return jnp.sum(value, axis=0, keepdims=True)


def write_out(total, place, keep_ref, send_ref):
    half = total.shape[0] // 2
    for r, ref in enumerate([keep_ref, send_ref]):
        rows = pl.ds(pl.multiple_of((place[0] ^ r) * half, half), half)
        ref[...] = total[rows, :].astype(BF)


def project_kernel(*refs, count, queries, source):
    token_refs = refs[:count]
    id_refs = refs[count : 2 * count]
    rest = refs[2 * count :]
    if source:
        source_ref, *rest = rest
        rest[8][...] = source_ref[...]
    gain_ref, shift_ref, weight_ref, bias_ref = rest[:4]
    n_ref, k_ref, v_ref, e_ref = rest[4:8]
    rows = token_refs[0].shape[0]
    width = token_refs[0].shape[1]
    for place in range(count):
        unit, _ = normalize(token_refs[place][...].astype(F32))
        normed = (unit * gain_ref[0:1, :] + shift_ref[0:1, :]).astype(BF)
        here = pl.ds(place * rows, rows)
        n_ref[here, :] = normed
        k_ref[here, :] = nn(normed, weight_ref[:, width : 2 * width]).astype(BF)
        v_ref[here, :] = (nn(normed, weight_ref[:, 2 * width :]) + bias_ref[1:2, :]).astype(BF)
        ids = id_refs[place][:, :rows]
        e_ref[here, :] = key_marks(ids)
        if queries and place == 0:
            q_ref, aux_ref = rest[8:10]
            joined = nn(normed, weight_ref[:, :width]) + bias_ref[0:1, :]
            q_ref[...] = (joined * (SCALE * LOG2E)).astype(BF)
            aux_ref[...] = query_marks(ids)


def project(tokens, ids, norm_gain, norm_bias, self_qkv, proj_bias, queries=False, source=(), after=()):
    count = len(tokens)
    rows, width = tokens[0].shape
    inputs = [*tokens, *ids, *source, norm_gain, norm_bias, self_qkv, proj_bias]
    outputs = [shape(count * rows, width)] * 3 + [shape(count * rows, 128)]
    if queries:
        outputs += [shape(rows, width), shape(rows, 128)]
    outputs += [shape(*item.shape) for item in source]
    return run(
        "project",
        6,
        functools.partial(project_kernel, count=count, queries=queries, source=bool(source)),
        inputs,
        outputs,
        after,
    )


def after_self_kernel(mixed, tokens, out, out_bias, gain, shift, cross_q, bias, first_ref, n_ref, q_ref):
    first = tokens[...].astype(F32) + nn(mixed[...], out[...]) + out_bias[0:1, :]
    first_ref[...] = first
    unit, _ = normalize(first)
    normed = (unit * gain[1:2, :] + shift[1:2, :]).astype(BF)
    n_ref[...] = normed
    q_ref[...] = ((nn(normed, cross_q[...]) + bias[2:3, :]) * (SCALE * LOG2E)).astype(BF)


def source_kernel(row_info, *refs, count):
    source_refs = refs[:count]
    id_refs = refs[count : 2 * count]
    weight, bias, k_ref, v_ref, e_ref = refs[2 * count :]
    rows, width = source_refs[0].shape
    for place in range(count):
        here = pl.ds(place * rows, rows)
        joined = nn(source_refs[place][...], weight[...])
        k_ref[here, :] = joined[:, :width].astype(BF)
        v_ref[here, :] = (joined[:, width:] + bias[3:4, :]).astype(BF)
        ids = id_refs[place][:, -rows:]
        spot = (row_info[1] ^ place) * rows + lax.broadcasted_iota(jnp.int32, ids.shape, 1)
        e_ref[here, :] = key_marks(jnp.where(spot < row_info[0], ids, -1))


def ffn_kernel(
    mixed,
    first,
    cross_out,
    out_bias,
    gain,
    shift,
    ffn_in,
    ffn_bias,
    ffn_out,
    out_grad,
    output_ref,
    grad_second_ref,
    grad_mixed_ref,
    grads_ref,
    sums_ref,
    active_ref,
    hidden_ref,
    normed_ref,
    second_ref,
):
    rows = mixed.shape[0]
    tile = rows // 3
    width = mixed.shape[1]
    sums = [0.0] * 4
    bias_sum = 0.0
    for start in range(0, rows, tile):
        here = pl.ds(start, tile)
        second = first[here, :] + nn(mixed[here, :], cross_out[...]) + out_bias[1:2, :]
        unit, inverse = normalize(second)
        normed = (unit * gain[2:3, :] + shift[2:3, :]).astype(BF)
        normed_ref[here, :] = normed
        grad = out_grad[here, :]
        hidden = nn(normed, ffn_in[...]) + ffn_bias[...]
        square = hidden * hidden
        bend = jnp.tanh(ROOT * (hidden + CUBE * (square * hidden)))
        half = 0.5 * (1.0 + bend)
        active = (hidden * half).astype(BF)
        active_ref[here, :] = active
        slope = half + 0.5 * hidden * (1.0 - bend * bend) * (ROOT * (1.0 + 3.0 * CUBE * square))
        grad_hidden32 = nt(grad, ffn_out[...]) * slope
        grad_hidden = grad_hidden32.astype(BF)
        hidden_ref[here, :] = grad_hidden
        bias_sum = bias_sum + columns_sum(grad_hidden.astype(F32))
        output_ref[here, :] = (second + nn(active, ffn_out[...]) + out_bias[2:3, :]).astype(BF)
        grad_three = nt(grad_hidden, ffn_in[...])
        grad32 = grad.astype(F32)
        sums[0] = sums[0] + columns_sum(grad_three * unit)
        sums[1] = sums[1] + columns_sum(grad_three)
        sums[2] = sums[2] + columns_sum(grad32)
        grad_second = grad32 + normalize_back(grad_three, unit, inverse, gain[2:3, :])
        grad_second_ref[here, :] = grad_second
        second_low = grad_second.astype(BF)
        second_ref[here, :] = second_low
        sums[3] = sums[3] + columns_sum(second_low.astype(F32))
        grad_mixed_ref[here, :] = nt(second_low, cross_out[...]).astype(BF)
    units = hidden_ref.shape[1]
    grads_ref[:, :units] = tn(normed_ref[...], hidden_ref[...]).astype(BF)
    for k in range(units // width):
        here = slice(k * width, (k + 1) * width)
        grads_ref[:, units + k * width : units + (k + 1) * width] = tn(
            active_ref[:, here], out_grad[...]
        ).astype(BF)
    grads_ref[:, 2 * units :] = tn(mixed[...], second_ref[...]).astype(BF)
    for k in range(4):
        sums_ref[k : k + 1, :] = sums[k]
        sums_ref[4 + k : 5 + k, :] = bias_sum[:, k * width : (k + 1) * width]


def after_cross_kernel(
    dq_ref,
    cross_q,
    first,
    normed,
    grad_second,
    gain,
    mixed,
    self_out,
    grad_first_ref,
    grad_mixed_ref,
    cross_q_grad,
    self_out_grad,
    sums_ref,
):
    dq = dq_ref[...]
    grad_two = nt(dq, cross_q[...])
    unit, inverse = normalize(first[...])
    grad_first = grad_second[...] + normalize_back(grad_two, unit, inverse, gain[1:2, :])
    grad_first_ref[...] = grad_first
    low = grad_first.astype(BF)
    grad_mixed_ref[...] = nt(low, self_out[...]).astype(BF)
    cross_q_grad[...] = tn(normed[...], dq)
    self_out_grad[...] = tn(mixed[...], low)
    sums_ref[0:1, :] = columns_sum(grad_two * unit)
    sums_ref[1:2, :] = columns_sum(grad_two)
    sums_ref[2:3, :] = columns_sum(low.astype(F32))
    sums_ref[3:4, :] = columns_sum(dq.astype(F32))
    sums_ref[4:8, :] = jnp.zeros((4, dq.shape[1]), F32)


def source_back_kernel(*refs, count):
    places, dk_ref, dv_ref, weight = refs[:4]
    source_refs = refs[4 : 4 + count]
    cross_q_grad, self_out_grad, sums_a, sums_b = refs[4 + count : 8 + count]
    part_refs = refs[8 + count : 8 + 2 * count]
    keep_ref, send_ref, total = refs[8 + 2 * count :]
    rows, width = source_refs[0].shape
    dk = dk_ref[...]
    dv = dv_ref[...]
    pair = jnp.concatenate([dk, dv], axis=1)
    for place in range(count):
        here = slice(place * rows, (place + 1) * rows)
        part_refs[place][...] = nt(pair[here], weight[...]).astype(BF)
    source = jnp.concatenate([ref[...] for ref in source_refs], axis=0)
    total[:, : 2 * width] = tn(source, pair)
    total[:, 2 * width : 3 * width] = self_out_grad[...]
    total[:, 3 * width : 4 * width] = cross_q_grad[...]
    small = jnp.concatenate(
        [
            sums_a[...],
            sums_b[0:4, :],
            columns_sum(dv.astype(F32)),
            jnp.zeros((128 - 13, width), F32),
        ],
        axis=0,
    )
    total[:, 4 * width :] = small.T
    write_out(total, places, keep_ref, send_ref)


def self_post_kernel(*refs, pieces, base, count, spans, begun):
    places = refs[0]
    at = 1
    dq_refs = refs[at : at + pieces]
    at += pieces
    number = len(spans)
    group_refs = []
    for group in range(number):
        group_refs.append((refs[at : at + pieces], refs[at + pieces : at + 2 * pieces]))
        at += 2 * pieces
    normed_refs = refs[at : at + number]
    token_refs = refs[at + number : at + number + count]
    at += number + count
    weight = refs[at]
    at += 1
    if begun:
        earlier = refs[at : at + count]
        small_ref = refs[at + count]
        at += count + 1
    part_refs = refs[at : at + count]
    keep_ref, send_ref = refs[at + count : at + count + 2]
    total = refs[-1]
    rows, width = token_refs[0].shape
    span = 128 * pieces
    weights = [weight[:, k * width + base : k * width + base + span] for k in range(3)]
    weight_pair = jnp.concatenate(weights[1:], axis=1)
    dq = jnp.concatenate([ref[...] for ref in dq_refs], axis=1)
    gain = shift = bias_v = 0.0
    block = 0
    for group, blocks in enumerate(spans):
        dk_refs, dv_refs = group_refs[group]
        for place in range(blocks):
            here = pl.ds(place * rows, rows)
            dk = jnp.concatenate([ref[here, :] for ref in dk_refs], axis=1)
            dv = jnp.concatenate([ref[here, :] for ref in dv_refs], axis=1)
            pair = jnp.concatenate([dk, dv], axis=1)
            grad = nt(pair, weight_pair)
            normed = normed_refs[group][here, :]
            if block == 0:
                grad = grad + nt(dq, weights[0])
                total[:, :span] = tn(normed, dq)
                total[:, span : 3 * span] = tn(normed, pair)
            else:
                total[:, span : 3 * span] += tn(normed, pair)
            if begun:
                grad = grad + earlier[block][...].astype(F32)
                unit, _ = normalize(token_refs[block][...].astype(F32))
                gain = gain + columns_sum(grad * unit)
                shift = shift + columns_sum(grad)
            bias_v = bias_v + columns_sum(dv.astype(F32))
            part_refs[block][...] = grad.astype(BF)
            block += 1
    bias_q = columns_sum(dq.astype(F32))
    if begun:
        bias_q = jnp.concatenate([small_ref[0:1, :], bias_q], axis=1)
        bias_v = jnp.concatenate([small_ref[1:2, :], bias_v], axis=1)
        small = jnp.concatenate([bias_q, bias_v, gain, shift, jnp.zeros((124, width), F32)], axis=0)
        total[:, 3 * span :] = small.T
    else:
        small_out = refs[at + count + 2]
        small_out[0:1, :] = bias_q
        small_out[1:2, :] = bias_v
        small_out[2:8, :] = jnp.zeros((6, span), F32)
    write_out(total, places, keep_ref, send_ref)


def combine_kernel(*refs, plan):
    given = sum(count for kind, count, ways in plan)
    ins, outs = refs[:given], refs[given:]
    i = o = 0
    for kind, count, ways in plan:
        mine = ins[i : i + count]
        i += count
        if kind == "copies":
            total = mine[0][0].astype(F32)
            for place in range(1, ways):
                total = total + mine[0][place].astype(F32)
            total = total.astype(BF)
            for place in range(ways):
                outs[o][place] = total
            o += 1
            continue
        if kind == "beside":
            left = 0
            for first, second in zip(mine[0::2], mine[1::2]):
                columns = first.shape[1]
                outs[o][:, left : left + columns] = (
                    first[...].astype(F32) + second[...].astype(F32)
                ).astype(BF)
                left += columns
            o += 1
            continue
        if kind == "copy":
            outs[o][...] = mine[0][...]
            o += 1
            continue
        size = mine[0].shape[0] // ways
        for way in range(ways):
            here = pl.ds(way * size, size)
            total = mine[0][here, :].astype(F32)
            for ref in mine[1:]:
                total = total + ref[here, :].astype(F32)
            outs[o][...] = total.astype(outs[o].dtype)
            o += 1


def combine(jobs, after=()):
    plan, inputs, outputs, sizes = [], [], [], []
    for job in jobs:
        if job[0] == "copies":
            plan.append(("copies", 1, job[1].shape[0]))
            inputs.append(job[1])
            made = [jax.ShapeDtypeStruct(job[1].shape, BF)]
        elif job[0] == "copy":
            plan.append(("copy", 1, 1))
            inputs.append(job[1])
            made = [jax.ShapeDtypeStruct(job[1].shape, job[1].dtype)]
        elif job[0] == "beside":
            arrays = job[1]
            plan.append(("beside", len(arrays), 1))
            inputs += arrays
            made = [shape(arrays[0].shape[0], sum(item.shape[1] for item in arrays[0::2]))]
        else:
            arrays, ways = job
            rows, columns = arrays[0].shape
            plan.append(("add", len(arrays), ways))
            inputs += arrays
            made = [shape(rows // ways, columns)] * ways
        outputs += made
        sizes.append(len(made))
    flat = run("combine", 2, functools.partial(combine_kernel, plan=plan), inputs, outputs, after)
    results, at = [], 0
    for size in sizes:
        results.append(flat[at : at + size])
        at += size
    return results


def place_kernel(*refs, plan):
    places = refs[0]
    given = sum(parts for parts, cuts in plan)
    ins, outs = refs[1 : 1 + given], refs[1 + given :]
    i = o = 0
    for parts, cuts in plan:
        for group in range(parts):
            ref = ins[i + group]
            block = ref.shape[0]
            number = places[0] ^ group if parts == 2 else 0
            at = 0
            for output, low, columns in cuts:
                first = pl.multiple_of(number * block, block) + low[0]
                outs[o + output][pl.ds(first, block), low[1] : low[1] + columns] = ref[
                    :, at : at + columns
                ].astype(F32)
                at += columns
        i += parts
        o += 1 + max(output for output, low, columns in cuts)


def place(places, parts, after=()):
    plan, inputs, outputs = [], [], []
    for arrays, shapes, cuts in parts:
        plan.append((len(arrays), cuts))
        inputs += arrays
        outputs += [shape(*dims, F32) for dims in shapes]
    return run(
        "place", 5, functools.partial(place_kernel, plan=plan), inputs, outputs, after, [places]
    )


def tokens_kernel(parts_a, parts_b, grad_first, tokens, gain, tokens_grad):
    grad = parts_a[...].astype(F32) + parts_b[...].astype(F32)
    unit, inverse = normalize(tokens[...].astype(F32))
    tokens_grad[...] = (grad_first[...] + normalize_back(grad, unit, inverse, gain[0:1, :])).astype(BF)


def vectors_kernel(small_a, small_b, gains, shifts, projs, outs, ffns):
    first = small_a[...].T
    last = small_b[...].T
    gains[0:1, :] = last[2:3]
    gains[1:2, :] = first[8:9]
    gains[2:3, :] = first[0:1]
    shifts[0:1, :] = last[3:4]
    shifts[1:2, :] = first[9:10]
    shifts[2:3, :] = first[1:2]
    projs[0:2, :] = last[0:2]
    projs[2:3, :] = first[11:12]
    projs[3:4, :] = first[12:13]
    outs[0:1, :] = first[10:11]
    outs[1:2, :] = first[3:4]
    outs[2:3, :] = first[2:3]
    ffns[...] = first[4:8]


def body(
    sizes,
    tokens,
    source,
    out_grad,
    target_ids,
    source_ids,
    source_len,
    self_qkv,
    self_out,
    cross_q,
    cross_kv,
    cross_out,
    ffn_in,
    ffn_out,
    norm_gain,
    norm_bias,
    proj_bias,
    out_bias,
    ffn_bias,
):
    width = tokens.shape[2]
    rows = tokens.shape[1]
    source_rows = source.shape[1]
    row = sizes["side"] * sizes["core"]
    core, side = "core", "side"
    chips = ("batch", "side")
    number = sizes["batch"] * sizes["side"]
    places = lax.axis_index(core).astype(jnp.int32)[None]

    def swap(value, link):
        return lax.ppermute(value, link, [(0, 1), (1, 0)])

    def exchange(half):
        rows, columns = half.shape
        return lax.all_to_all(half.reshape(number, rows // number, columns), chips, 0, 0, tiled=True)

    def regather(copies):
        own = lax.all_to_all(copies, chips, 0, 0, tiled=True)
        return own.reshape(-1, own.shape[2])

    ids = jnp.concatenate([target_ids, source_ids], axis=1)
    by_side = swap(tokens[0], side)
    by_core = swap(tokens[0], core)
    ids_core, ids_side = swap(ids, core), swap(ids, side)
    shared = (norm_gain, norm_bias, self_qkv, proj_bias)
    normed_a, k_a, v_a, e_a, queries, aux = project(
        [tokens[0], by_core], [ids, ids_core], *shared, queries=True
    )
    begun = attend(queries, aux, [(k_a, v_a, e_a)], ended=False)
    (by_side,), (ids_side,) = combine([("copy", by_side), ("copy", ids_side)], [begun])
    token_parts = [tokens[0], by_core, by_side, swap(by_side, core)]
    id_parts = [ids, ids_core, ids_side, swap(ids_side, core)]
    normed_b, k_b, v_b, e_b = project(token_parts[2:3], id_parts[2:3], *shared, after=[begun])
    normed_c, k_c, v_c, e_c, own_source = project(
        token_parts[3:], id_parts[3:], *shared, source=[source[0]], after=[k_b]
    )
    across = lax.ppermute(own_source, (side, core), [(i, row - 1 - i) for i in range(row)])
    source_parts = [own_source, swap(own_source, core), swap(own_source, side), across]
    self_keys = [(k_a, v_a, e_a), (k_b, v_b, e_b), (k_c, v_c, e_c)]
    mixed, self_aux = attend(queries, aux, self_keys[1:], begun)
    normed_parts = [normed_a, normed_b, normed_c]
    position = (lax.axis_index(side) * sizes[core] + lax.axis_index(core)).astype(jnp.int32)
    row_info = jnp.stack([source_len[0], position])
    first, normed_two, cross_queries = run(
        "after_self",
        4,
        after_self_kernel,
        [mixed, tokens[0], self_out, out_bias, norm_gain, norm_bias, cross_q, proj_bias],
        [shape(rows, width, F32), shape(rows, width), shape(rows, width)],
    )
    cross_keys = [
        run(
            "project_source",
        5,
            functools.partial(source_kernel, count=row),
            [*source_parts, *id_parts, cross_kv, proj_bias],
            [shape(row * source_rows, width)] * 2 + [shape(row * source_rows, 128)],
            [mixed],
            [row_info],
        )
    ]
    cross_mixed, cross_aux = attend(cross_queries, aux, cross_keys)

    units = ffn_in.shape[1]
    (
        output,
        grad_second,
        grad_cross_mixed,
        ffn_grads,
        sums_a,
    ) = run(
        "ffn",
        21,
        ffn_kernel,
        [
            cross_mixed,
            first,
            cross_out,
            out_bias,
            norm_gain,
            norm_bias,
            ffn_in,
            ffn_bias[None],
            ffn_out,
            out_grad[0],
        ],
        [
            shape(rows, width),
            shape(rows, width, F32),
            shape(rows, width),
            shape(width, 2 * units + width),
            shape(8, width, F32),
        ],
        scratch=[
            pltpu.VMEM((rows, units), BF),
            pltpu.VMEM((rows, units), BF),
            pltpu.VMEM((rows, width), BF),
            pltpu.VMEM((rows, width), BF),
        ],
    )
    ffn_sums = lax.psum(ffn_grads, ("batch", "side", "core"))
    def backward():
        cross_args = (cross_queries, grad_cross_mixed, cross_mixed, cross_aux, cross_keys)
        dcq, dck, dcv = attend_back(*cross_args, (0, width // 128), [ffn_grads])

        grad_first, grad_mixed, cross_q_grad, self_out_grad, sums_b = run(
            "after_cross",
            6,
            after_cross_kernel,
            [dcq, cross_q, first, normed_two, grad_second, norm_gain, mixed, self_out],
            [
                shape(rows, width, F32),
                shape(rows, width),
                shape(width, width, F32),
                shape(width, width, F32),
                shape(8, width, F32),
            ],
        )
        *source_sums, mid_keep, mid_send = run(
            "source_back",
            9,
            functools.partial(source_back_kernel, count=row),
            [
                dck,
                dcv,
                cross_kv,
                *source_parts,
                cross_q_grad,
                self_out_grad,
                sums_a,
                sums_b,
            ],
            [shape(source_rows, width)] * row
            + [shape(width // 2, 4 * width + 128)] * 2,
            scalars=[places],
            scratch=[pltpu.VMEM((width, 4 * width + 128), F32)],
        )
        mid_come = swap(mid_send, core)
        source_come = [swap(source_sums[1], core), swap(source_sums[3], core)]
        (mid_own,), (source_keep,), (source_send,) = combine(
            [
                ([mid_keep, mid_come], 1),
                ([source_sums[0], source_come[0]], 1),
                ([source_sums[2], source_come[1]], 1),
            ]
        )
        mid_all = exchange(mid_own)
        source_come = swap(source_send, side)

        self_args = (queries, grad_mixed, mixed, self_aux, self_keys)
        back = [attend_back(*self_args, (0, 1), [mid_own])]
        back.append(attend_back(*self_args, (1, 1), [back[0][0]]))
        back.append(attend_back(*self_args, (2, 1), [back[1][0]]))
        (mid_copies,), (source_grad,) = combine(
            [("copies", mid_all), ([source_keep, source_come], 1)], [back[2][0]]
        )
        mid_half = regather(mid_copies)

        def post(pieces, base, earlier, after):
            flat = [item[0] for item in pieces]
            for group in range(len(self_keys)):
                flat += [item[1 + 2 * group] for item in pieces]
                flat += [item[2 + 2 * group] for item in pieces]
            span = 128 * len(pieces)
            wide = 3 * span + (128 if earlier else 0)
            return run(
                "self_post",
                4 * len(pieces),
                functools.partial(
                    self_post_kernel,
                    pieces=len(pieces),
                    base=base,
                    count=row,
                    spans=[item.shape[0] // rows for item in normed_parts],
                    begun=bool(earlier),
                ),
                [*flat, *normed_parts, *token_parts, self_qkv, *earlier],
                [shape(rows, width)] * row
                + [shape(width // 2, wide)] * 2
                + ([] if earlier else [shape(8, span, F32)]),
                after,
                [places],
                [pltpu.VMEM((width, wide), F32)],
            )

        *parts, early_keep, early_send, early_small = post(back[:3], 0, [], [mid_copies])
        early_come = swap(early_send, core)
        back.append(attend_back(*self_args, (3, 1), [early_keep]))
        *parts, late_keep, late_send = post(back[3:], width - 128, [*parts, early_small], [])
        late_come = swap(late_send, core)
        parts_come = [swap(parts[1], core), swap(parts[3], core)]
        (late_own,), (mid_half,) = combine(
            [("beside", [early_keep, early_come, late_keep, late_come]), ("copy", mid_half)]
        )
        (own_sum,), (side_sum,) = combine(
            [([parts[0], parts_come[0]], 1), ([parts[2], parts_come[1]], 1)], [late_own]
        )
        return late_own, own_sum, side_sum, mid_half, source_grad, grad_first

    def nothing():
        return jax.tree.map(lambda item: jnp.zeros(item.shape, item.dtype), jax.eval_shape(backward))

    late_own, own_sum, side_sum, mid_half, source_grad, grad_first = lax.cond(
        source_len[0] > 0, backward, nothing
    )
    late_all = exchange(late_own)
    own_come = swap(side_sum, side)
    mid_halves = [mid_half, swap(mid_half, core)]
    ffn_in_grad, ffn_out_grad, cross_out_grad = place(
        places,
        [
            (
                [ffn_sums],
                [(width, units), (units, width), (width, width)],
                [(0, (0, 0), units)]
                + [(1, (k * width, 0), width) for k in range(units // width)]
                + [(2, (0, 0), width)],
            )
        ],
        [side_sum],
    )
    cross_kv_grad, self_out_grad, cross_q_grad, small_a = place(
        places,
        [
            (
                mid_halves,
                [(width, 2 * width), (width, width), (width, width), (width, 128)],
                [(0, (0, 0), 2 * width), (1, (0, 0), width), (2, (0, 0), width), (3, (0, 0), 128)],
            )
        ],
        [ffn_in_grad],
    )
    (tokens_grad,) = run(
        "tokens",
        4,
        tokens_kernel,
        [own_sum, own_come, grad_first, tokens[0], norm_gain],
        [shape(rows, width)],
        [small_a],
    )
    ((late_copies,),) = combine([("copies", late_all)], [tokens_grad])
    late_half = regather(late_copies)
    late_halves = [late_half, swap(late_half, core)]
    lead = width - 128
    self_qkv_grad, small_b = place(
        places,
        [
            (
                late_halves,
                [(width, 3 * width), (width, 128)],
                [(0, (0, k * width), lead) for k in range(3)]
                + [(0, (0, k * width + lead), 128) for k in range(3)]
                + [(1, (0, 0), 128)],
            )
        ],
    )
    gains, shifts, projs, outs, ffns = run(
        "vectors",
        2,
        vectors_kernel,
        [small_a, small_b],
        [
            shape(3, width, F32),
            shape(3, width, F32),
            shape(4, width, F32),
            shape(3, width, F32),
            shape(4, width, F32),
        ],
    )
    return (
        output[None],
        tokens_grad[None],
        source_grad[None],
        self_qkv_grad,
        self_out_grad,
        cross_q_grad,
        cross_kv_grad,
        cross_out_grad,
        ffn_in_grad,
        ffn_out_grad,
        gains,
        shifts,
        projs,
        outs,
        ffns.reshape(units),
    )


def solution(mesh):
    row_size = mesh.shape["seq"]
    split = jax.sharding.Mesh(
        mesh.devices.reshape(mesh.shape["batch"], row_size // 2, 2), ("batch", "side", "core")
    )
    row = P("batch", ("side", "core"), None)
    flat = P("batch", ("side", "core"))
    return jax.shard_map(
        functools.partial(body, dict(split.shape)),
        mesh=split,
        in_specs=(row, row, row, flat, flat, P("batch")) + (P(),) * 12,
        out_specs=(row, row, row) + (P(),) * 12,
        check_vma=False,
    )
```

time: 521 us -> 369 us (0.71)
  Pallas kernels: 123 us -> 251 us
  waiting for transfers between devices: 145 us -> 26.6 us
  matrix products: 83.5 us -> 0 us
  other arithmetic: 66.2 us -> 0.59 us
  local copies, waits for them, and re-layouts: 56 us -> 11.9 us
  blocking collectives: 0 us -> 27.7 us
    pallas_call x4 -> x29, Pallas kernels: 123 us -> 251 us  [the longest x21 113 us: run(): pl.pallas_call(wrapped, in_specs=[small] * len(scalars) + [whole] * len(i...]
    ppermute x35 -> x20, waiting for transfers between devices: 145 us -> 26.6 us  [the longest x19 26.6 us: swap(): return lax.ppermute(value, link, [(0, 1), (1, 0)])]
    dot_general x30 -> x0, matrix products: 83.5 us -> none  [the longest x10 29.1 us: nt(): lax.dot_general(left, right, (((1,), (1,)), ((), ())), preferred_element_...]
    all_to_all x0 -> x1, blocking collectives: none -> 27.7 us  [regather(): own = lax.all_to_all(copies, chips, 0, 0, tiled=True)]
    reduce_sum x16 -> x0, other arithmetic: 26.7 us -> none  [the longest x1 5.23 us: body(): jnp.sum(blocks[k] * all_unit[k * count:(k + 1) * count], axis=0)]
    all_to_all x0 -> x3, starting transfers between devices: none -> 19.4 us  [the longest x2 13.6 us: exchange(): lax.all_to_all(half.reshape(number, rows // number, columns), chips, 0, 0...]
    convert_element_type x18 -> x0, other arithmetic: 16.4 us -> none  [the longest x2 5.24 us: key_marks(): return hit.astype(BF)]
    ppermute x35 -> x20, starting transfers between devices: 27.1 us -> 11.7 us  [the longest x19 11 us: swap(): return lax.ppermute(value, link, [(0, 1), (1, 0)])]
  transfers between devices with their start and end apart: 36 -> 24, of which waited for: 18 -> 7; matrix products, arithmetic and copies ran while one was open for 15% -> 1% of each run, Pallas kernels for 0% -> 54%
where the time goes in v2:
time: 369 us; the launch traced here: 365 us
  Pallas kernels  251 us (68%)
  starting transfers between devices  31.2 us (8%)
  blocking collectives  27.7 us (8%)
  waiting for transfers between devices  26.6 us (7%)
  between operations  15.4 us (4%)
  local copies, waits for them, and re-layouts  11.9 us (3%)
    pallas_call x21, Pallas kernels, run(): pl.pallas_call(wrapped, in_specs=[small] * len(scalars) + [whole] * len(i...  113 us
    pallas_call x5, Pallas kernels, attend_back(): pl.pallas_call(functools.partial(backward_kernel, blocks=[largest_block(k...  91.2 us
    pallas_call x3, Pallas kernels, attend(): pl.pallas_call(functools.partial(forward_kernel, blocks=blocks, begun=beg...  47.2 us
    all_to_all x1, blocking collectives, regather(): own = lax.all_to_all(copies, chips, 0, 0, tiled=True)  27.7 us
    ppermute x19, waiting for transfers between devices, swap(): return lax.ppermute(value, link, [(0, 1), (1, 0)])  26.6 us
    all_to_all x2, starting transfers between devices, exchange(): lax.all_to_all(half.reshape(number, rows // number, columns), chips, 0, 0...  13.6 us
    ppermute x19, starting transfers between devices, swap(): return lax.ppermute(value, link, [(0, 1), (1, 0)])  11 us
  transfers between devices with their start and end apart: 24, of which 7 were waited for; matrix products, arithmetic and copies ran while one was open for 1% of the time, Pallas kernels for 54%

profile of v2, /device:TPU:0, one launch (start us, length us, event | category | flops | bytes accessed | tf_op | source)
XLA Modules:
  0.0 364.8 jit_solution(2764175261270945440)
XLA Ops:
  13.4 6.2 %project.3 = (bf16[1536,512]{1,0:T(8,128)(2,1)}, bf16[1536,512]{1,0:T(8,128)(2,1)S(1)}, bf16[1536,512]{1,0:T(8,128)(2,1)}, bf16[1536,128]{1,0:T(8,128)(2,1)S(1)}...) custom-call(bf16[768,512]{1,0:T(8,128)(2,1)} %bitcast.18, bf16[768,512]{1,0:T(8,128)(2,1)S(1)} %collective-permute-done.8.refs_1_, ...), custom_call_target="tpu_custom_call" | custom-call | flops 1800000000 | tf_op jit(solution)/shard_map/project/pallas_call | solution.py:52
  20.8 14.5 %attend.3.refs_2_.refs_6_.refs_8_ = f32[8,768,128]{2,1,0:T(8,128)} custom-call(bf16[768,512]{1,0:T(8,128)(2,1)} %get-tuple-element.255.refs_0_, bf16[768,128]{1,0:T(8,128)(2,1)} %get-tuple-element.256.refs_1_, bf16[1536,512]{1,0:T(8,128)(2,1)S(1)} %get-tuple-element.257.refs_2_, bf16[1536,512]{1,0:T(8,128)(2,1)} %get-tuple-element.258.refs_3_, ...), custom_call_target="tpu_custom_call" | custom-call | flops 3900000000 | tf_op jit(solution)/shard_map/attend/pallas_call | solution.py:154
  40.3 3.0 project.4
  43.9 3.6 project.5
  49.4 17.2 %attend.4 = (bf16[768,512]{1,0:T(8,128)(2,1)}, bf16[8,768,128]{2,1,0:T(8,128)(2,1)}) custom-call(bf16[768,512]{1,0:T(8,128)(2,1)} %get-tuple-element.255.refs_0_, bf16[768,128]{1,0:T(8,128)(2,1)} %get-tuple-element.256.refs_1_, bf16[768,512]{1,0:T(8,128)(2,1)} %get-tuple-element.262.refs_7_.refs_2_, bf16[768,512]{1,0:T(8,128)(2,1)} %get-tuple-element.263.refs_3_, ...), custom_call_target="tpu_custom_call" | custom-call | flops 3900000000 | tf_op jit(solution)/shard_map/attend/pallas_call | solution.py:154
  66.6 3.5 after_self.1
  70.1 5.0 %project_source.1 = (bf16[1536,512]{1,0:T(8,128)(2,1)}, bf16[1536,512]{1,0:T(8,128)(2,1)}, bf16[1536,128]{1,0:T(8,128)(2,1)S(1)}) custom-call(s32[2]{0:T(128)} %pad_add_fusion.refs_0_, bf16[384,512]{1,0:T(8,128)(2,1)} %get-tuple-element.270.refs_1_, bf16[384,512]{1,0:T(8,128)(2,1)} %collective-permute-done.14.refs_2_, ...), custom_call_target="tpu_custom_call" | custom-call | flops 1500000000 | tf_op jit(solution)/shard_map/project_source/pallas_call | solution.py:52
  75.1 15.6 %attend.5 = (bf16[768,512]{1,0:T(8,128)(2,1)}, bf16[8,768,128]{2,1,0:T(8,128)(2,1)}) custom-call(bf16[768,512]{1,0:T(8,128)(2,1)} %get-tuple-element.269.refs_0_, bf16[768,128]{1,0:T(8,128)(2,1)} %get-tuple-element.256.refs_1_, bf16[1536,512]{1,0:T(8,128)(2,1)} %get-tuple-element.271.refs_2_, bf16[1536,512]{1,0:T(8,128)(2,1)} %get-tuple-element.272.refs_3_, ...), custom_call_target="tpu_custom_call" | custom-call | flops 3900000000 | tf_op jit(solution)/shard_map/attend/pallas_call | solution.py:154
  90.7 21.0 %ffn.1 = (bf16[768,512]{1,0:T(8,128)(2,1)}, f32[768,512]{1,0:T(8,128)}, bf16[768,512]{1,0:T(8,128)(2,1)}, bf16[512,4608]{1,0:T(8,128)(2,1)}, f32[8,512]{1,0:T(8,128)S(1)}) custom-call(bf16[768,512]{1,0:T(8,128)(2,1)} %get-tuple-element.274.refs_0_, f32[768,512]{1,0:T(8,128)} %get-tuple-element.275.refs_1_, bf16[512,512]{1,0:T(8,128)(2,1)} %refs_2_.5, ...), custom_call_target="tpu_custom_call" | custom-call | flops 6300000256 | tf_op jit(solution)/shard_map/ffn/pallas_call | solution.py:52
  111.7 167.0 %conditional.1 = (bf16[256,1664]{1,0:T(8,128)(2,1)}, bf16[768,512]{1,0:T(8,128)(2,1)}, bf16[768,512]{1,0:T(8,128)(2,1)}, bf16[256,2176]{1,0:T(8,128)(2,1)S(1)}, ...) conditional(s32[]{:T(128)} %bitcast.9, () %tuple.18, (bf16[768,512]{1,0:T(8,128)(2,1)}, ...), branch_computations={%region_0.0_spmd, %region_1.0_spmd} | conditional | flops 36899999744 | bytes 61735792 | solution.py:911
  111.8 28.9 %attend_back.5 = (bf16[768,512]{1,0:T(8,128)(2,1)}, bf16[1536,512]{1,0:T(8,128)(2,1)}, bf16[1536,512]{1,0:T(8,128)(2,1)}) custom-call(bf16[768,512]{1,0:T(8,128)(2,1)} %get-tuple-element.85.refs_0_, bf16[768,512]{1,0:T(8,128)(2,1)} %get-tuple-element.86.refs_1_, bf16[768,512]{1,0:T(8,128)(2,1)} %get-tuple-element.87.refs_2_, ...), custom_call_target="tpu_custom_call" | custom-call | flops 8400000000 | tf_op jit(solution)/shard_map/cond/branch_1_fun/attend_back/pallas_call | solution.py:244
  140.8 6.5 %after_cross.1 = (f32[768,512]{1,0:T(8,128)S(1)}, bf16[768,512]{1,0:T(8,128)(2,1)}, f32[512,512]{1,0:T(8,128)}, f32[512,512]{1,0:T(8,128)}, f32[8,512]{1,0:T(8,128)}) custom-call(bf16[768,512]{1,0:T(8,128)(2,1)} %get-tuple-element.93.refs_0_, bf16[512,512]{1,0:T(8,128)(2,1)} %copy-done.21, f32[768,512]{1,0:T(8,128)} %get-tuple-element.95.refs_2_, ...), custom_call_target="tpu_custom_call" | custom-call | flops 1800000000 | tf_op jit(solution)/shard_map/cond/branch_1_fun/after_cross/pallas_call | solution.py:52
  147.3 8.0 %source_back.1 = (bf16[384,512]{1,0:T(8,128)(2,1)}, bf16[384,512]{1,0:T(8,128)(2,1)}, bf16[384,512]{1,0:T(8,128)(2,1)}, bf16[384,512]{1,0:T(8,128)(2,1)}, bf16[2...) custom-call(s32[1]{0:T(128)} %get-tuple-element.83.refs_0_, bf16[1536,512]{1,0:T(8,128)(2,1)} %get-tuple-element.112.refs_1_, ...), custom_call_target="tpu_custom_call" | custom-call | flops 2700000000 | tf_op jit(solution)/shard_map/cond/branch_1_fun/source_back/pallas_call | solution.py:52
  161.1 3.5 combine.6
  164.6 6.6 %all-to-all-start = ((bf16[16,16,2176]{2,1,0:T(8,128)(2,1)}), bf16[16,16,2176]{2,1,0:T(8,128)(2,1)S(1)}, u32[]{:S(2)}, u32[]{:S(2)}) async-start(bf16[16,16,2176]{2,1,0:T(8,128)(2,1)} %bitcast.24), calls=%async_computation | async-start | bytes 2228224 | tf_op jit(solution)/shard_map/cond/branch_1_fun/all_to_all | solution.py:723
  173.2 15.4 %attend_back.6 = (bf16[768,128]{1,0:T(8,128)(2,1)}, bf16[1536,128]{1,0:T(8,128)(2,1)}, bf16[1536,128]{1,0:T(8,128)(2,1)}, bf16[768,128]{1,0:T(8,128)(2,1)}, bf16...) custom-call(bf16[768,512]{1,0:T(8,128)(2,1)} %get-tuple-element.84.refs_0_, ...), custom_call_target="tpu_custom_call" | custom-call | flops 4200000000 | tf_op jit(solution)/shard_map/cond/branch_1_fun/attend_back/pallas_call | solution.py:244
  188.6 15.6 %attend_back.7 = (bf16[768,128]{1,0:T(8,128)(2,1)}, bf16[1536,128]{1,0:T(8,128)(2,1)}, bf16[1536,128]{1,0:T(8,128)(2,1)}, bf16[768,128]{1,0:T(8,128)(2,1)}, bf16...) custom-call(bf16[768,512]{1,0:T(8,128)(2,1)} %get-tuple-element.84.refs_0_, ...), custom_call_target="tpu_custom_call" | custom-call | flops 4200000000 | tf_op jit(solution)/shard_map/cond/branch_1_fun/attend_back/pallas_call | solution.py:244
  204.2 15.4 %attend_back.8 = (bf16[768,128]{1,0:T(8,128)(2,1)}, bf16[1536,128]{1,0:T(8,128)(2,1)}, bf16[1536,128]{1,0:T(8,128)(2,1)}, bf16[768,128]{1,0:T(8,128)(2,1)}, bf16...) custom-call(bf16[768,512]{1,0:T(8,128)(2,1)} %get-tuple-element.84.refs_0_, ...), custom_call_target="tpu_custom_call" | custom-call | flops 4200000000 | tf_op jit(solution)/shard_map/cond/branch_1_fun/attend_back/pallas_call | solution.py:244
  220.7 2.8 combine.7
  223.4 5.8 %all-to-all-start.1 = ((bf16[16,16,2176]{2,1,0:T(8,128)(2,1)}), bf16[16,16,2176]{2,1,0:T(8,128)(2,1)S(1)}, u32[]{:S(2)}, u32[]{:S(2)}) async-start(bf16[16,16,2176]{2,1,0:T(8,128)(2,1)} %get-tuple-element.161.refs_30_), calls=%async_computation.1 | async-start | bytes 2228224 | tf_op jit(solution)/shard_map/cond/branch_1_fun/all_to_all | solution.py:726
  229.2 11.8 %self_post.2 = (bf16[768,512]{1,0:T(8,128)(2,1)}, bf16[768,512]{1,0:T(8,128)(2,1)}, bf16[768,512]{1,0:T(8,128)(2,1)}, bf16[768,512]{1,0:T(8,128)(2,1)}, bf16[256...) custom-call(s32[1]{0:T(128)} %get-tuple-element.83.refs_0_, ...), custom_call_target="tpu_custom_call" | custom-call | flops 3600000000 | tf_op jit(solution)/shard_map/cond/branch_1_fun/self_post/pallas_call | solution.py:52
  241.1 15.8 %attend_back.9 = (bf16[768,128]{1,0:T(8,128)(2,1)}, bf16[1536,128]{1,0:T(8,128)(2,1)}, bf16[1536,128]{1,0:T(8,128)(2,1)}, bf16[768,128]{1,0:T(8,128)(2,1)}, bf16...) custom-call(bf16[768,512]{1,0:T(8,128)(2,1)} %get-tuple-element.84.refs_0_, ...), custom_call_target="tpu_custom_call" | custom-call | flops 4200000000 | tf_op jit(solution)/shard_map/cond/branch_1_fun/attend_back/pallas_call | solution.py:244
  256.9 9.3 %self_post.3 = (bf16[768,512]{1,0:T(8,128)(2,1)}, bf16[768,512]{1,0:T(8,128)(2,1)}, bf16[768,512]{1,0:T(8,128)(2,1)}, bf16[768,512]{1,0:T(8,128)(2,1)}, bf16[256...) custom-call(s32[1]{0:T(128)} %get-tuple-element.83.refs_0_, bf16[768,128]{1,0:T(8,128)(2,1)} %get-tuple-element.164.refs_1_, ...), custom_call_target="tpu_custom_call" | custom-call | flops 1200000000 | tf_op jit(solution)/shard_map/cond/branch_1_fun/self_post/pallas_call | solution.py:52
  272.3 2.9 combine.8
  275.3 3.2 combine.9
  278.8 7.0 %all-to-all-start.2 = ((bf16[16,16,1664]{2,1,0:T(8,128)(2,1)}), bf16[16,16,1664]{2,1,0:T(8,128)(2,1)}, u32[]{:S(2)}, u32[]{:S(2)}) async-start(bf16[16,16,1664]{2,1,0:T(8,128)(2,1)} %bitcast.12), calls=%async_computation.2 | async-start | bytes 1703936 | tf_op jit(solution)/shard_map/all_to_all | solution.py:723
  287.8 6.2 %place.3 = (f32[512,2048]{1,0:T(8,128)}, f32[2048,512]{1,0:T(8,128)}, f32[512,512]{1,0:T(8,128)}) custom-call(s32[1]{0:T(128)} %bitcast.10.refs_0_, bf16[512,4608]{1,0:T(8,128)(2,1)} %all-reduce.2.cloned.1.call-done.refs_1_, bf16[768,512]{1,0:T(8,128)(2,1)} %get-tuple-element.288.refs_2_), custom_call_target="tpu_custom_call" | custom-call | flops 1500000000 | tf_op jit(solution)/shard_map/place/pallas_call | solution.py:52
  294.0 3.5 place.4
  297.5 16.9 %collective-permute-done.17.refs_1_ = bf16[768,512]{1,0:T(8,128)(2,1)} collective-permute-done((bf16[768,512]{1,0:T(8,128)(2,1)}, bf16[768,512]{1,0:T(8,128)(2,1)}, u32[]{:S(2)}, u32[]{:S(2)}) %collective-permute-start.17) | collective-permute-done | bytes 786464 | tf_op jit(solution)/shard_map/ppermute | solution.py:719
  314.4 3.4 tokens.1.refs_1_
  320.0 27.7 %all_to_all.18 = bf16[16,16,1664]{2,1,0:T(8,128)(2,1)S(1)} all-to-all(bf16[16,16,1664]{2,1,0:T(8,128)(2,1)} %combine.11), channel_id=1, replica_groups=mesh['batch'=8,'side'=2,'core'=2] {'batch','side'}, dimensions={0} | all-to-all | bytes 1703936 | tf_op jit(solution)/shard_map/all_to_all | solution.py:726
  351.0 3.4 place.5
  (116 shorter events, 39.7 us)
Async XLA Ops:
  7.2 280.6 %all-reduce.2.cloned.1.call-start = ((), (), s32[]{:S(2)}) async-start(), calls=%async_computation.4 | async-start | bytes 9437184 | tf_op jit(solution)/shard_map/psum | solution.py:809
  7.2 5.6 %collective-permute-start.8 = (bf16[768,512]{1,0:T(8,128)(2,1)}, bf16[768,512]{1,0:T(8,128)(2,1)S(1)}, u32[]{:S(2)}, u32[]{:S(2)}) collective-permute-start(bf16[768,512]{1,0:T(8,128)(2,1)} %bitcast.16), channel_id=1, source_target_pairs={{0,1},{1,0},{2,3},{3,2},{4,5},{5,4},{6,7},{7,6},{8,9},{9,8},{10,11... | collective-permute-start | bytes 2359304 | tf_op jit(solution)/shard_map/ppermute | solution.py:719
  7.7 27.6 %collective-permute-start.10 = (bf16[768,512]{1,0:T(8,128)(2,1)}, bf16[768,512]{1,0:T(8,128)(2,1)S(1)}, u32[]{:S(2)}, u32[]{:S(2)}) collective-permute-start(bf16[768,512]{1,0:T(8,128)(2,1)} %bitcast.17), channel_id=1, source_target_pairs={{0,2},{2,0},{1,3},{3,1},{4,6},{6,4},{5,7},{7,5},{8,10},{10,8},{9,1... | collective-permute-start | bytes 2359304 | tf_op jit(solution)/shard_map/ppermute | solution.py:719
  11.7 1.2 collective-permute-start.9
  11.8 23.5 %collective-permute-start.11 = (s32[1,1152]{1,0:T(1,128)S(1)}, s32[1,1152]{1,0:T(1,128)S(1)}, u32[]{:S(2)}, u32[]{:S(2)}) collective-permute-start(s32[1,1152]{1,0:T(1,128)S(1)} %constant_dynamic-update-slice_fusion.refs_2_.refs_5_), channel_id=1, source_target_pairs={{0,2},{2,0},{1,3},{3,1},{4,6},{6,4},{5,7},{7,5},{8,10},{10,8},{9,1... | collective-permute-start | bytes 13832 | tf_op jit(solution)/shard_map/ppermute | solution.py:719
  38.5 4.8 %collective-permute-start.12 = (bf16[768,512]{1,0:T(8,128)(2,1)S(1)}, bf16[768,512]{1,0:T(8,128)(2,1)S(1)}, u32[]{:S(2)}, u32[]{:S(2)}) collective-permute-start(bf16[768,512]{1,0:T(8,128)(2,1)S(1)} %get-tuple-element.260.refs_0_), channel_id=1, source_target_pairs={{0,1},{1,0},{2,3},{3,2},{4,5},{5,4},{6,7},{7,6},{8,9},{9,8},{10,11... | collective-permute-start | bytes 2359304 | tf_op jit(solution)/shard_map/ppermute | solution.py:719
  39.9 3.4 collective-permute-start.13
  47.5 22.6 %collective-permute-start.16 = (bf16[384,512]{1,0:T(8,128)(2,1)}, bf16[384,512]{1,0:T(8,128)(2,1)}, u32[]{:S(2)}, u32[]{:S(2)}) collective-permute-start(bf16[384,512]{1,0:T(8,128)(2,1)} %get-tuple-element.270.refs_1_), channel_id=1, source_target_pairs={{0,3},{1,2},{2,1},{3,0},{4,7},{5,6},{6,5},{7,4},{8,11},{9,10},{10,... | collective-permute-start | bytes 1179656 | tf_op jit(solution)/shard_map/ppermute | solution.py:745
  48.2 21.9 %collective-permute-start.15 = (bf16[384,512]{1,0:T(8,128)(2,1)}, bf16[384,512]{1,0:T(8,128)(2,1)}, u32[]{:S(2)}, u32[]{:S(2)}) collective-permute-start(bf16[384,512]{1,0:T(8,128)(2,1)} %get-tuple-element.270.refs_1_), channel_id=1, source_target_pairs={{0,2},{2,0},{1,3},{3,1},{4,6},{6,4},{5,7},{7,5},{8,10},{10,8},{9,1... | collective-permute-start | bytes 1179656 | tf_op jit(solution)/shard_map/ppermute | solution.py:719
  49.3 20.8 %collective-permute-start.14 = (bf16[384,512]{1,0:T(8,128)(2,1)}, bf16[384,512]{1,0:T(8,128)(2,1)}, u32[]{:S(2)}, u32[]{:S(2)}) collective-permute-start(bf16[384,512]{1,0:T(8,128)(2,1)} %get-tuple-element.270.refs_1_), channel_id=1, source_target_pairs={{0,1},{1,0},{2,3},{3,2},{4,5},{5,4},{6,7},{7,6},{8,9},{9,8},{10,11... | collective-permute-start | bytes 1179656 | tf_op jit(solution)/shard_map/ppermute | solution.py:719
  49.4 17.2 %copy-start = (bf16[1,768,512]{2,1,0:T(8,128)(2,1)S(1)}, bf16[1,768,512]{2,1,0:T(8,128)(2,1)}, u32[]{:S(2)}) copy-start(bf16[1,768,512]{2,1,0:T(8,128)(2,1)} %param.20) | copy-start | bytes 2359300
  49.4 17.2 %copy-start.18 = (bf16[512,512]{1,0:T(8,128)(2,1)S(1)}, bf16[512,512]{1,0:T(8,128)(2,1)}, u32[]{:S(2)}) copy-start(bf16[512,512]{1,0:T(8,128)(2,1)} %refs_2_.4) | copy-start | bytes 1572868
  49.4 17.2 %copy-start.20 = (bf16[512,512]{1,0:T(8,128)(2,1)S(1)}, bf16[512,512]{1,0:T(8,128)(2,1)}, u32[]{:S(2)}) copy-start(bf16[512,512]{1,0:T(8,128)(2,1)} %refs_6_.6) | copy-start | bytes 1572868
  111.8 29.0 %copy-start.4 = (bf16[768,512]{1,0:T(8,128)(2,1)}, bf16[768,512]{1,0:T(8,128)(2,1)S(1)}, u32[]{:S(2)}) copy-start(bf16[768,512]{1,0:T(8,128)(2,1)S(1)} %get-tuple-element.156.refs_27_.refs_13_) | copy-start | bytes 2359300 | tf_op jit(solution)/shard_map/cond
  111.8 29.0 %copy-start.5 = (bf16[768,512]{1,0:T(8,128)(2,1)}, bf16[768,512]{1,0:T(8,128)(2,1)S(1)}, u32[]{:S(2)}) copy-start(bf16[768,512]{1,0:T(8,128)(2,1)S(1)} %get-tuple-element.157.refs_28_.refs_14_) | copy-start | bytes 2359300 | tf_op jit(solution)/shard_map/cond
  111.8 29.0 %copy-start.21 = (bf16[512,512]{1,0:T(8,128)(2,1)}, bf16[512,512]{1,0:T(8,128)(2,1)S(1)}, u32[]{:S(2)}) copy-start(bf16[512,512]{1,0:T(8,128)(2,1)S(1)} %get-tuple-element.94.refs_1_) | copy-start | bytes 1572868 | tf_op jit(solution)/shard_map/cond
  111.8 29.0 %copy-start.24 = (bf16[768,128]{1,0:T(8,128)(2,1)}, bf16[768,128]{1,0:T(8,128)(2,1)S(1)}, u32[]{:S(2)}) copy-start(bf16[768,128]{1,0:T(8,128)(2,1)S(1)} %get-tuple-element.108.refs_9_) | copy-start | bytes 589828 | tf_op jit(solution)/shard_map/cond
  111.8 29.0 %copy-start.19 = (bf16[512,512]{1,0:T(8,128)(2,1)S(1)}, bf16[512,512]{1,0:T(8,128)(2,1)}, u32[]{:S(2)}) copy-start(bf16[512,512]{1,0:T(8,128)(2,1)} %get-tuple-element.100.refs_7_) | copy-start | bytes 1572868 | tf_op jit(solution)/shard_map/cond
  155.3 4.1 %collective-permute-start = (bf16[256,2176]{1,0:T(8,128)(2,1)}, bf16[256,2176]{1,0:T(8,128)(2,1)S(1)}, u32[]{:S(2)}, u32[]{:S(2)}) collective-permute-start(bf16[256,2176]{1,0:T(8,128)(2,1)} %get-tuple-element.124), channel_id=1, source_target_pairs={{0,1},{1,0},{2,3},{3,2},{4,5},{5,4},{6,7},{7,6},{8,9},{9,8},{10,11... | collective-permute-start | bytes 3342344 | tf_op jit(solution)/shard_map/cond/branch_1_fun/ppermute | solution.py:719
  155.7 3.2 collective-permute-start.1
  155.8 3.6 collective-permute-start.2
  164.6 55.0 %all-to-all-start = ((bf16[16,16,2176]{2,1,0:T(8,128)(2,1)}), bf16[16,16,2176]{2,1,0:T(8,128)(2,1)S(1)}, u32[]{:S(2)}, u32[]{:S(2)}) async-start(bf16[16,16,2176]{2,1,0:T(8,128)(2,1)} %bitcast.24), calls=%async_computation | async-start | bytes 2228224 | tf_op jit(solution)/shard_map/cond/branch_1_fun/all_to_all | solution.py:723
  171.2 48.4 %collective-permute-start.3 = (bf16[384,512]{1,0:T(8,128)(2,1)}, bf16[384,512]{1,0:T(8,128)(2,1)}, u32[]{:S(2)}, u32[]{:S(2)}) collective-permute-start(bf16[384,512]{1,0:T(8,128)(2,1)} %get-tuple-element.160), channel_id=1, source_target_pairs={{0,2},{2,0},{1,3},{3,1},{4,6},{6,4},{5,7},{7,5},{8,10},{10,8},{9,1... | collective-permute-start | bytes 1179656 | tf_op jit(solution)/shard_map/cond/branch_1_fun/ppermute | solution.py:719
  223.4 47.9 %all-to-all-start.1 = ((bf16[16,16,2176]{2,1,0:T(8,128)(2,1)}), bf16[16,16,2176]{2,1,0:T(8,128)(2,1)S(1)}, u32[]{:S(2)}, u32[]{:S(2)}) async-start(bf16[16,16,2176]{2,1,0:T(8,128)(2,1)} %get-tuple-element.161.refs_30_), calls=%async_computation.1 | async-start | bytes 2228224 | tf_op jit(solution)/shard_map/cond/branch_1_fun/all_to_all | solution.py:726
  266.2 9.1 %collective-permute-start.6 = (bf16[768,512]{1,0:T(8,128)(2,1)}, bf16[768,512]{1,0:T(8,128)(2,1)}, u32[]{:S(2)}, u32[]{:S(2)}) collective-permute-start(bf16[768,512]{1,0:T(8,128)(2,1)} %get-tuple-element.180), channel_id=1, source_target_pairs={{0,1},{1,0},{2,3},{3,2},{4,5},{5,4},{6,7},{7,6},{8,9},{9,8},{10,11... | collective-permute-start | bytes 2359304 | tf_op jit(solution)/shard_map/cond/branch_1_fun/ppermute | solution.py:719
  266.2 9.1 %collective-permute-start.7 = (bf16[768,512]{1,0:T(8,128)(2,1)}, bf16[768,512]{1,0:T(8,128)(2,1)}, u32[]{:S(2)}, u32[]{:S(2)}) collective-permute-start(bf16[768,512]{1,0:T(8,128)(2,1)} %get-tuple-element.182), channel_id=1, source_target_pairs={{0,1},{1,0},{2,3},{3,2},{4,5},{5,4},{6,7},{7,6},{8,9},{9,8},{10,11... | collective-permute-start | bytes 2359304 | tf_op jit(solution)/shard_map/cond/branch_1_fun/ppermute | solution.py:719
  266.7 4.6 %collective-permute-start.4 = (bf16[256,1152]{1,0:T(8,128)(2,1)}, bf16[256,1152]{1,0:T(8,128)(2,1)}, u32[]{:S(2)}, u32[]{:S(2)}) collective-permute-start(bf16[256,1152]{1,0:T(8,128)(2,1)} %get-tuple-element.163), channel_id=1, source_target_pairs={{0,1},{1,0},{2,3},{3,2},{4,5},{5,4},{6,7},{7,6},{8,9},{9,8},{10,11... | collective-permute-start | bytes 1769480 | tf_op jit(solution)/shard_map/cond/branch_1_fun/ppermute | solution.py:719
  266.8 2.7 collective-permute-start.5
  278.8 39.0 %all-to-all-start.2 = ((bf16[16,16,1664]{2,1,0:T(8,128)(2,1)}), bf16[16,16,1664]{2,1,0:T(8,128)(2,1)}, u32[]{:S(2)}, u32[]{:S(2)}) async-start(bf16[16,16,1664]{2,1,0:T(8,128)(2,1)} %bitcast.12), calls=%async_computation.2 | async-start | bytes 1703936 | tf_op jit(solution)/shard_map/all_to_all | solution.py:723
  285.8 8.2 %collective-permute-start.18 = (bf16[256,2176]{1,0:T(8,128)(2,1)S(1)}, bf16[256,2176]{1,0:T(8,128)(2,1)}, u32[]{:S(2)}, u32[]{:S(2)}) collective-permute-start(bf16[256,2176]{1,0:T(8,128)(2,1)S(1)} %get-tuple-element.290.refs_1_), channel_id=1, source_target_pairs={{0,1},{1,0},{2,3},{3,2},{4,5},{5,4},{6,7},{7,6},{8,9},{9,8},{10,11... | collective-permute-start | bytes 3342344 | tf_op jit(solution)/shard_map/ppermute | solution.py:719
  285.9 28.5 %collective-permute-start.17 = (bf16[768,512]{1,0:T(8,128)(2,1)}, bf16[768,512]{1,0:T(8,128)(2,1)}, u32[]{:S(2)}, u32[]{:S(2)}) collective-permute-start(bf16[768,512]{1,0:T(8,128)(2,1)} %get-tuple-element.288.refs_2_), channel_id=1, source_target_pairs={{0,2},{2,0},{1,3},{3,1},{4,6},{6,4},{5,7},{7,5},{8,10},{10,8},{9,1... | collective-permute-start | bytes 2359304 | tf_op jit(solution)/shard_map/ppermute | solution.py:719
  347.7 2.4 collective-permute-start.19
  (24 other events, 122.4 us)
Sparse Core Ops, SparseCore 0:
  111.9 167.7 all-reduce.1

commit v3 on v2

--- a/solution.py
+++ b/solution.py
@@ -149,7 +149,7 @@
     if begun is not None:
         specs.append(by_head)
         flat.append(begun)
-    blocks = [largest_block(k.shape[0], 1024) for k, v, e in keys]
+    blocks = [512 if k.shape[0] % 512 == 0 else largest_block(k.shape[0], 1024) for k, v, e in keys]
     totals = jax.ShapeDtypeStruct((width // 64, rows, 128), F32)
     return pl.pallas_call(
         functools.partial(forward_kernel, blocks=blocks, begun=begun is not None, ended=ended),
@@ -244,7 +244,7 @@
     return pl.pallas_call(
         functools.partial(
             backward_kernel,
-            blocks=[largest_block(k.shape[0], 512) for k, v, e in keys],
+            blocks=[largest_block(k.shape[0], 768) for k, v, e in keys],
             fences=len(after),
         ),
         grid=(number,),
@@ -298,9 +298,9 @@
     rest = refs[2 * count :]
     if source:
         source_ref, *rest = rest
-        rest[8][...] = source_ref[...]
+        rest[9][...] = source_ref[...]
     gain_ref, shift_ref, weight_ref, bias_ref = rest[:4]
-    n_ref, k_ref, v_ref, e_ref = rest[4:8]
+    n_ref, k_ref, v_ref, e_ref, u_ref = rest[4:9]
     rows = token_refs[0].shape[0]
     width = token_refs[0].shape[1]
     for place in range(count):
@@ -308,12 +308,13 @@
         normed = (unit * gain_ref[0:1, :] + shift_ref[0:1, :]).astype(BF)
         here = pl.ds(place * rows, rows)
         n_ref[here, :] = normed
+        u_ref[here, :] = unit.astype(BF)
         k_ref[here, :] = nn(normed, weight_ref[:, width : 2 * width]).astype(BF)
         v_ref[here, :] = (nn(normed, weight_ref[:, 2 * width :]) + bias_ref[1:2, :]).astype(BF)
         ids = id_refs[place][:, :rows]
         e_ref[here, :] = key_marks(ids)
         if queries and place == 0:
-            q_ref, aux_ref = rest[8:10]
+            q_ref, aux_ref = rest[9:11]
             joined = nn(normed, weight_ref[:, :width]) + bias_ref[0:1, :]
             q_ref[...] = (joined * (SCALE * LOG2E)).astype(BF)
             aux_ref[...] = query_marks(ids)
@@ -323,7 +324,8 @@
     count = len(tokens)
     rows, width = tokens[0].shape
     inputs = [*tokens, *ids, *source, norm_gain, norm_bias, self_qkv, proj_bias]
-    outputs = [shape(count * rows, width)] * 3 + [shape(count * rows, 128)]
+    outputs = [shape(count * rows, width)] * 3
+    outputs += [shape(count * rows, 128), shape(count * rows, width)]
     if queries:
         outputs += [shape(rows, width), shape(rows, 128)]
     outputs += [shape(*item.shape) for item in source]
@@ -383,7 +385,7 @@
     second_ref,
 ):
     rows = mixed.shape[0]
-    tile = rows // 3
+    tile = rows
     width = mixed.shape[1]
     sums = [0.0] * 4
     bias_sum = 0.0
@@ -502,19 +504,20 @@
         group_refs.append((refs[at : at + pieces], refs[at + pieces : at + 2 * pieces]))
         at += 2 * pieces
     normed_refs = refs[at : at + number]
-    token_refs = refs[at + number : at + number + count]
-    at += number + count
+    at += number
     weight = refs[at]
     at += 1
     if begun:
+        unit_refs = refs[at : at + number]
+        at += number
         earlier = refs[at : at + count]
         small_ref = refs[at + count]
         at += count + 1
     part_refs = refs[at : at + count]
     keep_ref, send_ref = refs[at + count : at + count + 2]
     total = refs[-1]
-    rows, width = token_refs[0].shape
-    span = 128 * pieces
+    rows, width = part_refs[0].shape
+    span = sum(ref.shape[1] for ref in dq_refs)
     weights = [weight[:, k * width + base : k * width + base + span] for k in range(3)]
     weight_pair = jnp.concatenate(weights[1:], axis=1)
     dq = jnp.concatenate([ref[...] for ref in dq_refs], axis=1)
@@ -537,8 +540,7 @@
                 total[:, span : 3 * span] += tn(normed, pair)
             if begun:
                 grad = grad + earlier[block][...].astype(F32)
-                unit, _ = normalize(token_refs[block][...].astype(F32))
-                gain = gain + columns_sum(grad * unit)
+                gain = gain + columns_sum(grad * unit_refs[group][here, :].astype(F32))
                 shift = shift + columns_sum(grad)
             bias_v = bias_v + columns_sum(dv.astype(F32))
             part_refs[block][...] = grad.astype(BF)
@@ -587,9 +589,10 @@
             outs[o][...] = mine[0][...]
             o += 1
             continue
-        size = mine[0].shape[0] // ways
-        for way in range(ways):
-            here = pl.ds(way * size, size)
+        low = 0
+        for size in ways:
+            here = pl.ds(low, size)
+            low += size
             total = mine[0][here, :].astype(F32)
             for ref in mine[1:]:
                 total = total + ref[here, :].astype(F32)
@@ -616,9 +619,10 @@
         else:
             arrays, ways = job
             rows, columns = arrays[0].shape
-            plan.append(("add", len(arrays), ways))
+            cuts = ways if isinstance(ways, list) else [rows // ways] * ways
+            plan.append(("add", len(arrays), cuts))
             inputs += arrays
-            made = [shape(rows // ways, columns)] * ways
+            made = [shape(size, columns) for size in cuts]
         outputs += made
         sizes.append(len(made))
     flat = run("combine", 2, functools.partial(combine_kernel, plan=plan), inputs, outputs, after)
@@ -661,13 +665,27 @@
     )
 
 
-def tokens_kernel(parts_a, parts_b, grad_first, tokens, gain, tokens_grad):
-    grad = parts_a[...].astype(F32) + parts_b[...].astype(F32)
+def tokens_kernel(parts, come_a, come_b, grad_first, tokens, gain, tokens_grad):
+    come = jnp.concatenate([come_a[...], come_b[...]], axis=0)
+    grad = parts[...].astype(F32) + come.astype(F32)
     unit, inverse = normalize(tokens[...].astype(F32))
     tokens_grad[...] = (grad_first[...] + normalize_back(grad, unit, inverse, gain[0:1, :])).astype(BF)
 
 
-def vectors_kernel(small_a, small_b, gains, shifts, projs, outs, ffns):
+def biases_kernel(small, ffns):
+    ffns[...] = small[...].T[4:8]
+
+
+def finish_kernel(places, half_a, half_b, small_a, qkv, gains, shifts, projs, outs, small_b):
+    half, width = half_a.shape[0], small_a.shape[0]
+    lead = width - 128
+    for group, ref in enumerate([half_a, half_b]):
+        rows = pl.ds(pl.multiple_of((places[0] ^ group) * half, half), half)
+        for k in range(3):
+            qkv[rows, k * width : k * width + lead] = ref[:, k * lead : (k + 1) * lead].astype(F32)
+            at = 3 * lead + 128 * k
+            qkv[rows, k * width + lead : (k + 1) * width] = ref[:, at : at + 128].astype(F32)
+        small_b[rows, :] = ref[:, 3 * width :].astype(F32)
     first = small_a[...].T
     last = small_b[...].T
     gains[0:1, :] = last[2:3]
@@ -682,7 +700,6 @@
     outs[0:1, :] = first[10:11]
     outs[1:2, :] = first[3:4]
     outs[2:3, :] = first[2:3]
-    ffns[...] = first[4:8]
 
 
 def body(
@@ -731,15 +748,15 @@
     by_core = swap(tokens[0], core)
     ids_core, ids_side = swap(ids, core), swap(ids, side)
     shared = (norm_gain, norm_bias, self_qkv, proj_bias)
-    normed_a, k_a, v_a, e_a, queries, aux = project(
+    normed_a, k_a, v_a, e_a, unit_a, queries, aux = project(
         [tokens[0], by_core], [ids, ids_core], *shared, queries=True
     )
     begun = attend(queries, aux, [(k_a, v_a, e_a)], ended=False)
     (by_side,), (ids_side,) = combine([("copy", by_side), ("copy", ids_side)], [begun])
     token_parts = [tokens[0], by_core, by_side, swap(by_side, core)]
     id_parts = [ids, ids_core, ids_side, swap(ids_side, core)]
-    normed_b, k_b, v_b, e_b = project(token_parts[2:3], id_parts[2:3], *shared, after=[begun])
-    normed_c, k_c, v_c, e_c, own_source = project(
+    normed_b, k_b, v_b, e_b, unit_b = project(token_parts[2:3], id_parts[2:3], *shared, after=[begun])
+    normed_c, k_c, v_c, e_c, unit_c, own_source = project(
         token_parts[3:], id_parts[3:], *shared, source=[source[0]], after=[k_b]
     )
     across = lax.ppermute(own_source, (side, core), [(i, row - 1 - i) for i in range(row)])
@@ -747,6 +764,7 @@
     self_keys = [(k_a, v_a, e_a), (k_b, v_b, e_b), (k_c, v_c, e_c)]
     mixed, self_aux = attend(queries, aux, self_keys[1:], begun)
     normed_parts = [normed_a, normed_b, normed_c]
+    unit_parts = [unit_a, unit_b, unit_c]
     position = (lax.axis_index(side) * sizes[core] + lax.axis_index(core)).astype(jnp.int32)
     row_info = jnp.stack([source_len[0], position])
     first, normed_two, cross_queries = run(
@@ -845,35 +863,30 @@
         )
         mid_come = swap(mid_send, core)
         source_come = [swap(source_sums[1], core), swap(source_sums[3], core)]
+        self_args = (queries, grad_mixed, mixed, self_aux, self_keys)
+        back = [attend_back(*self_args, (0, 1), [mid_keep])]
         (mid_own,), (source_keep,), (source_send,) = combine(
             [
                 ([mid_keep, mid_come], 1),
                 ([source_sums[0], source_come[0]], 1),
                 ([source_sums[2], source_come[1]], 1),
-            ]
+            ],
+            [back[0][0]],
         )
         mid_all = exchange(mid_own)
         source_come = swap(source_send, side)
-
-        self_args = (queries, grad_mixed, mixed, self_aux, self_keys)
-        back = [attend_back(*self_args, (0, 1), [mid_own])]
-        back.append(attend_back(*self_args, (1, 1), [back[0][0]]))
-        back.append(attend_back(*self_args, (2, 1), [back[1][0]]))
-        (mid_copies,), (source_grad,) = combine(
-            [("copies", mid_all), ([source_keep, source_come], 1)], [back[2][0]]
-        )
-        mid_half = regather(mid_copies)
+        back.append(attend_back(*self_args, (1, 2), [mid_own]))
 
         def post(pieces, base, earlier, after):
             flat = [item[0] for item in pieces]
+            span = sum(item[0].shape[1] for item in pieces)
             for group in range(len(self_keys)):
                 flat += [item[1 + 2 * group] for item in pieces]
                 flat += [item[2 + 2 * group] for item in pieces]
-            span = 128 * len(pieces)
             wide = 3 * span + (128 if earlier else 0)
             return run(
                 "self_post",
-                4 * len(pieces),
+                span // 32,
                 functools.partial(
                     self_post_kernel,
                     pieces=len(pieces),
@@ -882,7 +895,7 @@
                     spans=[item.shape[0] // rows for item in normed_parts],
                     begun=bool(earlier),
                 ),
-                [*flat, *normed_parts, *token_parts, self_qkv, *earlier],
+                [*flat, *normed_parts, self_qkv, *earlier],
                 [shape(rows, width)] * row
                 + [shape(width // 2, wide)] * 2
                 + ([] if earlier else [shape(8, span, F32)]),
@@ -891,29 +904,46 @@
                 [pltpu.VMEM((width, wide), F32)],
             )
 
-        *parts, early_keep, early_send, early_small = post(back[:3], 0, [], [mid_copies])
+        (mid_copies,), (source_grad,) = combine(
+            [("copies", mid_all), ([source_keep, source_come], 1)], [back[1][0]]
+        )
+        mid_half = regather(mid_copies)
+        *parts, early_keep, early_send, early_small = post(back, 0, [], [mid_copies])
         early_come = swap(early_send, core)
-        back.append(attend_back(*self_args, (3, 1), [early_keep]))
-        *parts, late_keep, late_send = post(back[3:], width - 128, [*parts, early_small], [])
+        last = [attend_back(*self_args, (3, 1), [early_small])]
+        *parts, late_keep, late_send = post(
+            last, width - 128, [*unit_parts, *parts, early_small], []
+        )
         late_come = swap(late_send, core)
-        parts_come = [swap(parts[1], core), swap(parts[3], core)]
-        (late_own,), (mid_half,) = combine(
-            [("beside", [early_keep, early_come, late_keep, late_come]), ("copy", mid_half)]
-        )
-        (own_sum,), (side_sum,) = combine(
-            [([parts[0], parts_come[0]], 1), ([parts[2], parts_come[1]], 1)], [late_own]
-        )
-        return late_own, own_sum, side_sum, mid_half, source_grad, grad_first
+        ((late_own,),) = combine([("beside", [early_keep, early_come, late_keep, late_come])])
+        return late_own, mid_half, source_grad, grad_first, *parts
 
     def nothing():
         return jax.tree.map(lambda item: jnp.zeros(item.shape, item.dtype), jax.eval_shape(backward))
 
-    late_own, own_sum, side_sum, mid_half, source_grad, grad_first = lax.cond(
+    late_own, mid_half, source_grad, grad_first, *parts = lax.cond(
         source_len[0] > 0, backward, nothing
     )
     late_all = exchange(late_own)
-    own_come = swap(side_sum, side)
+    parts_come = [swap(parts[1], core), swap(parts[3], core)]
     mid_halves = [mid_half, swap(mid_half, core)]
+    cross_kv_grad, self_out_grad, cross_q_grad, small_a = place(
+        places,
+        [
+            (
+                mid_halves,
+                [(width, 2 * width), (width, width), (width, width), (width, 128)],
+                [(0, (0, 0), 2 * width), (1, (0, 0), width), (2, (0, 0), width), (3, (0, 0), 128)],
+            )
+        ],
+        [late_own],
+    )
+    cuts = [rows // 4, rows - rows // 4]
+    (own_sum,), side_sums = combine(
+        [([parts[0], parts_come[0]], 1), ([parts[2], parts_come[1]], cuts)], [small_a]
+    )
+    own_come = [swap(item, side) for item in side_sums]
+    (ffn_biases,) = run("biases", 1, biases_kernel, [small_a], [shape(4, width, F32)], [own_sum])
     ffn_in_grad, ffn_out_grad, cross_out_grad = place(
         places,
         [
@@ -925,55 +955,33 @@
                 + [(2, (0, 0), width)],
             )
         ],
-        [side_sum],
-    )
-    cross_kv_grad, self_out_grad, cross_q_grad, small_a = place(
-        places,
-        [
-            (
-                mid_halves,
-                [(width, 2 * width), (width, width), (width, width), (width, 128)],
-                [(0, (0, 0), 2 * width), (1, (0, 0), width), (2, (0, 0), width), (3, (0, 0), 128)],
-            )
-        ],
-        [ffn_in_grad],
-    )
+        [ffn_biases],
+    )
+    ((late_copies,),) = combine([("copies", late_all)], [ffn_in_grad, own_come[0]])
+    late_half = regather(late_copies)
     (tokens_grad,) = run(
         "tokens",
+        20,
+        tokens_kernel,
+        [own_sum, *own_come, grad_first, tokens[0], norm_gain],
+        [shape(rows, width)],
+        [late_copies],
+    )
+    self_qkv_grad, gains, shifts, projs, outs = run(
+        "finish",
         4,
-        tokens_kernel,
-        [own_sum, own_come, grad_first, tokens[0], norm_gain],
-        [shape(rows, width)],
-        [small_a],
-    )
-    ((late_copies,),) = combine([("copies", late_all)], [tokens_grad])
-    late_half = regather(late_copies)
-    late_halves = [late_half, swap(late_half, core)]
-    lead = width - 128
-    self_qkv_grad, small_b = place(
-        places,
+        finish_kernel,
+        [late_half, swap(late_half, core), small_a],
         [
-            (
-                late_halves,
-                [(width, 3 * width), (width, 128)],
-                [(0, (0, k * width), lead) for k in range(3)]
-                + [(0, (0, k * width + lead), 128) for k in range(3)]
-                + [(1, (0, 0), 128)],
-            )
-        ],
-    )
-    gains, shifts, projs, outs, ffns = run(
-        "vectors",
-        2,
-        vectors_kernel,
-        [small_a, small_b],
-        [
+            shape(width, 3 * width, F32),
             shape(3, width, F32),
             shape(3, width, F32),
             shape(4, width, F32),
             shape(3, width, F32),
-            shape(4, width, F32),
         ],
+        [tokens_grad],
+        [places],
+        [pltpu.VMEM((width, 128), F32)],
     )
     return (
         output[None],
@@ -990,7 +998,7 @@
         shifts,
         projs,
         outs,
-        ffns.reshape(units),
+        ffn_biases.reshape(units),
     )
 
 

time: 369 us -> 342 us (0.927)
  blocking collectives: 27.7 us -> 0 us
  Pallas kernels: 251 us -> 241 us
  starting transfers between devices: 31.2 us -> 39 us
    all_to_all x1 -> x0, blocking collectives: 27.7 us -> none  [regather(): own = lax.all_to_all(copies, chips, 0, 0, tiled=True)]
    all_to_all x1 -> x2, waiting for transfers between devices: 0.01 us -> 19.1 us  [regather(): own = lax.all_to_all(copies, chips, 0, 0, tiled=True)]
    ppermute x19 -> x20, waiting for transfers between devices: 26.6 us -> 10.5 us  [swap(): return lax.ppermute(value, link, [(0, 1), (1, 0)])]
    all_to_all x1 -> x2, starting transfers between devices: 5.8 us -> 11.9 us  [regather(): own = lax.all_to_all(copies, chips, 0, 0, tiled=True)]
    pallas_call x5 -> x4, Pallas kernels: 91.2 us -> 85.2 us  [attend_back(): pl.pallas_call(functools.partial(backward_kernel, blocks=[largest_block(k...]
    ppermute x19 -> x20, starting transfers between devices: 11 us -> 13 us  [swap(): return lax.ppermute(value, link, [(0, 1), (1, 0)])]
    unnamed x34 -> x40, local copies, waits for them, and re-layouts: 6.71 us -> 8.53 us
  transfers between devices with their start and end apart: 24 -> 26, of which waited for: 7 -> 6; matrix products, arithmetic and copies ran while one was open for 1% -> 1% of each run, Pallas kernels for 54% -> 56%
where the time goes in v3:
time: 342 us; the launch traced here: 338 us
  Pallas kernels  241 us (70%)
  starting transfers between devices  39 us (11%)
  waiting for transfers between devices  29.6 us (9%)
  between operations  15.1 us (4%)
  local copies, waits for them, and re-layouts  12.3 us (4%)
    pallas_call x21, Pallas kernels, run(): pl.pallas_call(wrapped, in_specs=[small] * len(scalars) + [whole] * len(i...  109 us
    pallas_call x4, Pallas kernels, attend_back(): pl.pallas_call(functools.partial(backward_kernel, blocks=[largest_block(k...  85.2 us
    pallas_call x3, Pallas kernels, attend(): pl.pallas_call(functools.partial(forward_kernel, blocks=blocks, begun=beg...  47 us
    all_to_all x2, waiting for transfers between devices, regather(): own = lax.all_to_all(copies, chips, 0, 0, tiled=True)  19.1 us
    all_to_all x2, starting transfers between devices, exchange(): lax.all_to_all(half.reshape(number, rows // number, columns), chips, 0, 0...  13.3 us
    ppermute x20, starting transfers between devices, swap(): return lax.ppermute(value, link, [(0, 1), (1, 0)])  13 us
    all_to_all x2, starting transfers between devices, regather(): own = lax.all_to_all(copies, chips, 0, 0, tiled=True)  11.9 us
    ppermute x20, waiting for transfers between devices, swap(): return lax.ppermute(value, link, [(0, 1), (1, 0)])  10.5 us
  transfers between devices with their start and end apart: 26, of which 6 were waited for; matrix products, arithmetic and copies ran while one was open for 1% of the time, Pallas kernels for 56%

profile of v3, /device:TPU:0, one launch (start us, length us, event | category | flops | bytes accessed | tf_op | source)
XLA Modules:
  0.0 338.4 jit_solution(2202238700300894630)
XLA Ops:
  7.7 2.6 collective-permute-start.8
  14.3 6.5 %project.3 = (bf16[1536,512]{1,0:T(8,128)(2,1)S(1)}, bf16[1536,512]{1,0:T(8,128)(2,1)}, bf16[1536,512]{1,0:T(8,128)(2,1)}, bf16[1536,128]{1,0:T(8,128)(2,1)S(1)}...) custom-call(bf16[768,512]{1,0:T(8,128)(2,1)} %bitcast.24, ...), custom_call_target="tpu_custom_call" | custom-call | flops 1800000000 | tf_op jit(solution)/shard_map/project/pallas_call | solution.py:52
  21.8 14.1 %attend.3.refs_2_.refs_6_.refs_8_ = f32[8,768,128]{2,1,0:T(8,128)} custom-call(bf16[768,512]{1,0:T(8,128)(2,1)S(1)} %get-tuple-element.247.refs_0_, bf16[768,128]{1,0:T(8,128)(2,1)} %get-tuple-element.248.refs_1_, bf16[1536,512]{1,0:T(8,128)(2,1)} %get-tuple-element.249.refs_2_, bf16[1536,512]{1,0:T(8,128)(2,1)} %get-tuple-element.250.refs_3_, ...), custom_call_target="tpu_custom_call" | custom-call | flops 3900000000 | tf_op jit(solution)/shard_map/attend/pallas_call | solution.py:154
  40.3 3.7 %project.4 = (bf16[768,512]{1,0:T(8,128)(2,1)}, bf16[768,512]{1,0:T(8,128)(2,1)}, bf16[768,512]{1,0:T(8,128)(2,1)}, bf16[768,128]{1,0:T(8,128)(2,1)}, bf16[768,512]{1,0:T(8,128)(2,1)}) custom-call(bf16[768,512]{1,0:T(8,128)(2,1)} %get-tuple-element.252.refs_0_, s32[1,1152]{1,0:T(1,128)} %get-tuple-element.253.refs_1_.refs_7_, f32[3,512]{1,0:T(4,128)S(1)} %copy-done.26, ...), custom_call_target="tpu_custom_call" | custom-call | flops 1800000000 | tf_op jit(solution)/shard_map/project/pallas_call | solution.py:52
  44.7 3.9 %project.5 = (bf16[768,512]{1,0:T(8,128)(2,1)}, bf16[768,512]{1,0:T(8,128)(2,1)}, bf16[768,512]{1,0:T(8,128)(2,1)}, bf16[768,128]{1,0:T(8,128)(2,1)}, bf16[768,5...) custom-call(bf16[768,512]{1,0:T(8,128)(2,1)} %collective-permute-done.10.refs_0_, s32[1,1152]{1,0:T(1,128)} %copy-done.28, ...), custom_call_target="tpu_custom_call" | custom-call | flops 1800000000 | tf_op jit(solution)/shard_map/project/pallas_call | solution.py:52
  50.4 17.3 %attend.4 = (bf16[768,512]{1,0:T(8,128)(2,1)}, bf16[8,768,128]{2,1,0:T(8,128)(2,1)}) custom-call(bf16[768,512]{1,0:T(8,128)(2,1)} %copy-done.31, bf16[768,128]{1,0:T(8,128)(2,1)} %get-tuple-element.248.refs_1_, bf16[768,512]{1,0:T(8,128)(2,1)} %get-tuple-element.254.refs_7_.refs_2_, bf16[768,512]{1,0:T(8,128)(2,1)} %get-tuple-element.255.refs_3_, ...), custom_call_target="tpu_custom_call" | custom-call | flops 3900000000 | tf_op jit(solution)/shard_map/attend/pallas_call | solution.py:154
  67.7 3.9 %after_self.1 = (f32[768,512]{1,0:T(8,128)}, bf16[768,512]{1,0:T(8,128)(2,1)}, bf16[768,512]{1,0:T(8,128)(2,1)}) custom-call(bf16[768,512]{1,0:T(8,128)(2,1)} %get-tuple-element.260.refs_0_.refs_11_, bf16[768,512]{1,0:T(8,128)(2,1)} %bitcast.25, bf16[512,512]{1,0:T(8,128)(2,1)S(1)} %copy-done.24, f32[3,512]{1,0:T(4,128)} %refs_3_.7, ...), custom_call_target="tpu_custom_call" | custom-call | flops 1200000000 | tf_op jit(solution)/shard_map/after_self/pallas_call | solution.py:52
  71.6 4.9 %project_source.1 = (bf16[1536,512]{1,0:T(8,128)(2,1)}, bf16[1536,512]{1,0:T(8,128)(2,1)}, bf16[1536,128]{1,0:T(8,128)(2,1)S(1)}) custom-call(s32[2]{0:T(128)} %pad_add_fusion.refs_0_, bf16[384,512]{1,0:T(8,128)(2,1)S(1)} %get-tuple-element.262.refs_1_, bf16[384,512]{1,0:T(8,128)(2,1)} %collective-permute-done.12.refs_2_, ...), custom_call_target="tpu_custom_call" | custom-call | flops 1500000000 | tf_op jit(solution)/shard_map/project_source/pallas_call | solution.py:52
  76.5 15.7 %attend.5 = (bf16[768,512]{1,0:T(8,128)(2,1)}, bf16[8,768,128]{2,1,0:T(8,128)(2,1)}) custom-call(bf16[768,512]{1,0:T(8,128)(2,1)} %get-tuple-element.261.refs_0_, bf16[768,128]{1,0:T(8,128)(2,1)} %get-tuple-element.248.refs_1_, bf16[1536,512]{1,0:T(8,128)(2,1)} %get-tuple-element.263.refs_2_, bf16[1536,512]{1,0:T(8,128)(2,1)} %get-tuple-element.264.refs_3_, ...), custom_call_target="tpu_custom_call" | custom-call | flops 3900000000 | tf_op jit(solution)/shard_map/attend/pallas_call | solution.py:154
  92.1 19.2 %ffn.1 = (bf16[768,512]{1,0:T(8,128)(2,1)}, f32[768,512]{1,0:T(8,128)}, bf16[768,512]{1,0:T(8,128)(2,1)}, bf16[512,4608]{1,0:T(8,128)(2,1)}, f32[8,512]{1,0:T(8,128)}) custom-call(bf16[768,512]{1,0:T(8,128)(2,1)} %get-tuple-element.266.refs_0_, f32[768,512]{1,0:T(8,128)} %get-tuple-element.267.refs_1_, bf16[512,512]{1,0:T(8,128)(2,1)} %refs_2_.5, ...), custom_call_target="tpu_custom_call" | custom-call | flops 6300000256 | tf_op jit(solution)/shard_map/ffn/pallas_call | solution.py:52
  111.3 146.9 %conditional.1 = (bf16[256,1664]{1,0:T(8,128)(2,1)}, bf16[256,2176]{1,0:T(8,128)(2,1)}, f32[768,512]{1,0:T(8,128)}, bf16[768,512]{1,0:T(8,128)(2,1)S(1)}, bf16[7...) conditional(s32[]{:T(128)} %bitcast.9, () %tuple.18, ...), branch_computations={%region_0.0_spmd, %region_1.0_spmd} | conditional | flops 36300005376 | bytes 68879120 | solution.py:924
  111.4 28.4 %attend_back.4 = (bf16[768,512]{1,0:T(8,128)(2,1)}, bf16[1536,512]{1,0:T(8,128)(2,1)}, bf16[1536,512]{1,0:T(8,128)(2,1)}) custom-call(bf16[768,512]{1,0:T(8,128)(2,1)} %get-tuple-element.83.refs_0_, bf16[768,512]{1,0:T(8,128)(2,1)} %get-tuple-element.84.refs_1_, bf16[768,512]{1,0:T(8,128)(2,1)} %get-tuple-element.85.refs_2_, ...), custom_call_target="tpu_custom_call" | custom-call | flops 8400000000 | tf_op jit(solution)/shard_map/cond/branch_1_fun/attend_back/pallas_call | solution.py:244
  139.8 6.6 %after_cross.1 = (f32[768,512]{1,0:T(8,128)}, bf16[768,512]{1,0:T(8,128)(2,1)}, f32[512,512]{1,0:T(8,128)}, f32[512,512]{1,0:T(8,128)}, f32[8,512]{1,0:T(8,128)}) custom-call(bf16[768,512]{1,0:T(8,128)(2,1)} %get-tuple-element.91.refs_0_, bf16[512,512]{1,0:T(8,128)(2,1)} %get-tuple-element.92.refs_1_, f32[768,512]{1,0:T(8,128)} %get-tuple-element.93.refs_2_, ...), custom_call_target="tpu_custom_call" | custom-call | flops 1800000000 | tf_op jit(solution)/shard_map/cond/branch_1_fun/after_cross/pallas_call | solution.py:52
  146.4 8.0 %source_back.1 = (bf16[384,512]{1,0:T(8,128)(2,1)}, bf16[384,512]{1,0:T(8,128)(2,1)}, bf16[384,512]{1,0:T(8,128)(2,1)}, bf16[384,512]{1,0:T(8,128)(2,1)}, bf16[2...) custom-call(s32[1]{0:T(128)} %get-tuple-element.81.refs_0_, bf16[1536,512]{1,0:T(8,128)(2,1)} %get-tuple-element.110.refs_1_, ...), custom_call_target="tpu_custom_call" | custom-call | flops 2700000000 | tf_op jit(solution)/shard_map/cond/branch_1_fun/source_back/pallas_call | solution.py:52
  155.4 14.9 %attend_back.5 = (bf16[768,128]{1,0:T(8,128)(2,1)}, bf16[1536,128]{1,0:T(8,128)(2,1)}, bf16[1536,128]{1,0:T(8,128)(2,1)}, bf16[768,128]{1,0:T(8,128)(2,1)}, bf16...) custom-call(bf16[768,512]{1,0:T(8,128)(2,1)} %get-tuple-element.82.refs_0_, ...), custom_call_target="tpu_custom_call" | custom-call | flops 4200000000 | tf_op jit(solution)/shard_map/cond/branch_1_fun/attend_back/pallas_call | solution.py:244
  171.6 3.6 %combine.6 = (bf16[256,2176]{1,0:T(8,128)(2,1)}, bf16[384,512]{1,0:T(8,128)(2,1)}, bf16[384,512]{1,0:T(8,128)(2,1)}) custom-call(bf16[256,2176]{1,0:T(8,128)(2,1)} %get-tuple-element.121.refs_13_.refs_0_, bf16[256,2176]{1,0:T(8,128)(2,1)} %copy-done.7, bf16[384,512]{1,0:T(8,128)(2,1)} %get-tuple-element.124.refs_2_, bf16[384,512]{1,0:T(8,128)(2,1)} %copy-done.12, ...), custom_call_target="tpu_custom_call" | custom-call | flops 600000000 | tf_op jit(solution)/shard_map/cond/branch_1_fun/combine/pallas_call | solution.py:52
  175.1 6.4 %all-to-all-start = ((bf16[16,16,2176]{2,1,0:T(8,128)(2,1)}), bf16[16,16,2176]{2,1,0:T(8,128)(2,1)S(1)}, u32[]{:S(2)}, u32[]{:S(2)}) async-start(bf16[16,16,2176]{2,1,0:T(8,128)(2,1)} %bitcast.16), calls=%async_computation | async-start | bytes 2228224 | tf_op jit(solution)/shard_map/cond/branch_1_fun/all_to_all | solution.py:740
  183.5 27.0 %attend_back.6 = (bf16[768,256]{1,0:T(8,128)(2,1)}, bf16[1536,256]{1,0:T(8,128)(2,1)}, bf16[1536,256]{1,0:T(8,128)(2,1)}, bf16[768,256]{1,0:T(8,128)(2,1)}, bf16...) custom-call(bf16[768,512]{1,0:T(8,128)(2,1)} %get-tuple-element.82.refs_0_, ...), custom_call_target="tpu_custom_call" | custom-call | flops 8400000000 | tf_op jit(solution)/shard_map/cond/branch_1_fun/attend_back/pallas_call | solution.py:244
  211.6 2.8 combine.7
  214.4 6.0 %all-to-all-start.1 = ((bf16[16,16,2176]{2,1,0:T(8,128)(2,1)}), bf16[16,16,2176]{2,1,0:T(8,128)(2,1)}, u32[]{:S(2)}, u32[]{:S(2)}) async-start(bf16[16,16,2176]{2,1,0:T(8,128)(2,1)} %get-tuple-element.148.refs_19_), calls=%async_computation.1 | async-start | bytes 2228224 | tf_op jit(solution)/shard_map/cond/branch_1_fun/all_to_all | solution.py:743
  220.4 10.1 %self_post.2 = (bf16[768,512]{1,0:T(8,128)(2,1)}, bf16[768,512]{1,0:T(8,128)(2,1)}, bf16[768,512]{1,0:T(8,128)(2,1)}, bf16[768,512]{1,0:T(8,128)(2,1)}, bf16[256...) custom-call(s32[1]{0:T(128)} %get-tuple-element.81.refs_0_, ...), custom_call_target="tpu_custom_call" | custom-call | flops 3600000000 | tf_op jit(solution)/shard_map/cond/branch_1_fun/self_post/pallas_call | solution.py:52
  230.5 14.9 %attend_back.7 = (bf16[768,128]{1,0:T(8,128)(2,1)}, bf16[1536,128]{1,0:T(8,128)(2,1)}, bf16[1536,128]{1,0:T(8,128)(2,1)}, bf16[768,128]{1,0:T(8,128)(2,1)}, bf16...) custom-call(bf16[768,512]{1,0:T(8,128)(2,1)} %get-tuple-element.82.refs_0_, ...), custom_call_target="tpu_custom_call" | custom-call | flops 4200000000 | tf_op jit(solution)/shard_map/cond/branch_1_fun/attend_back/pallas_call | solution.py:244
  245.4 7.4 %self_post.3 = (bf16[768,512]{1,0:T(8,128)(2,1)S(1)}, bf16[768,512]{1,0:T(8,128)(2,1)}, bf16[768,512]{1,0:T(8,128)(2,1)S(1)}, bf16[768,512]{1,0:T(8,128)(2,1)}, ...) custom-call(s32[1]{0:T(128)} %get-tuple-element.81.refs_0_, bf16[768,128]{1,0:T(8,128)(2,1)} %get-tuple-element.152.refs_1_, ...), custom_call_target="tpu_custom_call" | custom-call | flops 1200000000 | tf_op jit(solution)/shard_map/cond/branch_1_fun/self_post/pallas_call | solution.py:52
  258.3 6.9 %all-to-all-start.2 = ((bf16[16,16,1664]{2,1,0:T(8,128)(2,1)}), bf16[16,16,1664]{2,1,0:T(8,128)(2,1)S(1)}, u32[]{:S(2)}, u32[]{:S(2)}) async-start(bf16[16,16,1664]{2,1,0:T(8,128)(2,1)} %bitcast.11), calls=%async_computation.2 | async-start | bytes 1703936 | tf_op jit(solution)/shard_map/all_to_all | solution.py:740
  265.8 3.4 %collective-permute-done.17.refs_2_ = bf16[256,2176]{1,0:T(8,128)(2,1)} collective-permute-done((bf16[256,2176]{1,0:T(8,128)(2,1)}, bf16[256,2176]{1,0:T(8,128)(2,1)}, u32[]{:S(2)}, u32[]{:S(2)}) %collective-permute-start.17) | collective-permute-done | bytes 1114144 | tf_op jit(solution)/shard_map/ppermute | solution.py:736
  269.2 3.8 %place.2 = (f32[512,1024]{1,0:T(8,128)}, f32[512,512]{1,0:T(8,128)}, f32[512,512]{1,0:T(8,128)}, f32[512,128]{1,0:T(8,128)}) custom-call(s32[1]{0:T(128)} %bitcast.10.refs_0_, bf16[256,2176]{1,0:T(8,128)(2,1)} %get-tuple-element.286.refs_1_, bf16[256,2176]{1,0:T(8,128)(2,1)} %collective-permute-done.17.refs_2_, bf16[256,1664]{1,0:T(8,128)(2,1)} %get-tuple-element.287.refs_3_), custom_call_target="tpu_custom_call" | custom-call | flops 1500000000 | tf_op jit(solution)/shard_map/place/pallas_call | solution.py:52
  273.9 2.7 combine.10
  280.1 6.2 %place.3 = (f32[512,2048]{1,0:T(8,128)}, f32[2048,512]{1,0:T(8,128)}, f32[512,512]{1,0:T(8,128)}) custom-call(s32[1]{0:T(128)} %bitcast.10.refs_0_, bf16[512,4608]{1,0:T(8,128)(2,1)} %all-reduce.2.cloned.1.call-done.refs_1_, f32[4,512]{1,0:T(4,128)} %biases.1.refs_2_), custom_call_target="tpu_custom_call" | custom-call | flops 1500000000 | tf_op jit(solution)/shard_map/place/pallas_call | solution.py:52
  291.8 6.0 %all-to-all-start.3 = ((bf16[16,16,1664]{2,1,0:T(8,128)(2,1)}), bf16[16,16,1664]{2,1,0:T(8,128)(2,1)S(1)}, u32[]{:S(2)}, u32[]{:S(2)}) async-start(bf16[16,16,1664]{2,1,0:T(8,128)(2,1)} %combine.11.refs_6_), calls=%async_computation.3 | async-start | bytes 1703936 | tf_op jit(solution)/shard_map/all_to_all | solution.py:743
  299.7 19.1 %all-to-all-done.3 = bf16[16,16,1664]{2,1,0:T(8,128)(2,1)S(1)} async-done(((bf16[16,16,1664]{2,1,0:T(8,128)(2,1)}), bf16[16,16,1664]{2,1,0:T(8,128)(2,1)S(1)}, u32[]{:S(2)}, u32[]{:S(2)}) %all-to-all-start.3) | async-done | bytes 852000 | tf_op jit(solution)/shard_map/all_to_all | solution.py:743
  322.8 4.1 %tokens.1.refs_4_ = bf16[768,512]{1,0:T(8,128)(2,1)} custom-call(bf16[768,512]{1,0:T(8,128)(2,1)} %get-tuple-element.289.refs_1_.refs_0_, bf16[192,512]{1,0:T(8,128)(2,1)} %copy-done.15, bf16[576,512]{1,0:T(8,128)(2,1)} %copy-done.23, f32[768,512]{1,0:T(8,128)} %get-tuple-element.292.refs_3_, bf16[768,512]{1,0:T(8,128)(2,1)} %bitcast.26, ...), custom_call_target="tpu_custom_call" | custom-call | flops 6000000000 | tf_op jit(solution)/shard_map/tokens/pallas_call | solution.py:52
  327.8 3.5 %finish.1 = (f32[512,1536]{1,0:T(8,128)}, f32[3,512]{1,0:T(4,128)}, f32[3,512]{1,0:T(4,128)}, f32[4,512]{1,0:T(4,128)}, f32[3,512]{1,0:T(4,128)}) custom-call(s32[1]{0:T(128)} %bitcast.10.refs_0_, bf16[256,1664]{1,0:T(8,128)(2,1)} %bitcast.18, bf16[256,1664]{1,0:T(8,128)(2,1)} %copy-done.20, f32[512,128]{1,0:T(8,128)} %get-tuple-element.288.refs_4_.refs_0_.refs_3_, ...), custom_call_target="tpu_custom_call" | custom-call | flops 1200000000 | tf_op jit(solution)/shard_map/finish/pallas_call | solution.py:52
  (122 shorter events, 39.6 us)
Async XLA Ops:
  7.2 272.9 %all-reduce.2.cloned.1.call-start = ((), (), s32[]{:S(2)}) async-start(), calls=%async_computation.4 | async-start | bytes 9437184 | tf_op jit(solution)/shard_map/psum | solution.py:827
  7.2 5.6 %collective-permute-start.6 = (bf16[768,512]{1,0:T(8,128)(2,1)}, bf16[768,512]{1,0:T(8,128)(2,1)S(1)}, u32[]{:S(2)}, u32[]{:S(2)}) collective-permute-start(bf16[768,512]{1,0:T(8,128)(2,1)} %bitcast.22), channel_id=1, source_target_pairs={{0,1},{1,0},{2,3},{3,2},{4,5},{5,4},{6,7},{7,6},{8,9},{9,8},{10,11... | collective-permute-start | bytes 2359304 | tf_op jit(solution)/shard_map/ppermute | solution.py:736
  7.7 28.2 %collective-permute-start.8 = (bf16[768,512]{1,0:T(8,128)(2,1)}, bf16[768,512]{1,0:T(8,128)(2,1)}, u32[]{:S(2)}, u32[]{:S(2)}) collective-permute-start(bf16[768,512]{1,0:T(8,128)(2,1)} %bitcast.23), channel_id=1, source_target_pairs={{0,2},{2,0},{1,3},{3,1},{4,6},{6,4},{5,7},{7,5},{8,10},{10,8},{9,1... | collective-permute-start | bytes 2359304 | tf_op jit(solution)/shard_map/ppermute | solution.py:736
  11.7 1.2 collective-permute-start.7
  11.8 24.1 %collective-permute-start.9 = (s32[1,1152]{1,0:T(1,128)S(1)}, s32[1,1152]{1,0:T(1,128)S(1)}, u32[]{:S(2)}, u32[]{:S(2)}) collective-permute-start(s32[1,1152]{1,0:T(1,128)S(1)} %constant_dynamic-update-slice_fusion.refs_2_.refs_5_), channel_id=1, source_target_pairs={{0,2},{2,0},{1,3},{3,1},{4,6},{6,4},{5,7},{7,5},{8,10},{10,8},{9,1... | collective-permute-start | bytes 13832 | tf_op jit(solution)/shard_map/ppermute | solution.py:736
  38.6 5.5 %collective-permute-start.10 = (bf16[768,512]{1,0:T(8,128)(2,1)}, bf16[768,512]{1,0:T(8,128)(2,1)}, u32[]{:S(2)}, u32[]{:S(2)}) collective-permute-start(bf16[768,512]{1,0:T(8,128)(2,1)} %get-tuple-element.252.refs_0_), channel_id=1, source_target_pairs={{0,1},{1,0},{2,3},{3,2},{4,5},{5,4},{6,7},{7,6},{8,9},{9,8},{10,11... | collective-permute-start | bytes 2359304 | tf_op jit(solution)/shard_map/ppermute | solution.py:736
  40.0 4.1 %collective-permute-start.11 = (s32[1,1152]{1,0:T(1,128)}, s32[1,1152]{1,0:T(1,128)S(1)}, u32[]{:S(2)}, u32[]{:S(2)}) collective-permute-start(s32[1,1152]{1,0:T(1,128)} %get-tuple-element.253.refs_1_.refs_7_), channel_id=1, source_target_pairs={{0,1},{1,0},{2,3},{3,2},{4,5},{5,4},{6,7},{7,6},{8,9},{9,8},{10,11... | collective-permute-start | bytes 13832 | tf_op jit(solution)/shard_map/ppermute | solution.py:736
  48.5 23.0 %collective-permute-start.14 = (bf16[384,512]{1,0:T(8,128)(2,1)S(1)}, bf16[384,512]{1,0:T(8,128)(2,1)}, u32[]{:S(2)}, u32[]{:S(2)}) collective-permute-start(bf16[384,512]{1,0:T(8,128)(2,1)S(1)} %get-tuple-element.262.refs_1_), channel_id=1, source_target_pairs={{0,3},{1,2},{2,1},{3,0},{4,7},{5,6},{6,5},{7,4},{8,11},{9,10},{10,... | collective-permute-start | bytes 1179656 | tf_op jit(solution)/shard_map/ppermute | solution.py:762
  49.2 22.3 %collective-permute-start.13 = (bf16[384,512]{1,0:T(8,128)(2,1)S(1)}, bf16[384,512]{1,0:T(8,128)(2,1)}, u32[]{:S(2)}, u32[]{:S(2)}) collective-permute-start(bf16[384,512]{1,0:T(8,128)(2,1)S(1)} %get-tuple-element.262.refs_1_), channel_id=1, source_target_pairs={{0,2},{2,0},{1,3},{3,1},{4,6},{6,4},{5,7},{7,5},{8,10},{10,8},{9,1... | collective-permute-start | bytes 1179656 | tf_op jit(solution)/shard_map/ppermute | solution.py:736
  50.3 21.2 %collective-permute-start.12 = (bf16[384,512]{1,0:T(8,128)(2,1)S(1)}, bf16[384,512]{1,0:T(8,128)(2,1)}, u32[]{:S(2)}, u32[]{:S(2)}) collective-permute-start(bf16[384,512]{1,0:T(8,128)(2,1)S(1)} %get-tuple-element.262.refs_1_), channel_id=1, source_target_pairs={{0,1},{1,0},{2,3},{3,2},{4,5},{5,4},{6,7},{7,6},{8,9},{9,8},{10,11... | collective-permute-start | bytes 1179656 | tf_op jit(solution)/shard_map/ppermute | solution.py:736
  50.4 17.3 %copy-start.24 = (bf16[512,512]{1,0:T(8,128)(2,1)S(1)}, bf16[512,512]{1,0:T(8,128)(2,1)}, u32[]{:S(2)}) copy-start(bf16[512,512]{1,0:T(8,128)(2,1)} %refs_2_.4) | copy-start | bytes 1572868
  76.5 15.7 %copy-start.30 = (bf16[1536,128]{1,0:T(8,128)(2,1)}, bf16[1536,128]{1,0:T(8,128)(2,1)S(1)}, u32[]{:S(2)}) copy-start(bf16[1536,128]{1,0:T(8,128)(2,1)S(1)} %get-tuple-element.265.refs_4_) | copy-start | bytes 1179652
  111.3 28.4 %copy-start.3 = (bf16[512,1536]{1,0:T(8,128)(2,1)}, bf16[512,1536]{1,0:T(8,128)(2,1)S(1)}, u32[]{:S(2)}) copy-start(bf16[512,1536]{1,0:T(8,128)(2,1)S(1)} %get-tuple-element.145.refs_18_.refs_11_) | copy-start | bytes 4718596 | tf_op jit(solution)/shard_map/cond
  111.3 109.1 %copy-start.6 = (bf16[1536,512]{1,0:T(8,128)(2,1)}, bf16[1536,512]{1,0:T(8,128)(2,1)S(1)}, u32[]{:S(2)}) copy-start(bf16[1536,512]{1,0:T(8,128)(2,1)S(1)} %get-tuple-element.142.refs_15_.refs_8_) | copy-start | bytes 4718596 | tf_op jit(solution)/shard_map/cond
  154.4 15.9 %collective-permute-start = (bf16[256,2176]{1,0:T(8,128)(2,1)}, bf16[256,2176]{1,0:T(8,128)(2,1)S(1)}, u32[]{:S(2)}, u32[]{:S(2)}) collective-permute-start(bf16[256,2176]{1,0:T(8,128)(2,1)} %get-tuple-element.123), channel_id=1, source_target_pairs={{0,1},{1,0},{2,3},{3,2},{4,5},{5,4},{6,7},{7,6},{8,9},{9,8},{10,11... | collective-permute-start | bytes 3342344 | tf_op jit(solution)/shard_map/cond/branch_1_fun/ppermute | solution.py:736
  154.9 15.4 %collective-permute-start.1 = (bf16[384,512]{1,0:T(8,128)(2,1)}, bf16[384,512]{1,0:T(8,128)(2,1)S(1)}, u32[]{:S(2)}, u32[]{:S(2)}) collective-permute-start(bf16[384,512]{1,0:T(8,128)(2,1)} %get-tuple-element.125), channel_id=1, source_target_pairs={{0,1},{1,0},{2,3},{3,2},{4,5},{5,4},{6,7},{7,6},{8,9},{9,8},{10,11... | collective-permute-start | bytes 1179656 | tf_op jit(solution)/shard_map/cond/branch_1_fun/ppermute | solution.py:736
  154.9 15.4 %collective-permute-start.2 = (bf16[384,512]{1,0:T(8,128)(2,1)}, bf16[384,512]{1,0:T(8,128)(2,1)S(1)}, u32[]{:S(2)}, u32[]{:S(2)}) collective-permute-start(bf16[384,512]{1,0:T(8,128)(2,1)} %get-tuple-element.127), channel_id=1, source_target_pairs={{0,1},{1,0},{2,3},{3,2},{4,5},{5,4},{6,7},{7,6},{8,9},{9,8},{10,11... | collective-permute-start | bytes 1179656 | tf_op jit(solution)/shard_map/cond/branch_1_fun/ppermute | solution.py:736
  175.1 35.4 %all-to-all-start = ((bf16[16,16,2176]{2,1,0:T(8,128)(2,1)}), bf16[16,16,2176]{2,1,0:T(8,128)(2,1)S(1)}, u32[]{:S(2)}, u32[]{:S(2)}) async-start(bf16[16,16,2176]{2,1,0:T(8,128)(2,1)} %bitcast.16), calls=%async_computation | async-start | bytes 2228224 | tf_op jit(solution)/shard_map/cond/branch_1_fun/all_to_all | solution.py:740
  181.5 29.0 %collective-permute-start.3 = (bf16[384,512]{1,0:T(8,128)(2,1)S(1)}, bf16[384,512]{1,0:T(8,128)(2,1)S(1)}, u32[]{:S(2)}, u32[]{:S(2)}) collective-permute-start(bf16[384,512]{1,0:T(8,128)(2,1)S(1)} %copy-done.25), channel_id=1, source_target_pairs={{0,2},{2,0},{1,3},{3,1},{4,6},{6,4},{5,7},{7,5},{8,10},{10,8},{9,1... | collective-permute-start | bytes 1179656 | tf_op jit(solution)/shard_map/cond/branch_1_fun/ppermute | solution.py:736
  214.4 43.6 %all-to-all-start.1 = ((bf16[16,16,2176]{2,1,0:T(8,128)(2,1)}), bf16[16,16,2176]{2,1,0:T(8,128)(2,1)}, u32[]{:S(2)}, u32[]{:S(2)}) async-start(bf16[16,16,2176]{2,1,0:T(8,128)(2,1)} %get-tuple-element.148.refs_19_), calls=%async_computation.1 | async-start | bytes 2228224 | tf_op jit(solution)/shard_map/cond/branch_1_fun/all_to_all | solution.py:743
  230.5 24.3 %collective-permute-start.4 = (bf16[256,1152]{1,0:T(8,128)(2,1)}, bf16[256,1152]{1,0:T(8,128)(2,1)}, u32[]{:S(2)}, u32[]{:S(2)}) collective-permute-start(bf16[256,1152]{1,0:T(8,128)(2,1)} %get-tuple-element.150), channel_id=1, source_target_pairs={{0,1},{1,0},{2,3},{3,2},{4,5},{5,4},{6,7},{7,6},{8,9},{9,8},{10,11... | collective-permute-start | bytes 1769480 | tf_op jit(solution)/shard_map/cond/branch_1_fun/ppermute | solution.py:736
  230.5 14.9 %copy-start.5 = (bf16[512,1536]{1,0:T(8,128)(2,1)S(1)}, bf16[512,1536]{1,0:T(8,128)(2,1)}, u32[]{:S(2)}) copy-start(bf16[512,1536]{1,0:T(8,128)(2,1)} %copy-done.3) | copy-start | bytes 4718596 | tf_op jit(solution)/shard_map/cond
  252.9 1.9 collective-permute-start.5
  258.3 30.4 %all-to-all-start.2 = ((bf16[16,16,1664]{2,1,0:T(8,128)(2,1)}), bf16[16,16,1664]{2,1,0:T(8,128)(2,1)S(1)}, u32[]{:S(2)}, u32[]{:S(2)}) async-start(bf16[16,16,1664]{2,1,0:T(8,128)(2,1)} %bitcast.11), calls=%async_computation.2 | async-start | bytes 1703936 | tf_op jit(solution)/shard_map/all_to_all | solution.py:740
  265.1 4.1 %collective-permute-start.17 = (bf16[256,2176]{1,0:T(8,128)(2,1)}, bf16[256,2176]{1,0:T(8,128)(2,1)}, u32[]{:S(2)}, u32[]{:S(2)}) collective-permute-start(bf16[256,2176]{1,0:T(8,128)(2,1)} %get-tuple-element.286.refs_1_), channel_id=1, source_target_pairs={{0,1},{1,0},{2,3},{3,2},{4,5},{5,4},{6,7},{7,6},{8,9},{9,8},{10,11... | collective-permute-start | bytes 3342344 | tf_op jit(solution)/shard_map/ppermute | solution.py:736
  265.3 7.8 %collective-permute-start.15 = (bf16[768,512]{1,0:T(8,128)(2,1)}, bf16[768,512]{1,0:T(8,128)(2,1)S(1)}, u32[]{:S(2)}, u32[]{:S(2)}) collective-permute-start(bf16[768,512]{1,0:T(8,128)(2,1)} %get-tuple-element.283), channel_id=1, source_target_pairs={{0,1},{1,0},{2,3},{3,2},{4,5},{5,4},{6,7},{7,6},{8,9},{9,8},{10,11... | collective-permute-start | bytes 2359304 | tf_op jit(solution)/shard_map/ppermute | solution.py:736
  265.7 7.3 %collective-permute-start.16 = (bf16[768,512]{1,0:T(8,128)(2,1)}, bf16[768,512]{1,0:T(8,128)(2,1)}, u32[]{:S(2)}, u32[]{:S(2)}) collective-permute-start(bf16[768,512]{1,0:T(8,128)(2,1)} %get-tuple-element.285), channel_id=1, source_target_pairs={{0,1},{1,0},{2,3},{3,2},{4,5},{5,4},{6,7},{7,6},{8,9},{9,8},{10,11... | collective-permute-start | bytes 2359304 | tf_op jit(solution)/shard_map/ppermute | solution.py:736
  276.6 12.0 %collective-permute-start.18 = (bf16[192,512]{1,0:T(8,128)(2,1)}, bf16[192,512]{1,0:T(8,128)(2,1)S(1)}, u32[]{:S(2)}, u32[]{:S(2)}) collective-permute-start(bf16[192,512]{1,0:T(8,128)(2,1)} %get-tuple-element.290), channel_id=1, source_target_pairs={{0,2},{2,0},{1,3},{3,1},{4,6},{6,4},{5,7},{7,5},{8,10},{10,8},{9,1... | collective-permute-start | bytes 589832 | tf_op jit(solution)/shard_map/ppermute | solution.py:736
  291.8 27.1 %copy-start.16 = (f32[4,512]{1,0:T(4,128)S(1)}, f32[4,512]{1,0:T(4,128)}, u32[]{:S(2)}) copy-start(f32[4,512]{1,0:T(4,128)} %biases.1.refs_2_) | copy-start | bytes 24580
  291.8 27.0 %all-to-all-start.3 = ((bf16[16,16,1664]{2,1,0:T(8,128)(2,1)}), bf16[16,16,1664]{2,1,0:T(8,128)(2,1)S(1)}, u32[]{:S(2)}, u32[]{:S(2)}) async-start(bf16[16,16,1664]{2,1,0:T(8,128)(2,1)} %combine.11.refs_6_), calls=%async_computation.3 | async-start | bytes 1703936 | tf_op jit(solution)/shard_map/all_to_all | solution.py:743
  297.8 24.2 %collective-permute-start.19 = (bf16[576,512]{1,0:T(8,128)(2,1)S(1)}, bf16[576,512]{1,0:T(8,128)(2,1)S(1)}, u32[]{:S(2)}, u32[]{:S(2)}) collective-permute-start(bf16[576,512]{1,0:T(8,128)(2,1)S(1)} %copy-done.22), channel_id=1, source_target_pairs={{0,2},{2,0},{1,3},{3,1},{4,6},{6,4},{5,7},{7,5},{8,10},{10,8},{9,1... | collective-permute-start | bytes 1769480 | tf_op jit(solution)/shard_map/ppermute | solution.py:736
  318.8 8.1 %collective-permute-start.20 = (bf16[256,1664]{1,0:T(8,128)(2,1)S(1)}, bf16[256,1664]{1,0:T(8,128)(2,1)S(1)}, u32[]{:S(2)}, u32[]{:S(2)}) collective-permute-start(bf16[256,1664]{1,0:T(8,128)(2,1)S(1)} %bitcast.17), channel_id=1, source_target_pairs={{0,1},{1,0},{2,3},{3,2},{4,5},{5,4},{6,7},{7,6},{8,9},{9,8},{10,11... | collective-permute-start | bytes 2555912 | tf_op jit(solution)/shard_map/ppermute | solution.py:736
  (28 other events, 87.8 us)
Sparse Core Ops, SparseCore 0:
  111.4 167.1 all-reduce.1

commit v4 on v3

--- a/solution.py
+++ b/solution.py
@@ -926,6 +926,11 @@
     )
     late_all = exchange(late_own)
     parts_come = [swap(parts[1], core), swap(parts[3], core)]
+    cuts = [rows // 4, rows - rows // 4]
+    (own_sum,), side_sums = combine(
+        [([parts[0], parts_come[0]], 1), ([parts[2], parts_come[1]], cuts)], [late_own]
+    )
+    own_come = [swap(item, side) for item in side_sums]
     mid_halves = [mid_half, swap(mid_half, core)]
     cross_kv_grad, self_out_grad, cross_q_grad, small_a = place(
         places,
@@ -936,14 +941,8 @@
                 [(0, (0, 0), 2 * width), (1, (0, 0), width), (2, (0, 0), width), (3, (0, 0), 128)],
             )
         ],
-        [late_own],
-    )
-    cuts = [rows // 4, rows - rows // 4]
-    (own_sum,), side_sums = combine(
-        [([parts[0], parts_come[0]], 1), ([parts[2], parts_come[1]], cuts)], [small_a]
-    )
-    own_come = [swap(item, side) for item in side_sums]
-    (ffn_biases,) = run("biases", 1, biases_kernel, [small_a], [shape(4, width, F32)], [own_sum])
+        [own_sum],
+    )
     ffn_in_grad, ffn_out_grad, cross_out_grad = place(
         places,
         [
@@ -955,17 +954,18 @@
                 + [(2, (0, 0), width)],
             )
         ],
-        [ffn_biases],
+        [small_a],
     )
     ((late_copies,),) = combine([("copies", late_all)], [ffn_in_grad, own_come[0]])
     late_half = regather(late_copies)
+    (ffn_biases,) = run("biases", 1, biases_kernel, [small_a], [shape(4, width, F32)], [late_copies])
     (tokens_grad,) = run(
         "tokens",
         20,
         tokens_kernel,
         [own_sum, *own_come, grad_first, tokens[0], norm_gain],
         [shape(rows, width)],
-        [late_copies],
+        [ffn_biases],
     )
     self_qkv_grad, gains, shifts, projs, outs = run(
         "finish",

time: 342 us -> 341 us (level)
    unnamed x40 -> x38, local copies, waits for them, and re-layouts: 8.53 us -> 8.74 us
where the time goes in v4:
time: 341 us; the launch traced here: 337 us
  Pallas kernels  242 us (71%)
  starting transfers between devices  38.8 us (11%)
  waiting for transfers between devices  28.1 us (8%)
  between operations  15.1 us (4%)
  local copies, waits for them, and re-layouts  12.4 us (4%)
    pallas_call x21, Pallas kernels, run(): pl.pallas_call(wrapped, in_specs=[small] * len(scalars) + [whole] * len(i...  110 us
    pallas_call x4, Pallas kernels, attend_back(): pl.pallas_call(functools.partial(backward_kernel, blocks=[largest_block(k...  85.2 us
    pallas_call x3, Pallas kernels, attend(): pl.pallas_call(functools.partial(forward_kernel, blocks=blocks, begun=beg...  46.9 us
    all_to_all x2, waiting for transfers between devices, regather(): own = lax.all_to_all(copies, chips, 0, 0, tiled=True)  18.9 us
    all_to_all x2, starting transfers between devices, exchange(): lax.all_to_all(half.reshape(number, rows // number, columns), chips, 0, 0...  13.3 us
    ppermute x20, starting transfers between devices, swap(): return lax.ppermute(value, link, [(0, 1), (1, 0)])  13 us
    all_to_all x2, starting transfers between devices, regather(): own = lax.all_to_all(copies, chips, 0, 0, tiled=True)  11.8 us
    ppermute x20, waiting for transfers between devices, swap(): return lax.ppermute(value, link, [(0, 1), (1, 0)])  9.14 us
  transfers between devices with their start and end apart: 26, of which 6 were waited for; matrix products, arithmetic and copies ran while one was open for 1% of the time, Pallas kernels for 56%

profile of v4, /device:TPU:0, one launch (start us, length us, event | category | flops | bytes accessed | tf_op | source)
XLA Modules:
  0.0 337.2 jit_solution(3363418916930321114)
XLA Ops:
  7.7 2.6 collective-permute-start.8
  14.3 6.5 %project.3 = (bf16[1536,512]{1,0:T(8,128)(2,1)S(1)}, bf16[1536,512]{1,0:T(8,128)(2,1)}, bf16[1536,512]{1,0:T(8,128)(2,1)}, bf16[1536,128]{1,0:T(8,128)(2,1)S(1)}...) custom-call(bf16[768,512]{1,0:T(8,128)(2,1)} %bitcast.24, ...), custom_call_target="tpu_custom_call" | custom-call | flops 1800000000 | tf_op jit(solution)/shard_map/project/pallas_call | solution.py:52
  21.8 14.1 %attend.3.refs_2_.refs_6_.refs_8_ = f32[8,768,128]{2,1,0:T(8,128)} custom-call(bf16[768,512]{1,0:T(8,128)(2,1)S(1)} %get-tuple-element.247.refs_0_, bf16[768,128]{1,0:T(8,128)(2,1)} %get-tuple-element.248.refs_1_, bf16[1536,512]{1,0:T(8,128)(2,1)} %get-tuple-element.249.refs_2_, bf16[1536,512]{1,0:T(8,128)(2,1)} %get-tuple-element.250.refs_3_, ...), custom_call_target="tpu_custom_call" | custom-call | flops 3900000000 | tf_op jit(solution)/shard_map/attend/pallas_call | solution.py:154
  40.3 3.7 %project.4 = (bf16[768,512]{1,0:T(8,128)(2,1)}, bf16[768,512]{1,0:T(8,128)(2,1)}, bf16[768,512]{1,0:T(8,128)(2,1)}, bf16[768,128]{1,0:T(8,128)(2,1)}, bf16[768,512]{1,0:T(8,128)(2,1)}) custom-call(bf16[768,512]{1,0:T(8,128)(2,1)} %get-tuple-element.252.refs_0_, s32[1,1152]{1,0:T(1,128)} %get-tuple-element.253.refs_1_.refs_7_, f32[3,512]{1,0:T(4,128)S(1)} %copy-done.25, ...), custom_call_target="tpu_custom_call" | custom-call | flops 1800000000 | tf_op jit(solution)/shard_map/project/pallas_call | solution.py:52
  44.7 3.9 %project.5 = (bf16[768,512]{1,0:T(8,128)(2,1)}, bf16[768,512]{1,0:T(8,128)(2,1)}, bf16[768,512]{1,0:T(8,128)(2,1)}, bf16[768,128]{1,0:T(8,128)(2,1)}, bf16[768,5...) custom-call(bf16[768,512]{1,0:T(8,128)(2,1)} %collective-permute-done.10.refs_0_, s32[1,1152]{1,0:T(1,128)} %copy-done.27, ...), custom_call_target="tpu_custom_call" | custom-call | flops 1800000000 | tf_op jit(solution)/shard_map/project/pallas_call | solution.py:52
  50.4 17.2 %attend.4 = (bf16[768,512]{1,0:T(8,128)(2,1)}, bf16[8,768,128]{2,1,0:T(8,128)(2,1)}) custom-call(bf16[768,512]{1,0:T(8,128)(2,1)} %copy-done.30, bf16[768,128]{1,0:T(8,128)(2,1)} %get-tuple-element.248.refs_1_, bf16[768,512]{1,0:T(8,128)(2,1)} %get-tuple-element.254.refs_7_.refs_2_, bf16[768,512]{1,0:T(8,128)(2,1)} %get-tuple-element.255.refs_3_, ...), custom_call_target="tpu_custom_call" | custom-call | flops 3900000000 | tf_op jit(solution)/shard_map/attend/pallas_call | solution.py:154
  67.6 3.9 %after_self.1 = (f32[768,512]{1,0:T(8,128)}, bf16[768,512]{1,0:T(8,128)(2,1)}, bf16[768,512]{1,0:T(8,128)(2,1)}) custom-call(bf16[768,512]{1,0:T(8,128)(2,1)} %get-tuple-element.260.refs_0_.refs_11_, bf16[768,512]{1,0:T(8,128)(2,1)} %bitcast.25, bf16[512,512]{1,0:T(8,128)(2,1)S(1)} %copy-done.23, f32[3,512]{1,0:T(4,128)} %refs_3_.7, ...), custom_call_target="tpu_custom_call" | custom-call | flops 1200000000 | tf_op jit(solution)/shard_map/after_self/pallas_call | solution.py:52
  71.5 4.9 %project_source.1 = (bf16[1536,512]{1,0:T(8,128)(2,1)}, bf16[1536,512]{1,0:T(8,128)(2,1)}, bf16[1536,128]{1,0:T(8,128)(2,1)S(1)}) custom-call(s32[2]{0:T(128)} %pad_add_fusion.refs_0_, bf16[384,512]{1,0:T(8,128)(2,1)S(1)} %get-tuple-element.262.refs_1_, bf16[384,512]{1,0:T(8,128)(2,1)} %collective-permute-done.12.refs_2_, ...), custom_call_target="tpu_custom_call" | custom-call | flops 1500000000 | tf_op jit(solution)/shard_map/project_source/pallas_call | solution.py:52
  76.4 15.7 %attend.5 = (bf16[768,512]{1,0:T(8,128)(2,1)}, bf16[8,768,128]{2,1,0:T(8,128)(2,1)}) custom-call(bf16[768,512]{1,0:T(8,128)(2,1)} %get-tuple-element.261.refs_0_, bf16[768,128]{1,0:T(8,128)(2,1)} %get-tuple-element.248.refs_1_, bf16[1536,512]{1,0:T(8,128)(2,1)} %get-tuple-element.263.refs_2_, bf16[1536,512]{1,0:T(8,128)(2,1)} %get-tuple-element.264.refs_3_, ...), custom_call_target="tpu_custom_call" | custom-call | flops 3900000000 | tf_op jit(solution)/shard_map/attend/pallas_call | solution.py:154
  92.1 19.2 %ffn.1 = (bf16[768,512]{1,0:T(8,128)(2,1)}, f32[768,512]{1,0:T(8,128)}, bf16[768,512]{1,0:T(8,128)(2,1)}, bf16[512,4608]{1,0:T(8,128)(2,1)}, f32[8,512]{1,0:T(8,128)}) custom-call(bf16[768,512]{1,0:T(8,128)(2,1)} %get-tuple-element.266.refs_0_, f32[768,512]{1,0:T(8,128)} %get-tuple-element.267.refs_1_, bf16[512,512]{1,0:T(8,128)(2,1)} %refs_2_.5, ...), custom_call_target="tpu_custom_call" | custom-call | flops 6300000256 | tf_op jit(solution)/shard_map/ffn/pallas_call | solution.py:52
  111.3 146.9 %conditional.1 = (bf16[256,1664]{1,0:T(8,128)(2,1)}, bf16[256,2176]{1,0:T(8,128)(2,1)}, f32[768,512]{1,0:T(8,128)}, bf16[768,512]{1,0:T(8,128)(2,1)S(1)}, bf16[7...) conditional(s32[]{:T(128)} %bitcast.9, () %tuple.18, ...), branch_computations={%region_0.0_spmd, %region_1.0_spmd} | conditional | flops 36300005376 | bytes 68879120 | solution.py:924
  111.3 28.5 %attend_back.4 = (bf16[768,512]{1,0:T(8,128)(2,1)}, bf16[1536,512]{1,0:T(8,128)(2,1)}, bf16[1536,512]{1,0:T(8,128)(2,1)}) custom-call(bf16[768,512]{1,0:T(8,128)(2,1)} %get-tuple-element.83.refs_0_, bf16[768,512]{1,0:T(8,128)(2,1)} %get-tuple-element.84.refs_1_, bf16[768,512]{1,0:T(8,128)(2,1)} %get-tuple-element.85.refs_2_, ...), custom_call_target="tpu_custom_call" | custom-call | flops 8400000000 | tf_op jit(solution)/shard_map/cond/branch_1_fun/attend_back/pallas_call | solution.py:244
  139.8 6.6 %after_cross.1 = (f32[768,512]{1,0:T(8,128)}, bf16[768,512]{1,0:T(8,128)(2,1)}, f32[512,512]{1,0:T(8,128)}, f32[512,512]{1,0:T(8,128)}, f32[8,512]{1,0:T(8,128)}) custom-call(bf16[768,512]{1,0:T(8,128)(2,1)} %get-tuple-element.91.refs_0_, bf16[512,512]{1,0:T(8,128)(2,1)} %get-tuple-element.92.refs_1_, f32[768,512]{1,0:T(8,128)} %get-tuple-element.93.refs_2_, ...), custom_call_target="tpu_custom_call" | custom-call | flops 1800000000 | tf_op jit(solution)/shard_map/cond/branch_1_fun/after_cross/pallas_call | solution.py:52
  146.4 8.0 %source_back.1 = (bf16[384,512]{1,0:T(8,128)(2,1)}, bf16[384,512]{1,0:T(8,128)(2,1)}, bf16[384,512]{1,0:T(8,128)(2,1)}, bf16[384,512]{1,0:T(8,128)(2,1)}, bf16[2...) custom-call(s32[1]{0:T(128)} %get-tuple-element.81.refs_0_, bf16[1536,512]{1,0:T(8,128)(2,1)} %get-tuple-element.110.refs_1_, ...), custom_call_target="tpu_custom_call" | custom-call | flops 2700000000 | tf_op jit(solution)/shard_map/cond/branch_1_fun/source_back/pallas_call | solution.py:52
  155.4 14.9 %attend_back.5 = (bf16[768,128]{1,0:T(8,128)(2,1)}, bf16[1536,128]{1,0:T(8,128)(2,1)}, bf16[1536,128]{1,0:T(8,128)(2,1)}, bf16[768,128]{1,0:T(8,128)(2,1)}, bf16...) custom-call(bf16[768,512]{1,0:T(8,128)(2,1)} %get-tuple-element.82.refs_0_, ...), custom_call_target="tpu_custom_call" | custom-call | flops 4200000000 | tf_op jit(solution)/shard_map/cond/branch_1_fun/attend_back/pallas_call | solution.py:244
  171.5 3.6 %combine.6 = (bf16[256,2176]{1,0:T(8,128)(2,1)}, bf16[384,512]{1,0:T(8,128)(2,1)}, bf16[384,512]{1,0:T(8,128)(2,1)}) custom-call(bf16[256,2176]{1,0:T(8,128)(2,1)} %get-tuple-element.121.refs_13_.refs_0_, bf16[256,2176]{1,0:T(8,128)(2,1)} %copy-done.7, bf16[384,512]{1,0:T(8,128)(2,1)} %get-tuple-element.124.refs_2_, bf16[384,512]{1,0:T(8,128)(2,1)} %copy-done.12, ...), custom_call_target="tpu_custom_call" | custom-call | flops 600000000 | tf_op jit(solution)/shard_map/cond/branch_1_fun/combine/pallas_call | solution.py:52
  175.1 6.4 %all-to-all-start = ((bf16[16,16,2176]{2,1,0:T(8,128)(2,1)}), bf16[16,16,2176]{2,1,0:T(8,128)(2,1)S(1)}, u32[]{:S(2)}, u32[]{:S(2)}) async-start(bf16[16,16,2176]{2,1,0:T(8,128)(2,1)} %bitcast.16), calls=%async_computation | async-start | bytes 2228224 | tf_op jit(solution)/shard_map/cond/branch_1_fun/all_to_all | solution.py:740
  183.5 27.0 %attend_back.6 = (bf16[768,256]{1,0:T(8,128)(2,1)}, bf16[1536,256]{1,0:T(8,128)(2,1)}, bf16[1536,256]{1,0:T(8,128)(2,1)}, bf16[768,256]{1,0:T(8,128)(2,1)}, bf16...) custom-call(bf16[768,512]{1,0:T(8,128)(2,1)} %get-tuple-element.82.refs_0_, ...), custom_call_target="tpu_custom_call" | custom-call | flops 8400000000 | tf_op jit(solution)/shard_map/cond/branch_1_fun/attend_back/pallas_call | solution.py:244
  211.6 2.8 combine.7
  214.4 6.0 %all-to-all-start.1 = ((bf16[16,16,2176]{2,1,0:T(8,128)(2,1)}), bf16[16,16,2176]{2,1,0:T(8,128)(2,1)}, u32[]{:S(2)}, u32[]{:S(2)}) async-start(bf16[16,16,2176]{2,1,0:T(8,128)(2,1)} %get-tuple-element.148.refs_19_), calls=%async_computation.1 | async-start | bytes 2228224 | tf_op jit(solution)/shard_map/cond/branch_1_fun/all_to_all | solution.py:743
  220.4 10.1 %self_post.2 = (bf16[768,512]{1,0:T(8,128)(2,1)}, bf16[768,512]{1,0:T(8,128)(2,1)}, bf16[768,512]{1,0:T(8,128)(2,1)}, bf16[768,512]{1,0:T(8,128)(2,1)}, bf16[256...) custom-call(s32[1]{0:T(128)} %get-tuple-element.81.refs_0_, ...), custom_call_target="tpu_custom_call" | custom-call | flops 3600000000 | tf_op jit(solution)/shard_map/cond/branch_1_fun/self_post/pallas_call | solution.py:52
  230.6 14.9 %attend_back.7 = (bf16[768,128]{1,0:T(8,128)(2,1)}, bf16[1536,128]{1,0:T(8,128)(2,1)}, bf16[1536,128]{1,0:T(8,128)(2,1)}, bf16[768,128]{1,0:T(8,128)(2,1)}, bf16...) custom-call(bf16[768,512]{1,0:T(8,128)(2,1)} %get-tuple-element.82.refs_0_, ...), custom_call_target="tpu_custom_call" | custom-call | flops 4200000000 | tf_op jit(solution)/shard_map/cond/branch_1_fun/attend_back/pallas_call | solution.py:244
  245.5 7.5 %self_post.3 = (bf16[768,512]{1,0:T(8,128)(2,1)S(1)}, bf16[768,512]{1,0:T(8,128)(2,1)}, bf16[768,512]{1,0:T(8,128)(2,1)S(1)}, bf16[768,512]{1,0:T(8,128)(2,1)}, ...) custom-call(s32[1]{0:T(128)} %get-tuple-element.81.refs_0_, bf16[768,128]{1,0:T(8,128)(2,1)} %get-tuple-element.152.refs_1_, ...), custom_call_target="tpu_custom_call" | custom-call | flops 1200000000 | tf_op jit(solution)/shard_map/cond/branch_1_fun/self_post/pallas_call | solution.py:52
  258.2 7.0 %all-to-all-start.2 = ((bf16[16,16,1664]{2,1,0:T(8,128)(2,1)}), bf16[16,16,1664]{2,1,0:T(8,128)(2,1)S(1)}, u32[]{:S(2)}, u32[]{:S(2)}) async-start(bf16[16,16,1664]{2,1,0:T(8,128)(2,1)} %bitcast.11), calls=%async_computation.2 | async-start | bytes 1703936 | tf_op jit(solution)/shard_map/all_to_all | solution.py:740
  265.8 4.4 %collective-permute-done.15.refs_1_ = bf16[768,512]{1,0:T(8,128)(2,1)S(1)} collective-permute-done((bf16[768,512]{1,0:T(8,128)(2,1)}, bf16[768,512]{1,0:T(8,128)(2,1)S(1)}, u32[]{:S(2)}, u32[]{:S(2)}) %collective-permute-start.15) | collective-permute-done | bytes 786464 | tf_op jit(solution)/shard_map/ppermute | solution.py:736
  271.1 2.7 combine.10
  275.6 3.9 %place.2 = (f32[512,1024]{1,0:T(8,128)}, f32[512,512]{1,0:T(8,128)}, f32[512,512]{1,0:T(8,128)}, f32[512,128]{1,0:T(8,128)}) custom-call(s32[1]{0:T(128)} %bitcast.10.refs_0_, bf16[256,2176]{1,0:T(8,128)(2,1)} %get-tuple-element.291.refs_1_, bf16[256,2176]{1,0:T(8,128)(2,1)} %collective-permute-done.19.refs_2_, ...), custom_call_target="tpu_custom_call" | custom-call | flops 1500000000 | tf_op jit(solution)/shard_map/place/pallas_call | solution.py:52
  279.5 6.2 %place.3 = (f32[512,2048]{1,0:T(8,128)}, f32[2048,512]{1,0:T(8,128)}, f32[512,512]{1,0:T(8,128)}) custom-call(s32[1]{0:T(128)} %bitcast.10.refs_0_, bf16[512,4608]{1,0:T(8,128)(2,1)} %all-reduce.2.cloned.1.call-done.refs_1_, f32[512,128]{1,0:T(8,128)} %get-tuple-element.292.refs_2_.refs_0_.refs_3_), custom_call_target="tpu_custom_call" | custom-call | flops 1500000000 | tf_op jit(solution)/shard_map/place/pallas_call | solution.py:52
  291.0 5.7 %all-to-all-start.3 = ((bf16[16,16,1664]{2,1,0:T(8,128)(2,1)}), bf16[16,16,1664]{2,1,0:T(8,128)(2,1)S(1)}, u32[]{:S(2)}, u32[]{:S(2)}) async-start(bf16[16,16,1664]{2,1,0:T(8,128)(2,1)} %combine.11.refs_1_), calls=%async_computation.3 | async-start | bytes 1703936 | tf_op jit(solution)/shard_map/all_to_all | solution.py:743
  298.7 18.9 %all-to-all-done.3 = bf16[16,16,1664]{2,1,0:T(8,128)(2,1)S(1)} async-done(((bf16[16,16,1664]{2,1,0:T(8,128)(2,1)}), bf16[16,16,1664]{2,1,0:T(8,128)(2,1)S(1)}, u32[]{:S(2)}, u32[]{:S(2)}) %all-to-all-start.3) | async-done | bytes 852000 | tf_op jit(solution)/shard_map/all_to_all | solution.py:743
  321.6 4.1 %tokens.1.refs_4_ = bf16[768,512]{1,0:T(8,128)(2,1)} custom-call(bf16[768,512]{1,0:T(8,128)(2,1)} %get-tuple-element.287.refs_3_.refs_0_, bf16[192,512]{1,0:T(8,128)(2,1)} %copy-done.15, bf16[576,512]{1,0:T(8,128)(2,1)} %copy-done.22, f32[768,512]{1,0:T(8,128)} %get-tuple-element.290.refs_3_, bf16[768,512]{1,0:T(8,128)(2,1)} %bitcast.26, ...), custom_call_target="tpu_custom_call" | custom-call | flops 6000000000 | tf_op jit(solution)/shard_map/tokens/pallas_call | solution.py:52
  326.6 3.5 %finish.1 = (f32[512,1536]{1,0:T(8,128)}, f32[3,512]{1,0:T(4,128)}, f32[3,512]{1,0:T(4,128)}, f32[4,512]{1,0:T(4,128)}, f32[3,512]{1,0:T(4,128)}) custom-call(s32[1]{0:T(128)} %bitcast.10.refs_0_, bf16[256,1664]{1,0:T(8,128)(2,1)} %bitcast.18, bf16[256,1664]{1,0:T(8,128)(2,1)} %copy-done.19, f32[512,128]{1,0:T(8,128)} %get-tuple-element.292.refs_2_.refs_0_.refs_3_, ...), custom_call_target="tpu_custom_call" | custom-call | flops 1200000000 | tf_op jit(solution)/shard_map/finish/pallas_call | solution.py:52
  (120 shorter events, 37.5 us)
Async XLA Ops:
  7.2 272.3 %all-reduce.2.cloned.1.call-start = ((), (), s32[]{:S(2)}) async-start(), calls=%async_computation.4 | async-start | bytes 9437184 | tf_op jit(solution)/shard_map/psum | solution.py:827
  7.2 5.6 %collective-permute-start.6 = (bf16[768,512]{1,0:T(8,128)(2,1)}, bf16[768,512]{1,0:T(8,128)(2,1)S(1)}, u32[]{:S(2)}, u32[]{:S(2)}) collective-permute-start(bf16[768,512]{1,0:T(8,128)(2,1)} %bitcast.22), channel_id=1, source_target_pairs={{0,1},{1,0},{2,3},{3,2},{4,5},{5,4},{6,7},{7,6},{8,9},{9,8},{10,11... | collective-permute-start | bytes 2359304 | tf_op jit(solution)/shard_map/ppermute | solution.py:736
  7.7 28.2 %collective-permute-start.8 = (bf16[768,512]{1,0:T(8,128)(2,1)}, bf16[768,512]{1,0:T(8,128)(2,1)}, u32[]{:S(2)}, u32[]{:S(2)}) collective-permute-start(bf16[768,512]{1,0:T(8,128)(2,1)} %bitcast.23), channel_id=1, source_target_pairs={{0,2},{2,0},{1,3},{3,1},{4,6},{6,4},{5,7},{7,5},{8,10},{10,8},{9,1... | collective-permute-start | bytes 2359304 | tf_op jit(solution)/shard_map/ppermute | solution.py:736
  11.7 1.2 collective-permute-start.7
  11.8 24.1 %collective-permute-start.9 = (s32[1,1152]{1,0:T(1,128)S(1)}, s32[1,1152]{1,0:T(1,128)S(1)}, u32[]{:S(2)}, u32[]{:S(2)}) collective-permute-start(s32[1,1152]{1,0:T(1,128)S(1)} %constant_dynamic-update-slice_fusion.refs_2_.refs_5_), channel_id=1, source_target_pairs={{0,2},{2,0},{1,3},{3,1},{4,6},{6,4},{5,7},{7,5},{8,10},{10,8},{9,1... | collective-permute-start | bytes 13832 | tf_op jit(solution)/shard_map/ppermute | solution.py:736
  38.6 5.5 %collective-permute-start.10 = (bf16[768,512]{1,0:T(8,128)(2,1)}, bf16[768,512]{1,0:T(8,128)(2,1)}, u32[]{:S(2)}, u32[]{:S(2)}) collective-permute-start(bf16[768,512]{1,0:T(8,128)(2,1)} %get-tuple-element.252.refs_0_), channel_id=1, source_target_pairs={{0,1},{1,0},{2,3},{3,2},{4,5},{5,4},{6,7},{7,6},{8,9},{9,8},{10,11... | collective-permute-start | bytes 2359304 | tf_op jit(solution)/shard_map/ppermute | solution.py:736
  40.0 4.1 %collective-permute-start.11 = (s32[1,1152]{1,0:T(1,128)}, s32[1,1152]{1,0:T(1,128)S(1)}, u32[]{:S(2)}, u32[]{:S(2)}) collective-permute-start(s32[1,1152]{1,0:T(1,128)} %get-tuple-element.253.refs_1_.refs_7_), channel_id=1, source_target_pairs={{0,1},{1,0},{2,3},{3,2},{4,5},{5,4},{6,7},{7,6},{8,9},{9,8},{10,11... | collective-permute-start | bytes 13832 | tf_op jit(solution)/shard_map/ppermute | solution.py:736
  48.5 23.0 %collective-permute-start.14 = (bf16[384,512]{1,0:T(8,128)(2,1)S(1)}, bf16[384,512]{1,0:T(8,128)(2,1)}, u32[]{:S(2)}, u32[]{:S(2)}) collective-permute-start(bf16[384,512]{1,0:T(8,128)(2,1)S(1)} %get-tuple-element.262.refs_1_), channel_id=1, source_target_pairs={{0,3},{1,2},{2,1},{3,0},{4,7},{5,6},{6,5},{7,4},{8,11},{9,10},{10,... | collective-permute-start | bytes 1179656 | tf_op jit(solution)/shard_map/ppermute | solution.py:762
  49.2 22.3 %collective-permute-start.13 = (bf16[384,512]{1,0:T(8,128)(2,1)S(1)}, bf16[384,512]{1,0:T(8,128)(2,1)}, u32[]{:S(2)}, u32[]{:S(2)}) collective-permute-start(bf16[384,512]{1,0:T(8,128)(2,1)S(1)} %get-tuple-element.262.refs_1_), channel_id=1, source_target_pairs={{0,2},{2,0},{1,3},{3,1},{4,6},{6,4},{5,7},{7,5},{8,10},{10,8},{9,1... | collective-permute-start | bytes 1179656 | tf_op jit(solution)/shard_map/ppermute | solution.py:736
  50.3 21.2 %collective-permute-start.12 = (bf16[384,512]{1,0:T(8,128)(2,1)S(1)}, bf16[384,512]{1,0:T(8,128)(2,1)}, u32[]{:S(2)}, u32[]{:S(2)}) collective-permute-start(bf16[384,512]{1,0:T(8,128)(2,1)S(1)} %get-tuple-element.262.refs_1_), channel_id=1, source_target_pairs={{0,1},{1,0},{2,3},{3,2},{4,5},{5,4},{6,7},{7,6},{8,9},{9,8},{10,11... | collective-permute-start | bytes 1179656 | tf_op jit(solution)/shard_map/ppermute | solution.py:736
  50.4 17.2 %copy-start.23 = (bf16[512,512]{1,0:T(8,128)(2,1)S(1)}, bf16[512,512]{1,0:T(8,128)(2,1)}, u32[]{:S(2)}) copy-start(bf16[512,512]{1,0:T(8,128)(2,1)} %refs_2_.4) | copy-start | bytes 1572868
  76.4 15.7 %copy-start.29 = (bf16[1536,128]{1,0:T(8,128)(2,1)}, bf16[1536,128]{1,0:T(8,128)(2,1)S(1)}, u32[]{:S(2)}) copy-start(bf16[1536,128]{1,0:T(8,128)(2,1)S(1)} %get-tuple-element.265.refs_4_) | copy-start | bytes 1179652
  111.3 28.5 %copy-start.3 = (bf16[512,1536]{1,0:T(8,128)(2,1)}, bf16[512,1536]{1,0:T(8,128)(2,1)S(1)}, u32[]{:S(2)}) copy-start(bf16[512,1536]{1,0:T(8,128)(2,1)S(1)} %get-tuple-element.145.refs_18_.refs_11_) | copy-start | bytes 4718596 | tf_op jit(solution)/shard_map/cond
  111.3 109.1 %copy-start.6 = (bf16[1536,512]{1,0:T(8,128)(2,1)}, bf16[1536,512]{1,0:T(8,128)(2,1)S(1)}, u32[]{:S(2)}) copy-start(bf16[1536,512]{1,0:T(8,128)(2,1)S(1)} %get-tuple-element.142.refs_15_.refs_8_) | copy-start | bytes 4718596 | tf_op jit(solution)/shard_map/cond
  154.4 15.9 %collective-permute-start = (bf16[256,2176]{1,0:T(8,128)(2,1)}, bf16[256,2176]{1,0:T(8,128)(2,1)S(1)}, u32[]{:S(2)}, u32[]{:S(2)}) collective-permute-start(bf16[256,2176]{1,0:T(8,128)(2,1)} %get-tuple-element.123), channel_id=1, source_target_pairs={{0,1},{1,0},{2,3},{3,2},{4,5},{5,4},{6,7},{7,6},{8,9},{9,8},{10,11... | collective-permute-start | bytes 3342344 | tf_op jit(solution)/shard_map/cond/branch_1_fun/ppermute | solution.py:736
  154.8 15.4 %collective-permute-start.1 = (bf16[384,512]{1,0:T(8,128)(2,1)}, bf16[384,512]{1,0:T(8,128)(2,1)S(1)}, u32[]{:S(2)}, u32[]{:S(2)}) collective-permute-start(bf16[384,512]{1,0:T(8,128)(2,1)} %get-tuple-element.125), channel_id=1, source_target_pairs={{0,1},{1,0},{2,3},{3,2},{4,5},{5,4},{6,7},{7,6},{8,9},{9,8},{10,11... | collective-permute-start | bytes 1179656 | tf_op jit(solution)/shard_map/cond/branch_1_fun/ppermute | solution.py:736
  154.9 15.4 %collective-permute-start.2 = (bf16[384,512]{1,0:T(8,128)(2,1)}, bf16[384,512]{1,0:T(8,128)(2,1)S(1)}, u32[]{:S(2)}, u32[]{:S(2)}) collective-permute-start(bf16[384,512]{1,0:T(8,128)(2,1)} %get-tuple-element.127), channel_id=1, source_target_pairs={{0,1},{1,0},{2,3},{3,2},{4,5},{5,4},{6,7},{7,6},{8,9},{9,8},{10,11... | collective-permute-start | bytes 1179656 | tf_op jit(solution)/shard_map/cond/branch_1_fun/ppermute | solution.py:736
  175.1 35.4 %all-to-all-start = ((bf16[16,16,2176]{2,1,0:T(8,128)(2,1)}), bf16[16,16,2176]{2,1,0:T(8,128)(2,1)S(1)}, u32[]{:S(2)}, u32[]{:S(2)}) async-start(bf16[16,16,2176]{2,1,0:T(8,128)(2,1)} %bitcast.16), calls=%async_computation | async-start | bytes 2228224 | tf_op jit(solution)/shard_map/cond/branch_1_fun/all_to_all | solution.py:740
  181.5 29.0 %collective-permute-start.3 = (bf16[384,512]{1,0:T(8,128)(2,1)S(1)}, bf16[384,512]{1,0:T(8,128)(2,1)S(1)}, u32[]{:S(2)}, u32[]{:S(2)}) collective-permute-start(bf16[384,512]{1,0:T(8,128)(2,1)S(1)} %copy-done.24), channel_id=1, source_target_pairs={{0,2},{2,0},{1,3},{3,1},{4,6},{6,4},{5,7},{7,5},{8,10},{10,8},{9,1... | collective-permute-start | bytes 1179656 | tf_op jit(solution)/shard_map/cond/branch_1_fun/ppermute | solution.py:736
  214.4 43.6 %all-to-all-start.1 = ((bf16[16,16,2176]{2,1,0:T(8,128)(2,1)}), bf16[16,16,2176]{2,1,0:T(8,128)(2,1)}, u32[]{:S(2)}, u32[]{:S(2)}) async-start(bf16[16,16,2176]{2,1,0:T(8,128)(2,1)} %get-tuple-element.148.refs_19_), calls=%async_computation.1 | async-start | bytes 2228224 | tf_op jit(solution)/shard_map/cond/branch_1_fun/all_to_all | solution.py:743
  230.6 24.2 %collective-permute-start.4 = (bf16[256,1152]{1,0:T(8,128)(2,1)}, bf16[256,1152]{1,0:T(8,128)(2,1)}, u32[]{:S(2)}, u32[]{:S(2)}) collective-permute-start(bf16[256,1152]{1,0:T(8,128)(2,1)} %get-tuple-element.150), channel_id=1, source_target_pairs={{0,1},{1,0},{2,3},{3,2},{4,5},{5,4},{6,7},{7,6},{8,9},{9,8},{10,11... | collective-permute-start | bytes 1769480 | tf_op jit(solution)/shard_map/cond/branch_1_fun/ppermute | solution.py:736
  230.6 14.9 %copy-start.5 = (bf16[512,1536]{1,0:T(8,128)(2,1)S(1)}, bf16[512,1536]{1,0:T(8,128)(2,1)}, u32[]{:S(2)}) copy-start(bf16[512,1536]{1,0:T(8,128)(2,1)} %copy-done.3) | copy-start | bytes 4718596 | tf_op jit(solution)/shard_map/cond
  230.6 14.9 %copy-start.10 = (bf16[768,512]{1,0:T(8,128)(2,1)S(1)}, bf16[768,512]{1,0:T(8,128)(2,1)}, u32[]{:S(2)}) copy-start(bf16[768,512]{1,0:T(8,128)(2,1)} %get-tuple-element.143.refs_16_.refs_9_) | copy-start | bytes 2359300 | tf_op jit(solution)/shard_map/cond
  252.9 1.8 collective-permute-start.5
  258.2 29.6 %all-to-all-start.2 = ((bf16[16,16,1664]{2,1,0:T(8,128)(2,1)}), bf16[16,16,1664]{2,1,0:T(8,128)(2,1)S(1)}, u32[]{:S(2)}, u32[]{:S(2)}) async-start(bf16[16,16,1664]{2,1,0:T(8,128)(2,1)} %bitcast.11), calls=%async_computation.2 | async-start | bytes 1703936 | tf_op jit(solution)/shard_map/all_to_all | solution.py:740
  265.1 10.5 %collective-permute-start.19 = (bf16[256,2176]{1,0:T(8,128)(2,1)}, bf16[256,2176]{1,0:T(8,128)(2,1)}, u32[]{:S(2)}, u32[]{:S(2)}) collective-permute-start(bf16[256,2176]{1,0:T(8,128)(2,1)} %get-tuple-element.291.refs_1_), channel_id=1, source_target_pairs={{0,1},{1,0},{2,3},{3,2},{4,5},{5,4},{6,7},{7,6},{8,9},{9,8},{10,11... | collective-permute-start | bytes 3342344 | tf_op jit(solution)/shard_map/ppermute | solution.py:736
  265.3 4.9 %collective-permute-start.15 = (bf16[768,512]{1,0:T(8,128)(2,1)}, bf16[768,512]{1,0:T(8,128)(2,1)S(1)}, u32[]{:S(2)}, u32[]{:S(2)}) collective-permute-start(bf16[768,512]{1,0:T(8,128)(2,1)} %get-tuple-element.283), channel_id=1, source_target_pairs={{0,1},{1,0},{2,3},{3,2},{4,5},{5,4},{6,7},{7,6},{8,9},{9,8},{10,11... | collective-permute-start | bytes 2359304 | tf_op jit(solution)/shard_map/ppermute | solution.py:736
  265.7 4.9 %collective-permute-start.16 = (bf16[768,512]{1,0:T(8,128)(2,1)}, bf16[768,512]{1,0:T(8,128)(2,1)}, u32[]{:S(2)}, u32[]{:S(2)}) collective-permute-start(bf16[768,512]{1,0:T(8,128)(2,1)} %get-tuple-element.285), channel_id=1, source_target_pairs={{0,1},{1,0},{2,3},{3,2},{4,5},{5,4},{6,7},{7,6},{8,9},{9,8},{10,11... | collective-permute-start | bytes 2359304 | tf_op jit(solution)/shard_map/ppermute | solution.py:736
  273.8 14.0 %collective-permute-start.17 = (bf16[192,512]{1,0:T(8,128)(2,1)}, bf16[192,512]{1,0:T(8,128)(2,1)S(1)}, u32[]{:S(2)}, u32[]{:S(2)}) collective-permute-start(bf16[192,512]{1,0:T(8,128)(2,1)} %get-tuple-element.288), channel_id=1, source_target_pairs={{0,2},{2,0},{1,3},{3,1},{4,6},{6,4},{5,7},{7,5},{8,10},{10,8},{9,1... | collective-permute-start | bytes 589832 | tf_op jit(solution)/shard_map/ppermute | solution.py:736
  291.0 26.7 %all-to-all-start.3 = ((bf16[16,16,1664]{2,1,0:T(8,128)(2,1)}), bf16[16,16,1664]{2,1,0:T(8,128)(2,1)S(1)}, u32[]{:S(2)}, u32[]{:S(2)}) async-start(bf16[16,16,1664]{2,1,0:T(8,128)(2,1)} %combine.11.refs_1_), calls=%async_computation.3 | async-start | bytes 1703936 | tf_op jit(solution)/shard_map/all_to_all | solution.py:743
  296.7 24.1 %collective-permute-start.18 = (bf16[576,512]{1,0:T(8,128)(2,1)S(1)}, bf16[576,512]{1,0:T(8,128)(2,1)S(1)}, u32[]{:S(2)}, u32[]{:S(2)}) collective-permute-start(bf16[576,512]{1,0:T(8,128)(2,1)S(1)} %copy-done.21), channel_id=1, source_target_pairs={{0,2},{2,0},{1,3},{3,1},{4,6},{6,4},{5,7},{7,5},{8,10},{10,8},{9,1... | collective-permute-start | bytes 1769480 | tf_op jit(solution)/shard_map/ppermute | solution.py:736
  317.6 8.1 %collective-permute-start.20 = (bf16[256,1664]{1,0:T(8,128)(2,1)S(1)}, bf16[256,1664]{1,0:T(8,128)(2,1)S(1)}, u32[]{:S(2)}, u32[]{:S(2)}) collective-permute-start(bf16[256,1664]{1,0:T(8,128)(2,1)S(1)} %bitcast.17), channel_id=1, source_target_pairs={{0,1},{1,0},{2,3},{3,2},{4,5},{5,4},{6,7},{7,6},{8,9},{9,8},{10,11... | collective-permute-start | bytes 2555912 | tf_op jit(solution)/shard_map/ppermute | solution.py:736
  (27 other events, 72.6 us)
Sparse Core Ops, SparseCore 0:
  111.4 166.7 all-reduce.1
